TPU v7x, 512 devices: a whole 4x4x16 slice. The times are simulated.
512 devices in a mesh: dp: 16 (over y, x), col: 32 (over z, core).
Axes of the slice: x: 4, y: 4, z: 16, core: 2. Of those that a mesh axis runs over, the one named last changes fastest.
Arguments:
- grad_parts: bfloat16 [16, 2048, 7168], P('dp', None, 'col'), may hold values from -1.5 to 1.5
- left_basis: bfloat16 [2048, 2048], P('dp'), may hold values from -0.125 to 0.125
- right_basis: bfloat16 [7168, 7168], P('col', 'dp'), may hold values from -0.0625 to 0.0625
- first_moment: float32 [7168, 2048], P('dp', 'col'), may hold values from -0.6 to 0.6
- second_moment: float32 [7168, 2048], P('dp', 'col'), may hold values from 0.005 to 0.5
Outputs:
- left_gram: float32 [2048, 2048], P('dp', 'col')
- new_first: float32 [7168, 2048], P('dp', 'col')
- new_second: float32 [7168, 2048], P('dp', 'col')
- direction: float32 [2048, 7168], P('dp', 'col')
All inputs are finite; a program needn't handle non-finite values.
Results may differ from a plain program's by a relative error of at most 0.035.
Values may be sent and summed in bfloat16 or wider, within the bound.
No kernel may reach another device: no remote copies, remote signals or barrier semaphores. Data moves between devices by JAX's collectives and lax.ppermute only.
A program may use at most 64 MiB of HBM per device.

v0:
```python
import jax
import jax.numpy as jnp
from jax import lax
from jax.sharding import PartitionSpec as P

D = 7168


def on_device(grad_parts, left_basis, right_basis, first_moment, second_moment):
    rows_here = left_basis.shape[0]
    dp_index = lax.axis_index("dp")
    grad_full = lax.psum(grad_parts[0].astype(jnp.float32).astype(jnp.bfloat16), "dp")
    grad_rows = lax.dynamic_slice_in_dim(grad_full, dp_index * rows_here, rows_here, 0)
    gram_term = (
        lax.dot_general(
            grad_rows, grad_full, (((1,), (1,)), ((), ())), preferred_element_type=jnp.float32
        )
        / D
    )
    left_term = lax.dot_general(
        left_basis, grad_rows, (((0,), (0,)), ((), ())), preferred_element_type=jnp.float32
    )
    turned = lax.psum(left_term.astype(jnp.bfloat16), "dp")
    right_term = lax.dot_general(
        right_basis, turned, (((0,), (1,)), ((), ())), preferred_element_type=jnp.float32
    )
    gram_share, rotated = (
        lax.psum_scatter(
            gram_term.astype(jnp.bfloat16), "col", scatter_dimension=1, tiled=True
        ).astype(jnp.float32),
        lax.psum_scatter(
            right_term.astype(jnp.bfloat16), "col", scatter_dimension=1, tiled=True
        ).astype(jnp.float32),
    )
    new_first = 0.9 * first_moment + 0.1 * rotated
    new_second = 0.95 * second_moment + 0.05 * rotated * rotated
    update = (new_first / 0.19 / (jnp.sqrt(new_second / 0.0975) + 1e-08)).astype(jnp.bfloat16)
    back_term = lax.dot_general(
        lax.all_gather(update, "col", axis=1, tiled=True),
        right_basis,
        (((0,), (1,)), ((), ())),
        preferred_element_type=jnp.float32,
    )
    turned_back = lax.psum(back_term.astype(jnp.bfloat16), "dp")
    direction = jnp.dot(left_basis, turned_back, preferred_element_type=jnp.float32)
    return (gram_share, new_first, new_second, direction)


def solution(mesh):
    in_specs = (P("dp", None, "col"), P("dp", None), P("col", "dp"), P("dp", "col"), P("dp", "col"))
    out_specs = (P("dp", "col"), P("dp", "col"), P("dp", "col"), P("dp", "col"))
    return jax.shard_map(
        on_device, mesh=mesh, in_specs=in_specs, out_specs=out_specs, check_vma=False
    )
```

profile of v0, /device:TPU:6, one launch (start us, length us, event | category | flops | bytes accessed | tf_op | source)
XLA Modules:
  0.0 671.2 jit_solution(14403953641210185513)
XLA Ops:
  7.2 0.0 copy-start
  7.2 0.0 copy-start.2
  7.2 0.0 all-reduce.4.cloned.1.call-start
  7.2 0.7 all-reduce.4.cloned.1.call-update
  7.9 0.0 all-reduce.6.cloned.1.call-start
  8.0 124.0 %all-reduce.4.cloned.1.call-done = bf16[2048,224]{0,1:T(8,128)(2,1)} async-done(((bf16[2048,224]{0,1:T(8,128)(2,1)}), bf16[2048,224]{0,1:T(8,128)(2,1)}) %all-reduce.4.cloned.1.call-update) | async-done | bytes 917520 | tf_op jit(solution)/shard_map/psum | solution.py:12
  131.9 0.0 copy-done
  131.9 2.2 fusion.1
  134.1 0.0 all-reduce.6.cloned.1.call-update
  134.2 0.0 reduce-scatter.7.cloned.1.call-start
  134.2 117.0 %all-reduce.6.cloned.1.call-done = bf16[2048,224]{0,1:T(8,128)(2,1)} async-done(((bf16[2048,224]{0,1:T(8,128)(2,1)}), bf16[2048,224]{0,1:T(8,128)(2,1)}) %all-reduce.6.cloned.1.call-update) | async-done | bytes 917520 | tf_op jit(solution)/shard_map/psum | solution.py:23
  251.2 0.0 copy-done.2
  251.2 1.9 fusion
  253.1 0.0 copy-start.3
  253.1 0.0 copy-start.4
  253.1 2.4 copy.19
  255.5 0.0 reduce-scatter.7.cloned.1.call-update
  255.6 0.0 all-gather.2.cloned.1.call-start
  255.6 110.0 %reduce-scatter.7.cloned.1.call-done = bf16[64,448]{1,0:T(8,128)(2,1)} async-done(((bf16[2048,448]{1,0:T(8,128)(2,1)}), bf16[64,448]{1,0:T(8,128)(2,1)}) %reduce-scatter.7.cloned.1.call-update) | async-done | bytes 57360
  365.6 1.6 divide_convert_fusion
  367.2 0.0 all-gather.2.cloned.1.call-update
  367.2 0.0 reduce-scatter.5.cloned.1.call-start
  367.3 1.4 fusion.2
  368.6 0.0 reduce-scatter.5.cloned.1.call-update
  368.7 0.0 all-reduce.8.cloned.1.call-start
  368.7 69.0 %all-gather.2.cloned.1.call-done = bf16[448,2048]{0,1:T(8,128)(2,1)} async-done(((bf16[448,64]{0,1:T(8,128)(2,1)}), bf16[448,2048]{0,1:T(8,128)(2,1)}) %all-gather.2.cloned.1.call-update) | async-done | bytes 1835024 | tf_op jit(solution)/shard_map/all_gather | solution.py:39
  437.7 3.3 convolution_convert_fusion.1
  441.0 0.0 all-reduce.8.cloned.1.call-update
  441.0 103.8 %reduce-scatter.5.cloned.1.call-done = bf16[128,64]{0,1:T(8,128)(2,1)} async-done(((bf16[128,2048]{0,1:T(8,128)(2,1)}), bf16[128,64]{0,1:T(8,128)(2,1)}) %reduce-scatter.5.cloned.1.call-update) | async-done | bytes 16400 | tf_op jit(solution)/shard_map/reduce_scatter | solution.py:28
  544.8 1.3 convert_element_type.30
  546.1 116.0 %all-reduce.8.cloned.1.call-done = bf16[2048,224]{0,1:T(8,128)(2,1)} async-done(((bf16[2048,224]{0,1:T(8,128)(2,1)}), bf16[2048,224]{0,1:T(8,128)(2,1)}) %all-reduce.8.cloned.1.call-update) | async-done | bytes 917520 | tf_op jit(solution)/shard_map/psum | solution.py:44
  662.1 2.2 convolution_bitcast_fusion
  (4 shorter events, 0.0 us)
Async XLA Ops:
  7.2 124.8 %copy-start = (bf16[128,2048]{1,0:T(8,128)(2,1)S(1)}, bf16[128,2048]{1,0:T(8,128)(2,1)}, u32[]{:S(2)}) copy-start(bf16[128,2048]{1,0:T(8,128)(2,1)} %param.6) | copy-start | bytes 1572868
  7.2 244.1 %copy-start.2 = (bf16[224,448]{1,0:T(8,128)(2,1)S(1)}, bf16[224,448]{1,0:T(8,128)(2,1)}, u32[]{:S(2)}) copy-start(bf16[224,448]{1,0:T(8,128)(2,1)} %param.7) | copy-start | bytes 602116
  7.2 124.8 %all-reduce.4.cloned.1.call-start = ((), (), s32[]{:S(2)}) async-start(), calls=%async_computation.2 | async-start | bytes 1835008 | tf_op jit(solution)/shard_map/psum | solution.py:12
  7.9 243.3 %all-reduce.6.cloned.1.call-start = ((), (), s32[]{:S(2)}) async-start(), calls=%async_computation.4 | async-start | bytes 1835008 | tf_op jit(solution)/shard_map/psum | solution.py:23
  134.2 231.4 %reduce-scatter.7.cloned.1.call-start = ((), (), s32[]{:S(2)}) async-start(), calls=%async_computation.7 | async-start | bytes 2162688
  253.1 112.5 %copy-start.3 = (f32[448,64]{0,1:T(8,128)S(1)}, f32[448,64]{0,1:T(8,128)}, u32[]{:S(2)}) copy-start(f32[448,64]{0,1:T(8,128)} %param.9) | copy-start | bytes 344068
  253.1 112.5 %copy-start.4 = (f32[448,64]{0,1:T(8,128)S(1)}, f32[448,64]{0,1:T(8,128)}, u32[]{:S(2)}) copy-start(f32[448,64]{0,1:T(8,128)} %param.8) | copy-start | bytes 344068
  255.5 111.7 %copy-start.1 = (bf16[2048,224]{0,1:T(8,128)(2,1)S(1)}, bf16[2048,224]{0,1:T(8,128)(2,1)}, u32[]{:S(2)}) copy-start(bf16[2048,224]{0,1:T(8,128)(2,1)} %all-reduce.4.cloned.1.call-done) | copy-start | bytes 2752516
  255.6 182.1 %all-gather.2.cloned.1.call-start = ((), (), s32[]{:S(2)}) async-start(), calls=%async_computation.5 | async-start | bytes 2162688 | tf_op jit(solution)/shard_map/all_gather | solution.py:39
  367.2 177.5 %reduce-scatter.5.cloned.1.call-start = ((), (), s32[]{:S(2)}) async-start(), calls=%async_computation.3 | async-start | bytes 540672 | tf_op jit(solution)/shard_map/reduce_scatter | solution.py:28
  368.7 293.5 %all-reduce.8.cloned.1.call-start = ((), (), s32[]{:S(2)}) async-start(), calls=%async_computation.6 | async-start | bytes 1835008 | tf_op jit(solution)/shard_map/psum | solution.py:44
Sparse Core Ops, SparseCore 0:
  11.3 120.5 all-reduce.3
  135.2 115.9 all-reduce.5
  255.7 109.8 reduce-scatter.6
  368.4 69.2 all-gather.1
  440.5 104.2 reduce-scatter.4
  547.9 114.1 all-reduce.7
where the time goes:
time: 672 us; the launch traced here: 671 us
  waiting for transfers between devices  640 us (95%)
  between operations  14.2 us (2%)
  matrix products  10.9 us (2%)
    psum x1, waiting for transfers between devices, on_device(): lax.psum(grad_parts[0].astype(jnp.float32).astype(jnp.bfloat16), 'dp')  124 us
    psum x1, waiting for transfers between devices, on_device(): turned = lax.psum(left_term.astype(jnp.bfloat16), 'dp')  117 us
    psum x1, waiting for transfers between devices, on_device(): turned_back = lax.psum(back_term.astype(jnp.bfloat16), 'dp')  116 us
    unnamed x7, waiting for transfers between devices  111 us
    reduce_scatter x1, waiting for transfers between devices, on_device(): lax.psum_scatter(gram_term.astype(jnp.bfloat16), 'col', scatter_dimension...  104 us
    all_gather x1, waiting for transfers between devices, on_device(): lax.all_gather(update, 'col', axis=1, tiled=True)  69 us
  transfers between devices with their start and end apart: 6, of which 6 were waited for; matrix products, arithmetic and copies ran while one was open for 1% of the time, Pallas kernels for 0%

commit v1 on v0

v1 whole, which is shorter than its diff:
```python
import jax
import jax.numpy as jnp
from jax import lax
from jax.sharding import Mesh, PartitionSpec as P

D = 7168
DP = ("y", "x")
F32 = jnp.float32
BF16 = jnp.bfloat16


def exchange(chunks, axes):
    return lax.all_to_all(chunks, axes, 0, 0, tiled=True)


def on_device(grad_parts, left_basis, right_basis, first_moment, second_moment):
    rows = left_basis.shape[0]
    cols = right_basis.shape[0]
    turns = right_basis.shape[1]
    n_dp = left_basis.shape[1] // rows
    n_z = lax.axis_size("z")
    sub = rows // n_dp
    half = rows // 2
    core = lax.axis_index("core")

    basis_z = lax.all_gather(right_basis, "z", axis=0, tiled=False)

    parts = grad_parts[0].T.reshape(cols, n_dp, rows).transpose(1, 0, 2)
    grad_t = jnp.sum(exchange(parts, DP).astype(F32), axis=0).astype(BF16)

    basis_p = (
        left_basis.reshape(rows, n_z, n_dp, sub).transpose(0, 2, 1, 3).reshape(rows, n_dp, rows)
    )
    left_term = lax.dot_general(
        basis_p, grad_t, (((0,), (1,)), ((), ())), preferred_element_type=F32
    )
    turned = jnp.sum(exchange(left_term.astype(BF16), DP).astype(F32), axis=0).astype(BF16)
    turned = exchange(turned.reshape(n_z, sub, cols), "z")
    turned = exchange(jnp.broadcast_to(turned[None], (n_dp, n_z, sub, cols)), DP)

    grad_all = exchange(jnp.broadcast_to(grad_t[None], (n_dp, cols, rows)), DP)
    gram = lax.dot_general(
        grad_all, grad_t, (((1,), (0,)), ((), ())), preferred_element_type=F32
    ).reshape(n_z, 2, half, rows) / D
    mine = lax.dynamic_index_in_dim(gram, core, 1, keepdims=False)
    other = lax.dynamic_index_in_dim(gram, 1 - core, 1, keepdims=False)
    swap = [(0, 1), (1, 0)]
    mine = mine + lax.ppermute(other.astype(BF16), "core", swap).astype(F32)
    left_gram = lax.psum_scatter(mine, "z", scatter_dimension=0, tiled=False).T

    rotated = jnp.einsum("iztc,zcn->itn", turned, basis_z, preferred_element_type=F32)
    rotated = rotated.reshape(2, half, turns)
    mine = lax.dynamic_index_in_dim(rotated, core, 0, keepdims=False)
    other = lax.dynamic_index_in_dim(rotated, 1 - core, 0, keepdims=False)
    mine = mine + lax.ppermute(other.astype(BF16), "core", swap).astype(F32)
    new_first = 0.9 * first_moment.T + 0.1 * mine
    new_second = 0.95 * second_moment.T + 0.05 * mine * mine
    update = (new_first / 0.19 / (jnp.sqrt(new_second / 0.0975) + 1e-08)).astype(BF16)
    theirs = lax.ppermute(update, "core", swap)
    update = jnp.where(core == 0, jnp.stack([update, theirs]), jnp.stack([theirs, update]))
    update = update.reshape(rows, turns)

    back = jnp.einsum("mn,zcn->zmc", update, basis_z, preferred_element_type=F32).astype(BF16)
    back = back.reshape(n_z, n_dp, sub, cols).transpose(1, 0, 2, 3)
    back = jnp.sum(exchange(back, DP).astype(F32), axis=0).astype(BF16)
    back = exchange(back, "z")
    back = exchange(jnp.broadcast_to(back[None], (n_dp, n_z, sub, cols)), DP)
    direction = jnp.dot(
        basis_p.reshape(rows, n_dp * rows),
        back.reshape(n_dp * rows, cols),
        preferred_element_type=F32,
    )
    return (left_gram, new_first.T, new_second.T, direction)


def solution(mesh):
    n_dp, n_col = mesh.shape["dp"], mesh.shape["col"]
    side = int(round(n_dp**0.5))
    fine = Mesh(
        mesh.devices.reshape(side, side, n_col // 2, 2), ("y", "x", "z", "core")
    )
    dp, col = ("y", "x"), ("z", "core")
    in_specs = (P(dp, None, col), P(dp, None), P(col, dp), P(dp, col), P(dp, col))
    out_specs = (P(dp, col), P(dp, col), P(dp, col), P(dp, col))
    return jax.shard_map(
        on_device, mesh=fine, in_specs=in_specs, out_specs=out_specs, check_vma=False
    )
```

time: 672 us -> 239 us (0.36)
  the two profiles are of different devices: /device:TPU:6 before, /device:TPU:2 now
where the time goes in v1:
time: 239 us; the launch traced here: 238 us
  waiting for transfers between devices  106 us (44%)
  blocking collectives  62.4 us (26%)
  starting transfers between devices  37.5 us (16%)
  between operations  14.2 us (6%)
  local copies, waits for them, and re-layouts  8.34 us (3%)
  matrix products  8.05 us (3%)
    all_to_all x3, blocking collectives, exchange(): return lax.all_to_all(chunks, axes, 0, 0, tiled=True)  62.4 us
    all_to_all x5, waiting for transfers between devices, exchange(): return lax.all_to_all(chunks, axes, 0, 0, tiled=True)  53 us
    reduce_scatter x1, waiting for transfers between devices, on_device(): left_gram = lax.psum_scatter(mine, 'z', scatter_dimension=0, tiled=False).T  49.7 us
    all_to_all x5, starting transfers between devices, exchange(): return lax.all_to_all(chunks, axes, 0, 0, tiled=True)  31.4 us
  transfers between devices with their start and end apart: 10, of which 7 were waited for; matrix products, arithmetic and copies ran while one was open for 8% of the time, Pallas kernels for 0%

profile of v1, /device:TPU:2, one launch (start us, length us, event | category | flops | bytes accessed | tf_op | source)
XLA Modules:
  0.0 238.3 jit_solution(744273157899023407)
XLA Ops:
  7.2 0.7 all-gather.3.cloned.1.call-update
  7.9 1.4 copy.49
  9.3 1.2 copy.30
  10.5 9.3 %all-to-all-start = ((bf16[16,224,128]{2,1,0:T(8,128)(2,1)}), bf16[16,224,128]{2,1,0:T(8,128)(2,1)S(1)}, u32[]{:S(2)}, u32[]{:S(2)}) async-start(bf16[16,224,128]{2,1,0:T(8,128)(2,1)} %copy.30), calls=%async_computation | async-start | bytes 1835008 | tf_op jit(solution)/shard_map/all_to_all | solution.py:13
  20.1 12.5 %all-to-all-done = bf16[16,224,128]{2,1,0:T(8,128)(2,1)S(1)} async-done(((bf16[16,224,128]{2,1,0:T(8,128)(2,1)}), bf16[16,224,128]{2,1,0:T(8,128)(2,1)S(1)}, u32[]{:S(2)}, u32[]{:S(2)}) %all-to-all-start) | async-done | bytes 917536 | tf_op jit(solution)/shard_map/all_to_all | solution.py:13
  33.1 16.3 %all_to_all.40 = bf16[16,128,224]{1,2,0:T(8,128)(2,1)S(1)} all-to-all(bf16[16,128,224]{1,2,0:T(8,128)(2,1)S(1)} %fusion), channel_id=1, replica_groups=mesh['y'=4,'x'=4,'z'=16,'core'=2] {'y','x'}, dimensions={0} | all-to-all | bytes 1835008 | tf_op jit(solution)/shard_map/all_to_all | solution.py:13
  49.6 30.1 %all_to_all.41 = bf16[16,8,224]{2,1,0:T(8,128)(2,1)S(1)} all-to-all(bf16[16,8,224]{2,1,0:T(8,128)(2,1)S(1)} %bitcast.106), channel_id=1, replica_groups=mesh['y'=4,'x'=4,'z'=16,'core'=2] {'z'}, dimensions={0} | all-to-all | bytes 114688 | tf_op jit(solution)/shard_map/all_to_all | solution.py:13
  79.7 1.1 broadcast_in_dim.7
  80.8 4.7 %all-to-all-start.4 = ((bf16[16,16,8,224]{3,2,1,0:T(8,128)(2,1)}), bf16[16,16,8,224]{3,2,1,0:T(8,128)(2,1)S(1)}, u32[]{:S(2)}, u32[]{:S(2)}) async-start(bf16[16,16,8,224]{3,2,1,0:T(8,128)(2,1)} %broadcast_in_dim.7), calls=%async_computation.5 | async-start | bytes 2097152 | tf_op jit(solution)/shard_map/all_to_all | solution.py:13
  85.5 13.9 %all-to-all-done.4 = bf16[16,16,8,224]{3,2,1,0:T(8,128)(2,1)S(1)} async-done(((bf16[16,16,8,224]{3,2,1,0:T(8,128)(2,1)}), bf16[16,16,8,224]{3,2,1,0:T(8,128)(2,1)S(1)}, u32[]{:S(2)}, u32[]{:S(2)}) %all-to-all-start.4) | async-done | bytes 917536 | tf_op jit(solution)/shard_map/all_to_all | solution.py:13
  99.4 1.1 broadcast_in_dim.6
  100.5 4.8 %all-to-all-start.1 = ((bf16[16,224,128]{2,1,0:T(8,128)(2,1)}), bf16[16,224,128]{2,1,0:T(8,128)(2,1)S(1)}, u32[]{:S(2)}, u32[]{:S(2)}) async-start(bf16[16,224,128]{2,1,0:T(8,128)(2,1)} %broadcast_in_dim.6), calls=%async_computation.1 | async-start | bytes 1835008 | tf_op jit(solution)/shard_map/all_to_all | solution.py:13
  105.3 2.8 %fusion.12 = f32[16,8,448,1]{2,1,3,0:T(8,128)S(1)} fusion(bf16[16,16,8,224]{3,2,1,0:T(8,128)(2,1)S(1)} %all-to-all-done.4, bf16[16,224,448,1]{2,1,0,3:T(8,128)(2,1)} %bitcast.94), kind=kOutput, calls=%fused_computation.24 | convolution fusion | flops 411041792 | bytes 4358144 | tf_op jit(solution)/shard_map/iztc,zcn->itn/dot_general | solution.py:51
  108.1 1.9 collective-permute-start.1
  110.1 1.2 collective-permute-done.1
  111.3 0.8 divide_convert_fusion
  112.1 2.1 collective-permute-start.2
  114.1 1.1 collective-permute-done.2
  115.2 3.2 %fusion.1 = bf16[16,128,224]{1,2,0:T(8,128)(2,1)S(1)} fusion(bf16[128,448,1]{1,0,2:T(8,128)(2,1)S(1)} %bitcast.105, bf16[16,224,448]{2,1,0:T(8,128)(2,1)} %bitcast.95), kind=kOutput, calls=%fused_computation.4 | convolution fusion | flops 411500544 | bytes 4243456 | tf_op jit(solution)/shard_map/mn,zcn->zmc/dot_general | solution.py:63
  118.4 0.5 copy.37
  118.9 1.1 copy.38
  120.0 7.3 %all-to-all-start.5 = ((bf16[16,16,8,224]{3,2,1,0:T(8,128)(2,1)}), bf16[16,16,8,224]{3,2,1,0:T(8,128)(2,1)S(1)}, u32[]{:S(2)}, u32[]{:S(2)}) async-start(bf16[16,16,8,224]{3,2,1,0:T(8,128)(2,1)} %copy.38), calls=%async_computation.6 | async-start | bytes 2097152 | tf_op jit(solution)/shard_map/all_to_all | solution.py:13
  127.3 0.5 copy.31
  128.3 2.1 collective-permute-start
  130.4 13.0 %all-to-all-done.5 = bf16[16,16,8,224]{3,2,1,0:T(8,128)(2,1)S(1)} async-done(((bf16[16,16,8,224]{3,2,1,0:T(8,128)(2,1)}), bf16[16,16,8,224]{3,2,1,0:T(8,128)(2,1)S(1)}, u32[]{:S(2)}, u32[]{:S(2)}) %all-to-all-start.5) | async-done | bytes 917536 | tf_op jit(solution)/shard_map/all_to_all | solution.py:13
  143.6 16.0 %all_to_all.42 = bf16[16,8,224]{2,1,0:T(8,128)(2,1)S(1)} all-to-all(bf16[16,8,224]{2,1,0:T(8,128)(2,1)S(1)} %reduce_sum.38), channel_id=1, replica_groups=mesh['y'=4,'x'=4,'z'=16,'core'=2] {'z'}, dimensions={0} | all-to-all | bytes 114688 | tf_op jit(solution)/shard_map/all_to_all | solution.py:13
  159.6 1.1 broadcast_in_dim.8
  160.7 5.3 %all-to-all-start.7 = ((bf16[16,16,8,224]{3,1,2,0:T(8,128)(2,1)}), bf16[16,16,8,224]{3,1,2,0:T(8,128)(2,1)S(1)}, u32[]{:S(2)}, u32[]{:S(2)}) async-start(bf16[16,16,8,224]{3,1,2,0:T(8,128)(2,1)} %broadcast_in_dim.8), calls=%async_computation.8 | async-start | bytes 2097152 | tf_op jit(solution)/shard_map/all_to_all | solution.py:13
  166.0 0.9 bitcast_add_fusion
  167.0 13.5 %all-to-all-done.7 = bf16[16,16,8,224]{3,1,2,0:T(8,128)(2,1)S(1)} async-done(((bf16[16,16,8,224]{3,1,2,0:T(8,128)(2,1)}), bf16[16,16,8,224]{3,1,2,0:T(8,128)(2,1)S(1)}, u32[]{:S(2)}, u32[]{:S(2)}) %all-to-all-start.7) | async-done | bytes 917536 | tf_op jit(solution)/shard_map/all_to_all | solution.py:13
  180.5 1.3 convolution_bitcast_fusion
  181.7 49.7 %reduce-scatter.2.cloned.1.call-done = f32[1,64,128]{2,1,0:T(8,128)} async-done(((f32[16,64,128]{2,1,0:T(8,128)}), f32[1,64,128]{2,1,0:T(8,128)}) %reduce-scatter.2.cloned.1.call-update) | async-done | bytes 32784 | tf_op jit(solution)/shard_map/reduce_scatter | solution.py:49
  (27 shorter events, 1.9 us)
Async XLA Ops:
  7.2 12.6 %copy-start.2 = (bf16[128,2048]{1,0:T(8,128)(2,1)S(1)}, bf16[128,2048]{1,0:T(8,128)(2,1)}, u32[]{:S(2)}) copy-start(bf16[128,2048]{1,0:T(8,128)(2,1)} %param.6) | copy-start | bytes 1572868
  7.2 98.1 %all-gather.3.cloned.1.call-start = ((), (), s32[]{:S(2)}) async-start(), calls=%async_computation.10 | async-start | bytes 3899392 | tf_op jit(solution)/shard_map/all_gather | solution.py:26
  10.5 22.1 %all-to-all-start = ((bf16[16,224,128]{2,1,0:T(8,128)(2,1)}), bf16[16,224,128]{2,1,0:T(8,128)(2,1)S(1)}, u32[]{:S(2)}, u32[]{:S(2)}) async-start(bf16[16,224,128]{2,1,0:T(8,128)(2,1)} %copy.30), calls=%async_computation | async-start | bytes 1835008 | tf_op jit(solution)/shard_map/all_to_all | solution.py:13
  20.1 60.7 %copy-start = (bf16[128,2048]{0,1:T(8,128)(2,1)}, bf16[128,2048]{0,1:T(8,128)(2,1)S(1)}, u32[]{:S(2)}) copy-start(bf16[128,2048]{0,1:T(8,128)(2,1)S(1)} %copy.32) | copy-start | bytes 1572868
  80.8 18.6 %all-to-all-start.4 = ((bf16[16,16,8,224]{3,2,1,0:T(8,128)(2,1)}), bf16[16,16,8,224]{3,2,1,0:T(8,128)(2,1)S(1)}, u32[]{:S(2)}, u32[]{:S(2)}) async-start(bf16[16,16,8,224]{3,2,1,0:T(8,128)(2,1)} %broadcast_in_dim.7), calls=%async_computation.5 | async-start | bytes 2097152 | tf_op jit(solution)/shard_map/all_to_all | solution.py:13
  100.5 19.6 %all-to-all-start.1 = ((bf16[16,224,128]{2,1,0:T(8,128)(2,1)}), bf16[16,224,128]{2,1,0:T(8,128)(2,1)S(1)}, u32[]{:S(2)}, u32[]{:S(2)}) async-start(bf16[16,224,128]{2,1,0:T(8,128)(2,1)} %broadcast_in_dim.6), calls=%async_computation.1 | async-start | bytes 1835008 | tf_op jit(solution)/shard_map/all_to_all | solution.py:13
  105.3 6.0 %copy-start.3 = (f32[448,64]{0,1:T(8,128)S(1)}, f32[448,64]{0,1:T(8,128)}, u32[]{:S(2)}) copy-start(f32[448,64]{0,1:T(8,128)} %param.8) | copy-start | bytes 344068
  105.3 6.0 %copy-start.4 = (f32[448,64]{0,1:T(8,128)S(1)}, f32[448,64]{0,1:T(8,128)}, u32[]{:S(2)}) copy-start(f32[448,64]{0,1:T(8,128)} %param.9) | copy-start | bytes 344068
  108.1 3.1 %collective-permute-start.1 = (bf16[64,448]{1,0:T(8,128)(2,1)S(1)}, bf16[64,448]{1,0:T(8,128)(2,1)S(1)}, u32[]{:S(2)}, u32[]{:S(2)}) collective-permute-start(bf16[64,448]{1,0:T(8,128)(2,1)S(1)} %fusion.7), channel_id=1, source_target_pairs={{0,1},{1,0},{2,3},{3,2},{4,5},{5,4},{6,7},{7,6},{8,9},{9,8},{10,11... | collective-permute-start | bytes 172040 | tf_op jit(solution)/shard_map/ppermute | solution.py:55
  112.1 3.1 %collective-permute-start.2 = (bf16[64,448]{1,0:T(8,128)(2,1)S(1)}, bf16[64,448]{1,0:T(8,128)(2,1)S(1)}, u32[]{:S(2)}, u32[]{:S(2)}) collective-permute-start(bf16[64,448]{1,0:T(8,128)(2,1)S(1)} %get-tuple-element.4), channel_id=1, source_target_pairs={{0,1},{1,0},{2,3},{3,2},{4,5},{5,4},{6,7},{7,6},{8,9},{9,8},{10,11... | collective-permute-start | bytes 172040 | tf_op jit(solution)/shard_map/ppermute | solution.py:59
  120.0 23.4 %all-to-all-start.5 = ((bf16[16,16,8,224]{3,2,1,0:T(8,128)(2,1)}), bf16[16,16,8,224]{3,2,1,0:T(8,128)(2,1)S(1)}, u32[]{:S(2)}, u32[]{:S(2)}) async-start(bf16[16,16,8,224]{3,2,1,0:T(8,128)(2,1)} %copy.38), calls=%async_computation.6 | async-start | bytes 2097152 | tf_op jit(solution)/shard_map/all_to_all | solution.py:13
  128.2 52.2 %copy-start.1 = (bf16[128,2048]{0,1:T(8,128)(2,1)S(1)}, bf16[128,2048]{0,1:T(8,128)(2,1)}, u32[]{:S(2)}) copy-start(bf16[128,2048]{0,1:T(8,128)(2,1)} %copy-done) | copy-start | bytes 1572868
  128.3 37.7 %collective-permute-start = (bf16[16,64,128]{2,1,0:T(8,128)(2,1)S(1)}, bf16[16,64,128]{2,1,0:T(8,128)(2,1)S(1)}, u32[]{:S(2)}, u32[]{:S(2)}) collective-permute-start(bf16[16,64,128]{2,1,0:T(8,128)(2,1)S(1)} %fusion.5), channel_id=1, source_target_pairs={{0,1},{1,0},{2,3},{3,2},{4,5},{5,4},{6,7},{7,6},{8,9},{9,8},{10,11... | collective-permute-start | bytes 786440 | tf_op jit(solution)/shard_map/ppermute | solution.py:48
  160.7 19.8 %all-to-all-start.7 = ((bf16[16,16,8,224]{3,1,2,0:T(8,128)(2,1)}), bf16[16,16,8,224]{3,1,2,0:T(8,128)(2,1)S(1)}, u32[]{:S(2)}, u32[]{:S(2)}) async-start(bf16[16,16,8,224]{3,1,2,0:T(8,128)(2,1)} %broadcast_in_dim.8), calls=%async_computation.8 | async-start | bytes 2097152 | tf_op jit(solution)/shard_map/all_to_all | solution.py:13
  166.0 65.4 %reduce-scatter.2.cloned.1.call-start = ((), (), s32[]{:S(2)}) async-start(), calls=%async_computation.9 | async-start | bytes 557056 | tf_op jit(solution)/shard_map/reduce_scatter | solution.py:49
Sparse Core Ops, SparseCore 0:
  10.1 84.2 all-gather.2
  170.2 61.1 reduce-scatter.1

commit v2 on v1

v2 whole, which is shorter than its diff:
```python
import jax
import jax.numpy as jnp
from jax import lax
from jax.sharding import Mesh, PartitionSpec as P

D = 7168
DP = ("y", "x")
F32 = jnp.float32
BF16 = jnp.bfloat16
LANES = 128


def exchange(chunks, axes):
    return lax.all_to_all(chunks, axes, 0, 0, tiled=True)


def swap_cores(block):
    return lax.ppermute(block, "core", [(0, 1), (1, 0)])


def to_tiles(block):
    z, sub, cols = block.shape
    block = jnp.pad(block, ((0, 0), (0, 0), (0, 2 * LANES - cols)))
    return block.reshape(z, sub, 2, LANES).transpose(0, 2, 1, 3).reshape(z, 2 * sub, LANES)


def from_tiles(block, cols):
    z, rows, _ = block.shape
    block = block.reshape(z, 2, rows // 2, LANES).transpose(0, 2, 1, 3)
    return block.reshape(z, rows // 2, 2 * LANES)[:, :, :cols]


def on_device(grad_parts, left_basis, right_basis, first_moment, second_moment):
    rows = left_basis.shape[0]
    cols = right_basis.shape[0]
    turns = right_basis.shape[1]
    n_dp = left_basis.shape[1] // rows
    n_z = lax.axis_size("z")
    sub = rows // n_dp
    half = rows // 2
    core = lax.axis_index("core")

    def both(block):
        theirs = swap_cores(block)
        return jnp.where(core == 0, jnp.stack([block, theirs]), jnp.stack([theirs, block]))

    basis_z = lax.all_gather(right_basis, "z", axis=0, tiled=False)

    parts = grad_parts[0].T.reshape(cols, n_dp, rows).transpose(1, 0, 2)
    grad_t = jnp.sum(exchange(parts, DP).astype(F32), axis=0).astype(BF16)

    basis_p = (
        left_basis.reshape(rows, n_z, n_dp, sub).transpose(0, 2, 1, 3).reshape(rows, n_dp, rows)
    )
    left_term = lax.dot_general(
        basis_p, grad_t, (((0,), (1,)), ((), ())), preferred_element_type=F32
    )
    turned = exchange(left_term.astype(BF16), DP)
    turned, copies = lax.optimization_barrier(
        (turned, jnp.broadcast_to(grad_t[None], (n_dp, cols, rows)))
    )
    turned = jnp.sum(turned.astype(F32), axis=0).astype(BF16)
    turned, grad_all, moments = lax.optimization_barrier(
        (turned, exchange(copies, DP), both(jnp.stack([first_moment.T, second_moment.T])))
    )
    turned = exchange(turned.reshape(n_z, sub, cols), "z")

    gram = lax.dot_general(
        grad_all, grad_t, (((1,), (0,)), ((), ())), preferred_element_type=F32
    ).reshape(n_z, 2, half, rows) / D
    mine = lax.dynamic_index_in_dim(gram, core, 1, keepdims=False)
    other = lax.dynamic_index_in_dim(gram, 1 - core, 1, keepdims=False)
    gram = (mine + swap_cores(other.astype(BF16)).astype(F32)).astype(BF16)

    turned, gram = lax.optimization_barrier((turned, gram))
    turned = exchange(jnp.broadcast_to(turned[None], (n_dp, n_z, sub, cols)), DP)

    rotated = jnp.einsum("iztc,zcn->itn", turned, basis_z, preferred_element_type=F32)
    rotated = rotated.reshape(rows, turns)
    rotated = rotated + swap_cores(rotated.astype(BF16)).astype(F32)
    new_first = 0.9 * moments[:, 0].reshape(rows, turns) + 0.1 * rotated
    new_second = 0.95 * moments[:, 1].reshape(rows, turns) + 0.05 * rotated * rotated
    update = (new_first / 0.19 / (jnp.sqrt(new_second / 0.0975) + 1e-08)).astype(BF16)
    new_first = lax.dynamic_slice_in_dim(new_first, core * half, half, 0)
    new_second = lax.dynamic_slice_in_dim(new_second, core * half, half, 0)

    back = jnp.einsum("mn,zcn->zmc", update, basis_z, preferred_element_type=F32).astype(BF16)
    back = back.reshape(n_z, n_dp, sub, cols).transpose(1, 0, 2, 3)
    back = jnp.sum(exchange(back, DP).astype(F32), axis=0).astype(BF16)
    packed = exchange(jnp.concatenate([to_tiles(back), gram], axis=1), "z")
    back = from_tiles(packed[:, : 2 * sub], cols)
    left_gram = jnp.sum(packed[:, 2 * sub :].astype(F32), axis=0)
    back = exchange(jnp.broadcast_to(back[None], (n_dp, n_z, sub, cols)), DP)
    direction = jnp.dot(
        basis_p.reshape(rows, n_dp * rows),
        back.reshape(n_dp * rows, cols),
        preferred_element_type=F32,
    )
    return (left_gram.T, new_first.T, new_second.T, direction)


def solution(mesh):
    n_dp, n_col = mesh.shape["dp"], mesh.shape["col"]
    side = int(round(n_dp**0.5))
    fine = Mesh(
        mesh.devices.reshape(side, side, n_col // 2, 2), ("y", "x", "z", "core")
    )
    dp, col = ("y", "x"), ("z", "core")
    in_specs = (P(dp, None, col), P(dp, None), P(col, dp), P(dp, col), P(dp, col))
    out_specs = (P(dp, col), P(dp, col), P(dp, col), P(dp, col))
    return jax.shard_map(
        on_device, mesh=fine, in_specs=in_specs, out_specs=out_specs, check_vma=False
    )
```

time: 239 us -> 204 us (0.85)
  the two profiles are of different devices: /device:TPU:2 before, /device:TPU:32 now
where the time goes in v2:
time: 204 us
  blocking collectives  81.9 us (40%)
  waiting for transfers between devices  55.6 us (27%)
  starting transfers between devices  35.3 us (17%)
  between operations  14.3 us (7%)
  local copies, waits for them, and re-layouts  7.72 us (4%)
  matrix products  6.2 us (3%)
  other arithmetic  2.46 us (1%)
    all_to_all x4, blocking collectives, exchange(): return lax.all_to_all(chunks, axes, 0, 0, tiled=True)  81.9 us
    all_to_all x4, waiting for transfers between devices, exchange(): return lax.all_to_all(chunks, axes, 0, 0, tiled=True)  52.1 us
    all_to_all x4, starting transfers between devices, exchange(): return lax.all_to_all(chunks, axes, 0, 0, tiled=True)  29.5 us
    ppermute x3, starting transfers between devices, swap_cores(): return lax.ppermute(block, 'core', [(0, 1), (1, 0)])  5.76 us
  transfers between devices with their start and end apart: 8, of which 6 were waited for; matrix products, arithmetic and copies ran while one was open for 4% of the time, Pallas kernels for 0%

profile of v2, /device:TPU:32, one launch (start us, length us, event | category | flops | bytes accessed | tf_op | source)
XLA Modules:
  0.0 203.5 jit_solution(575497357553699418)
XLA Ops:
  7.2 0.7 all-gather.3.cloned.1.call-update
  7.9 1.4 copy.47
  9.3 1.2 copy.30
  10.4 7.0 %all-to-all-start = ((bf16[16,224,128]{2,1,0:T(8,128)(2,1)}), bf16[16,224,128]{2,1,0:T(8,128)(2,1)S(1)}, u32[]{:S(2)}, u32[]{:S(2)}) async-start(bf16[16,224,128]{2,1,0:T(8,128)(2,1)} %copy.30), calls=%async_computation | async-start | bytes 1835008 | tf_op jit(solution)/shard_map/all_to_all | solution.py:14
  17.8 15.8 %all-to-all-done = bf16[16,224,128]{2,1,0:T(8,128)(2,1)S(1)} async-done(((bf16[16,224,128]{2,1,0:T(8,128)(2,1)}), bf16[16,224,128]{2,1,0:T(8,128)(2,1)S(1)}, u32[]{:S(2)}, u32[]{:S(2)}) %all-to-all-start) | async-done | bytes 917536 | tf_op jit(solution)/shard_map/all_to_all | solution.py:14
  34.1 18.1 %all_to_all.40 = bf16[16,128,224]{1,2,0:T(8,128)(2,1)S(1)} all-to-all(bf16[16,128,224]{1,2,0:T(8,128)(2,1)S(1)} %fusion), channel_id=1, replica_groups=mesh['y'=4,'x'=4,'z'=16,'core'=2] {'y','x'}, dimensions={0} | all-to-all | bytes 1835008 | tf_op jit(solution)/shard_map/all_to_all | solution.py:14
  52.2 1.1 broadcast_in_dim.6
  53.2 3.6 %all-to-all-start.2 = ((bf16[16,224,128]{2,1,0:T(8,128)(2,1)}), bf16[16,224,128]{2,1,0:T(8,128)(2,1)S(1)}, u32[]{:S(2)}, u32[]{:S(2)}) async-start(bf16[16,224,128]{2,1,0:T(8,128)(2,1)} %broadcast_in_dim.6), calls=%async_computation.2 | async-start | bytes 1835008 | tf_op jit(solution)/shard_map/all_to_all | solution.py:14
  56.9 1.9 collective-permute-start
  58.9 1.6 collective-permute-done
  60.5 1.1 maximum_select_fusion
  61.7 10.0 %all-to-all-done.2 = bf16[16,224,128]{2,1,0:T(8,128)(2,1)S(1)} async-done(((bf16[16,224,128]{2,1,0:T(8,128)(2,1)}), bf16[16,224,128]{2,1,0:T(8,128)(2,1)S(1)}, u32[]{:S(2)}, u32[]{:S(2)}) %all-to-all-start.2) | async-done | bytes 917536 | tf_op jit(solution)/shard_map/all_to_all | solution.py:14
  71.7 0.5 copy.35
  72.2 0.4 convolution_multiply_fusion
  72.7 1.9 collective-permute-start.1
  74.7 0.7 copy.34
  75.4 15.2 %all-to-all-start.3 = ((bf16[16,8,224]{2,1,0:T(8,128)(2,1)}), bf16[16,8,224]{2,1,0:T(8,128)(2,1)S(1)}, u32[]{:S(2)}, u32[]{:S(2)}) async-start(bf16[16,8,224]{2,1,0:T(8,128)(2,1)} %bitcast.15), calls=%async_computation.3 | async-start | bytes 131072 | tf_op jit(solution)/shard_map/all_to_all | solution.py:14
  90.7 12.5 %all-to-all-done.3 = bf16[16,8,224]{2,1,0:T(8,128)(2,1)S(1)} async-done(((bf16[16,8,224]{2,1,0:T(8,128)(2,1)}), bf16[16,8,224]{2,1,0:T(8,128)(2,1)S(1)}, u32[]{:S(2)}, u32[]{:S(2)}) %all-to-all-start.3) | async-done | bytes 57376 | tf_op jit(solution)/shard_map/all_to_all | solution.py:14
  103.3 19.2 %all_to_all.41 = bf16[16,16,8,224]{3,2,1,0:T(8,128)(2,1)S(1)} all-to-all(bf16[16,16,8,224]{3,2,1,0:T(8,128)(2,1)S(1)} %broadcast_in_dim.7), channel_id=1, replica_groups=mesh['y'=4,'x'=4,'z'=16,'core'=2] {'y','x'}, dimensions={0} | all-to-all | bytes 1835008 | tf_op jit(solution)/shard_map/all_to_all | solution.py:14
  122.5 2.9 %fusion.17 = (bf16[128,448]{1,0:T(8,128)(2,1)S(1)}, f32[128,448]{1,0:T(8,128)S(1)}) fusion(bf16[16,16,8,224]{3,2,1,0:T(8,128)(2,1)S(1)} %all_to_all.41, bf16[16,224,448,1]{2,1,0,3:T(8,128)(2,1)} %bitcast.91), kind=kOutput, calls=%fused_computation.38 | convolution fusion | flops 411099136 | bytes 4472832 | tf_op jit(solution)/shard_map/iztc,zcn->itn/dot_general | solution.py:78
  125.4 1.9 collective-permute-start.2
  127.4 1.3 collective-permute-done.2
  128.7 1.2 fusion.1
  130.0 0.5 copy.37
  130.6 20.4 %all_to_all.42 = bf16[16,16,8,224]{3,2,1,0:T(8,128)(2,1)S(1)} all-to-all(bf16[16,16,8,224]{3,2,1,0:T(8,128)(2,1)S(1)} %copy.38), channel_id=1, replica_groups=mesh['y'=4,'x'=4,'z'=16,'core'=2] {'y','x'}, dimensions={0} | all-to-all | bytes 1835008 | tf_op jit(solution)/shard_map/all_to_all | solution.py:14
  151.2 24.2 %all_to_all.43 = bf16[16,80,128]{2,1,0:T(8,128)(2,1)S(1)} all-to-all(bf16[16,80,128]{2,1,0:T(8,128)(2,1)S(1)} %pad_maximum_fusion), channel_id=1, replica_groups=mesh['y'=4,'x'=4,'z'=16,'core'=2] {'z'}, dimensions={0} | all-to-all | bytes 655360 | tf_op jit(solution)/shard_map/all_to_all | solution.py:14
  175.4 1.1 broadcast_in_dim.8
  176.5 3.7 %all-to-all-start.7 = ((bf16[16,16,8,224]{3,1,2,0:T(8,128)(2,1)}), bf16[16,16,8,224]{3,1,2,0:T(8,128)(2,1)S(1)}, u32[]{:S(2)}, u32[]{:S(2)}) async-start(bf16[16,16,8,224]{3,1,2,0:T(8,128)(2,1)} %broadcast_in_dim.8), calls=%async_computation.7 | async-start | bytes 2097152 | tf_op jit(solution)/shard_map/all_to_all | solution.py:14
  180.2 0.7 dynamic-slice_bitcast_fusion
  180.9 0.7 convert_reduce_fusion
  181.6 13.8 %all-to-all-done.7 = bf16[16,16,8,224]{3,1,2,0:T(8,128)(2,1)S(1)} async-done(((bf16[16,16,8,224]{3,1,2,0:T(8,128)(2,1)}), bf16[16,16,8,224]{3,1,2,0:T(8,128)(2,1)S(1)}, u32[]{:S(2)}, u32[]{:S(2)}) %all-to-all-start.7) | async-done | bytes 917536 | tf_op jit(solution)/shard_map/all_to_all | solution.py:14
  195.4 1.3 convolution_bitcast_fusion.1
  (27 shorter events, 1.7 us)
Async XLA Ops:
  7.2 10.3 %copy-start.1 = (bf16[128,2048]{1,0:T(8,128)(2,1)S(1)}, bf16[128,2048]{1,0:T(8,128)(2,1)}, u32[]{:S(2)}) copy-start(bf16[128,2048]{1,0:T(8,128)(2,1)} %param.6) | copy-start | bytes 1572868
  7.2 115.3 %all-gather.3.cloned.1.call-start = ((), (), s32[]{:S(2)}) async-start(), calls=%async_computation.8 | async-start | bytes 3899392 | tf_op jit(solution)/shard_map/all_gather | solution.py:47
  10.4 23.1 %all-to-all-start = ((bf16[16,224,128]{2,1,0:T(8,128)(2,1)}), bf16[16,224,128]{2,1,0:T(8,128)(2,1)S(1)}, u32[]{:S(2)}, u32[]{:S(2)}) async-start(bf16[16,224,128]{2,1,0:T(8,128)(2,1)} %copy.30), calls=%async_computation | async-start | bytes 1835008 | tf_op jit(solution)/shard_map/all_to_all | solution.py:14
  17.8 39.1 %copy-start.2 = (f32[448,64]{0,1:T(8,128)S(1)}, f32[448,64]{0,1:T(8,128)}, u32[]{:S(2)}) copy-start(f32[448,64]{0,1:T(8,128)} %param.9) | copy-start | bytes 344068
  17.8 39.1 %copy-start.3 = (f32[448,64]{0,1:T(8,128)S(1)}, f32[448,64]{0,1:T(8,128)}, u32[]{:S(2)}) copy-start(f32[448,64]{0,1:T(8,128)} %param.8) | copy-start | bytes 344068
  53.2 18.5 %all-to-all-start.2 = ((bf16[16,224,128]{2,1,0:T(8,128)(2,1)}), bf16[16,224,128]{2,1,0:T(8,128)(2,1)S(1)}, u32[]{:S(2)}, u32[]{:S(2)}) async-start(bf16[16,224,128]{2,1,0:T(8,128)(2,1)} %broadcast_in_dim.6), calls=%async_computation.2 | async-start | bytes 1835008 | tf_op jit(solution)/shard_map/all_to_all | solution.py:14
  56.9 3.6 %collective-permute-start = (f32[2,64,448]{2,1,0:T(8,128)S(1)}, f32[2,64,448]{2,1,0:T(8,128)}, u32[]{:S(2)}, u32[]{:S(2)}) collective-permute-start(f32[2,64,448]{2,1,0:T(8,128)S(1)} %get-tuple-element.23), channel_id=1, source_target_pairs={{0,1},{1,0},{2,3},{3,2},{4,5},{5,4},{6,7},{7,6},{8,9},{9,8},{10,11... | collective-permute-start | bytes 688136 | tf_op jit(solution)/shard_map/ppermute | solution.py:18
  72.7 17.9 %collective-permute-start.1 = (bf16[16,64,128]{2,1,0:T(8,128)(2,1)S(1)}, bf16[16,64,128]{2,1,0:T(8,128)(2,1)S(1)}, u32[]{:S(2)}, u32[]{:S(2)}) collective-permute-start(bf16[16,64,128]{2,1,0:T(8,128)(2,1)S(1)} %fusion.7), channel_id=1, source_target_pairs={{0,1},{1,0},{2,3},{3,2},{4,5},{5,4},{6,7},{7,6},{8,9},{9,8},{10,11... | collective-permute-start | bytes 786440 | tf_op jit(solution)/shard_map/ppermute | solution.py:18
  75.4 27.8 %all-to-all-start.3 = ((bf16[16,8,224]{2,1,0:T(8,128)(2,1)}), bf16[16,8,224]{2,1,0:T(8,128)(2,1)S(1)}, u32[]{:S(2)}, u32[]{:S(2)}) async-start(bf16[16,8,224]{2,1,0:T(8,128)(2,1)} %bitcast.15), calls=%async_computation.3 | async-start | bytes 131072 | tf_op jit(solution)/shard_map/all_to_all | solution.py:14
  122.5 6.3 %copy-start = (bf16[3584,448]{1,0:T(8,128)(2,1)S(1)}, bf16[3584,448]{1,0:T(8,128)(2,1)}, u32[]{:S(2)}) copy-start(bf16[3584,448]{1,0:T(8,128)(2,1)} %all-gather.3.cloned.1.call-done) | copy-start | bytes 9633796
  125.4 3.2 %collective-permute-start.2 = (bf16[128,448]{1,0:T(8,128)(2,1)S(1)}, bf16[128,448]{1,0:T(8,128)(2,1)S(1)}, u32[]{:S(2)}, u32[]{:S(2)}) collective-permute-start(bf16[128,448]{1,0:T(8,128)(2,1)S(1)} %get-tuple-element.24), channel_id=1, source_target_pairs={{0,1},{1,0},{2,3},{3,2},{4,5},{5,4},{6,7},{7,6},{8,9},{9,8},{10,11... | collective-permute-start | bytes 344072 | tf_op jit(solution)/shard_map/ppermute | solution.py:18
  176.5 18.9 %all-to-all-start.7 = ((bf16[16,16,8,224]{3,1,2,0:T(8,128)(2,1)}), bf16[16,16,8,224]{3,1,2,0:T(8,128)(2,1)S(1)}, u32[]{:S(2)}, u32[]{:S(2)}) async-start(bf16[16,16,8,224]{3,1,2,0:T(8,128)(2,1)} %broadcast_in_dim.8), calls=%async_computation.7 | async-start | bytes 2097152 | tf_op jit(solution)/shard_map/all_to_all | solution.py:14
Sparse Core Ops, SparseCore 0:
  10.1 81.7 all-gather.2

commit v3 on v2

--- a/solution.py
+++ b/solution.py
@@ -55,15 +55,20 @@
     left_term = lax.dot_general(
         basis_p, grad_t, (((0,), (1,)), ((), ())), preferred_element_type=F32
     )
-    turned = exchange(left_term.astype(BF16), DP)
-    turned, copies = lax.optimization_barrier(
-        (turned, jnp.broadcast_to(grad_t[None], (n_dp, cols, rows)))
+    turned, moments = lax.optimization_barrier(
+        (
+            exchange(left_term.astype(BF16), DP),
+            both(jnp.stack([first_moment.T, second_moment.T])),
+        )
     )
-    turned = jnp.sum(turned.astype(F32), axis=0).astype(BF16)
-    turned, grad_all, moments = lax.optimization_barrier(
-        (turned, exchange(copies, DP), both(jnp.stack([first_moment.T, second_moment.T])))
+    turned = jnp.sum(turned.astype(F32), axis=0).astype(BF16).reshape(n_z, sub, cols)
+
+    turned, grad_here = lax.optimization_barrier((turned, grad_t))
+    turned, grad_all = lax.optimization_barrier(
+        (exchange(turned, "z"), lax.all_gather(grad_here, DP, axis=0, tiled=False))
     )
-    turned = exchange(turned.reshape(n_z, sub, cols), "z")
+    turned = turned.transpose(1, 0, 2).reshape(1, sub, n_z * cols)
+    turned = exchange(jnp.broadcast_to(turned, (n_dp, sub, n_z * cols)), DP)
 
     gram = lax.dot_general(
         grad_all, grad_t, (((1,), (0,)), ((), ())), preferred_element_type=F32
@@ -71,12 +76,12 @@
     mine = lax.dynamic_index_in_dim(gram, core, 1, keepdims=False)
     other = lax.dynamic_index_in_dim(gram, 1 - core, 1, keepdims=False)
     gram = (mine + swap_cores(other.astype(BF16)).astype(F32)).astype(BF16)
+    turned, gram = lax.optimization_barrier((turned, gram))
 
-    turned, gram = lax.optimization_barrier((turned, gram))
-    turned = exchange(jnp.broadcast_to(turned[None], (n_dp, n_z, sub, cols)), DP)
-
-    rotated = jnp.einsum("iztc,zcn->itn", turned, basis_z, preferred_element_type=F32)
-    rotated = rotated.reshape(rows, turns)
+    basis_z = basis_z.reshape(n_z * cols, turns)
+    rotated = jnp.dot(
+        turned.reshape(rows, n_z * cols), basis_z, preferred_element_type=F32
+    )
     rotated = rotated + swap_cores(rotated.astype(BF16)).astype(F32)
     new_first = 0.9 * moments[:, 0].reshape(rows, turns) + 0.1 * rotated
     new_second = 0.95 * moments[:, 1].reshape(rows, turns) + 0.05 * rotated * rotated
@@ -84,17 +89,19 @@
     new_first = lax.dynamic_slice_in_dim(new_first, core * half, half, 0)
     new_second = lax.dynamic_slice_in_dim(new_second, core * half, half, 0)
 
-    back = jnp.einsum("mn,zcn->zmc", update, basis_z, preferred_element_type=F32).astype(BF16)
-    back = back.reshape(n_z, n_dp, sub, cols).transpose(1, 0, 2, 3)
-    back = jnp.sum(exchange(back, DP).astype(F32), axis=0).astype(BF16)
+    back = lax.dot_general(
+        update, basis_z, (((1,), (1,)), ((), ())), preferred_element_type=F32
+    ).astype(BF16)
+    back = exchange(back.reshape(n_dp, sub, n_z * cols), DP)
+    back = jnp.sum(back.astype(F32), axis=0).astype(BF16)
+    back = back.reshape(sub, n_z, cols).transpose(1, 0, 2)
     packed = exchange(jnp.concatenate([to_tiles(back), gram], axis=1), "z")
     back = from_tiles(packed[:, : 2 * sub], cols)
     left_gram = jnp.sum(packed[:, 2 * sub :].astype(F32), axis=0)
-    back = exchange(jnp.broadcast_to(back[None], (n_dp, n_z, sub, cols)), DP)
-    direction = jnp.dot(
-        basis_p.reshape(rows, n_dp * rows),
-        back.reshape(n_dp * rows, cols),
-        preferred_element_type=F32,
+    back = back.reshape(rows, cols).T
+    back = exchange(jnp.broadcast_to(back[None], (n_dp, cols, rows)), DP)
+    direction = lax.dot_general(
+        basis_p, back, (((1, 2), (0, 2)), ((), ())), preferred_element_type=F32
     )
     return (left_gram.T, new_first.T, new_second.T, direction)
 

time: 204 us -> 200 us (0.980)
  blocking collectives: 81.9 us -> 74 us
  waiting for transfers between devices: 55.6 us -> 48.4 us
  starting transfers between devices: 35.3 us -> 40.2 us
  matrix products: 6.2 us -> 10.6 us
    all_to_all x4 -> x2, blocking collectives: 81.9 us -> 51.6 us  [exchange(): return lax.all_to_all(chunks, axes, 0, 0, tiled=True)]
    all_gather x0 -> x1, blocking collectives: none -> 22.4 us  [on_device(): lax.all_gather(grad_here, DP, axis=0, tiled=False)]
    all_to_all x4 -> x5, waiting for transfers between devices: 52.1 us -> 43.7 us  [exchange(): return lax.all_to_all(chunks, axes, 0, 0, tiled=True)]
    all_to_all x4 -> x5, starting transfers between devices: 29.5 us -> 34.3 us  [exchange(): return lax.all_to_all(chunks, axes, 0, 0, tiled=True)]
    dot_general x3, matrix products: 5.37 us -> 8 us  [the longest x1 3.52 us: on_device(): jnp.dot(turned.reshape(rows, n_z * cols), basis_z, preferred_element_type...]
  transfers between devices with their start and end apart: 8 -> 9, of which waited for: 6 -> 7; matrix products, arithmetic and copies ran while one was open for 4% -> 6% of each run, Pallas kernels for 0% -> 0%
where the time goes in v3:
time: 200 us; the launch traced here: 199 us
  blocking collectives  74 us (37%)
  waiting for transfers between devices  48.4 us (24%)
  starting transfers between devices  40.2 us (20%)
  between operations  14.3 us (7%)
  matrix products  10.6 us (5%)
  local copies, waits for them, and re-layouts  8.63 us (4%)
  other arithmetic  2.83 us (1%)
    all_to_all x2, blocking collectives, exchange(): return lax.all_to_all(chunks, axes, 0, 0, tiled=True)  51.6 us
    all_to_all x5, waiting for transfers between devices, exchange(): return lax.all_to_all(chunks, axes, 0, 0, tiled=True)  43.7 us
    all_to_all x5, starting transfers between devices, exchange(): return lax.all_to_all(chunks, axes, 0, 0, tiled=True)  34.3 us
    all_gather x1, blocking collectives, on_device(): lax.all_gather(grad_here, DP, axis=0, tiled=False)  22.4 us
    ppermute x3, starting transfers between devices, swap_cores(): return lax.ppermute(block, 'core', [(0, 1), (1, 0)])  5.89 us
  transfers between devices with their start and end apart: 9, of which 7 were waited for; matrix products, arithmetic and copies ran while one was open for 6% of the time, Pallas kernels for 0%

profile of v3, /device:TPU:32, one launch (start us, length us, event | category | flops | bytes accessed | tf_op | source)
XLA Modules:
  0.0 199.0 jit_solution(806816985132028405)
XLA Ops:
  7.9 1.4 copy.68
  9.3 1.2 copy.50
  10.5 7.2 %all-to-all-start = ((bf16[16,224,128]{2,1,0:T(8,128)(2,1)}), bf16[16,224,128]{2,1,0:T(8,128)(2,1)S(1)}, u32[]{:S(2)}, u32[]{:S(2)}) async-start(bf16[16,224,128]{2,1,0:T(8,128)(2,1)} %copy.50), calls=%async_computation | async-start | bytes 1835008 | tf_op jit(solution)/shard_map/all_to_all | solution.py:14
  17.9 15.8 %all-to-all-done = bf16[16,224,128]{2,1,0:T(8,128)(2,1)S(1)} async-done(((bf16[16,224,128]{2,1,0:T(8,128)(2,1)}), bf16[16,224,128]{2,1,0:T(8,128)(2,1)S(1)}, u32[]{:S(2)}, u32[]{:S(2)}) %all-to-all-start) | async-done | bytes 917536 | tf_op jit(solution)/shard_map/all_to_all | solution.py:14
  33.8 1.4 fusion.1
  35.2 3.6 %all-to-all-start.1 = ((bf16[16,128,224]{1,2,0:T(8,128)(2,1)}), bf16[16,128,224]{1,2,0:T(8,128)(2,1)S(1)}, u32[]{:S(2)}, u32[]{:S(2)}) async-start(bf16[16,128,224]{1,2,0:T(8,128)(2,1)} %fusion.1), calls=%async_computation.1 | async-start | bytes 1835008 | tf_op jit(solution)/shard_map/all_to_all | solution.py:14
  38.9 1.9 collective-permute-start
  40.8 1.5 collective-permute-done
  42.3 0.8 maximum_select_fusion
  43.2 10.5 %all-to-all-done.1 = bf16[16,128,224]{1,2,0:T(8,128)(2,1)S(1)} async-done(((bf16[16,128,224]{1,2,0:T(8,128)(2,1)}), bf16[16,128,224]{1,2,0:T(8,128)(2,1)S(1)}, u32[]{:S(2)}, u32[]{:S(2)}) %all-to-all-start.1) | async-done | bytes 917536 | tf_op jit(solution)/shard_map/all_to_all | solution.py:14
  53.8 0.7 copy.54
  54.5 15.2 %all-to-all-start.2 = ((bf16[16,8,224]{2,1,0:T(8,128)(2,1)}), bf16[16,8,224]{2,1,0:T(8,128)(2,1)S(1)}, u32[]{:S(2)}, u32[]{:S(2)}) async-start(bf16[16,8,224]{2,1,0:T(8,128)(2,1)} %bitcast.15), calls=%async_computation.2 | async-start | bytes 131072 | tf_op jit(solution)/shard_map/all_to_all | solution.py:14
  69.8 22.4 %all-gather = bf16[3584,128]{1,0:T(8,128)(2,1)S(1)} all-gather(bf16[224,128]{1,0:T(8,128)(2,1)S(1)} %reduce_sum.45), channel_id=2, replica_groups=mesh['y'=4,'x'=4,'z'=16,'core'=2] {'y','x'}, dimensions={0}, use_global_device_ids=true | all-gather | bytes 974848 | tf_op jit(solution)/shard_map/all_gather | solution.py:68
  92.9 1.0 broadcast_in_dim.14
  93.9 4.6 %all-to-all-start.3 = ((bf16[16,8,3584]{2,1,0:T(8,128)(2,1)}), bf16[16,8,3584]{2,1,0:T(8,128)(2,1)S(1)}, u32[]{:S(2)}, u32[]{:S(2)}) async-start(bf16[16,8,3584]{2,1,0:T(8,128)(2,1)} %broadcast_in_dim.14), calls=%async_computation.3 | async-start | bytes 1835008 | tf_op jit(solution)/shard_map/all_to_all | solution.py:14
  98.5 1.2 convolution_multiply_fusion
  99.8 2.1 %collective-permute-start.1 = (bf16[16,64,128]{2,1,0:T(8,128)(2,1)S(1)}, bf16[16,64,128]{2,1,0:T(8,128)(2,1)S(1)}, u32[]{:S(2)}, u32[]{:S(2)}) collective-permute-start(bf16[16,64,128]{2,1,0:T(8,128)(2,1)S(1)} %fusion.9), channel_id=1, source_target_pairs={{0,1},{1,0},{2,3},{3,2},{4,5},{5,4},{6,7},{7,6},{8,9},{9,8},{10,11... | collective-permute-start | bytes 786440 | tf_op jit(solution)/shard_map/ppermute | solution.py:18
  101.9 1.5 collective-permute-done.1
  103.4 0.8 fusion.4
  104.2 6.8 %all-to-all-done.3 = bf16[16,8,3584]{2,1,0:T(8,128)(2,1)S(1)} async-done(((bf16[16,8,3584]{2,1,0:T(8,128)(2,1)}), bf16[16,8,3584]{2,1,0:T(8,128)(2,1)S(1)}, u32[]{:S(2)}, u32[]{:S(2)}) %all-to-all-start.3) | async-done | bytes 917536 | tf_op jit(solution)/shard_map/all_to_all | solution.py:14
  111.0 3.5 %fusion.20 = (bf16[128,448]{0,1:T(8,128)(2,1)S(1)}, f32[128,448]{0,1:T(8,128)S(1)}) fusion(bf16[3584,448]{1,0:T(8,128)(2,1)} %all-gather.4.cloned.1.call-done, bf16[16,8,3584]{2,1,0:T(8,128)(2,1)S(1)} %all-to-all-done.3), kind=kOutput, calls=%fused_computation.41 | convolution fusion | flops 411099136 | bytes 4472832 | tf_op jit(solution)/shard_map/dot_general | solution.py:82
  114.5 1.9 collective-permute-start.2
  116.8 1.0 collective-permute-done.2
  117.8 3.4 %fusion = bf16[16,8,3584]{2,1,0:T(8,128)(2,1)S(1)} fusion(bf16[3584,448]{1,0:T(8,128)(2,1)} %all-gather.4.cloned.1.call-done, f32[128,448]{0,1:T(8,128)S(1)} %get-tuple-element.43, f32[128,448]{0,1:T(8,128)S(1)} %get-tuple-element.42), kind=kOutput, calls=%fused_computation.1 | convolution fusion | flops 411787264 | bytes 4587520 | tf_op jit(solution)/shard_map/dot_general | solution.py:92
  121.2 19.1 %all_to_all.35 = bf16[16,8,3584]{2,1,0:T(8,128)(2,1)S(1)} all-to-all(bf16[16,8,3584]{2,1,0:T(8,128)(2,1)S(1)} %fusion), channel_id=1, replica_groups=mesh['y'=4,'x'=4,'z'=16,'core'=2] {'y','x'}, dimensions={0} | all-to-all | bytes 1835008 | tf_op jit(solution)/shard_map/all_to_all | solution.py:14
  140.7 32.6 %all_to_all.36 = bf16[16,80,128]{2,1,0:T(8,128)(2,1)S(1)} all-to-all(bf16[16,80,128]{2,1,0:T(8,128)(2,1)S(1)} %pad_maximum_fusion), channel_id=1, replica_groups=mesh['y'=4,'x'=4,'z'=16,'core'=2] {'z'}, dimensions={0} | all-to-all | bytes 655360 | tf_op jit(solution)/shard_map/all_to_all | solution.py:14
  173.4 1.1 broadcast_in_dim.15
  174.4 3.6 %all-to-all-start.6 = ((bf16[16,224,128]{2,1,0:T(8,128)(2,1)}), bf16[16,224,128]{2,1,0:T(8,128)(2,1)S(1)}, u32[]{:S(2)}, u32[]{:S(2)}) async-start(bf16[16,224,128]{2,1,0:T(8,128)(2,1)} %broadcast_in_dim.15), calls=%async_computation.6 | async-start | bytes 1835008 | tf_op jit(solution)/shard_map/all_to_all | solution.py:14
  178.2 0.8 copy.62
  179.0 0.8 copy.63
  180.4 10.7 %all-to-all-done.6 = bf16[16,224,128]{2,1,0:T(8,128)(2,1)S(1)} async-done(((bf16[16,224,128]{2,1,0:T(8,128)(2,1)}), bf16[16,224,128]{2,1,0:T(8,128)(2,1)S(1)}, u32[]{:S(2)}, u32[]{:S(2)}) %all-to-all-start.6) | async-done | bytes 917536 | tf_op jit(solution)/shard_map/all_to_all | solution.py:14
  191.1 1.0 convolution_bitcast_fusion
  (38 shorter events, 3.7 us)
Async XLA Ops:
  7.2 10.5 %copy-start.3 = (bf16[128,2048]{1,0:T(8,128)(2,1)S(1)}, bf16[128,2048]{1,0:T(8,128)(2,1)}, u32[]{:S(2)}) copy-start(bf16[128,2048]{1,0:T(8,128)(2,1)} %param.6) | copy-start | bytes 1572868
  7.2 103.8 %all-gather.4.cloned.1.call-start = ((), (), s32[]{:S(2)}) async-start(), calls=%async_computation.7 | async-start | bytes 3899392 | tf_op jit(solution)/shard_map/all_gather | solution.py:47
  10.5 28.4 %copy-start.4 = (f32[448,64]{0,1:T(8,128)S(1)}, f32[448,64]{0,1:T(8,128)}, u32[]{:S(2)}) copy-start(f32[448,64]{0,1:T(8,128)} %param.9) | copy-start | bytes 344068
  10.5 28.4 %copy-start.5 = (f32[448,64]{0,1:T(8,128)S(1)}, f32[448,64]{0,1:T(8,128)}, u32[]{:S(2)}) copy-start(f32[448,64]{0,1:T(8,128)} %param.8) | copy-start | bytes 344068
  10.5 23.2 %all-to-all-start = ((bf16[16,224,128]{2,1,0:T(8,128)(2,1)}), bf16[16,224,128]{2,1,0:T(8,128)(2,1)S(1)}, u32[]{:S(2)}, u32[]{:S(2)}) async-start(bf16[16,224,128]{2,1,0:T(8,128)(2,1)} %copy.50), calls=%async_computation | async-start | bytes 1835008 | tf_op jit(solution)/shard_map/all_to_all | solution.py:14
  33.8 58.3 %copy-start.2 = (bf16[224,128]{1,0:T(8,128)(2,1)}, bf16[224,128]{1,0:T(8,128)(2,1)S(1)}, u32[]{:S(2)}) copy-start(bf16[224,128]{1,0:T(8,128)(2,1)S(1)} %reduce_sum.45) | copy-start | bytes 172036
  35.2 18.5 %all-to-all-start.1 = ((bf16[16,128,224]{1,2,0:T(8,128)(2,1)}), bf16[16,128,224]{1,2,0:T(8,128)(2,1)S(1)}, u32[]{:S(2)}, u32[]{:S(2)}) async-start(bf16[16,128,224]{1,2,0:T(8,128)(2,1)} %fusion.1), calls=%async_computation.1 | async-start | bytes 1835008 | tf_op jit(solution)/shard_map/all_to_all | solution.py:14
  38.9 3.4 %collective-permute-start = (f32[2,64,448]{2,1,0:T(8,128)S(1)}, f32[2,64,448]{2,1,0:T(8,128)S(1)}, u32[]{:S(2)}, u32[]{:S(2)}) collective-permute-start(f32[2,64,448]{2,1,0:T(8,128)S(1)} %get-tuple-element.45), channel_id=1, source_target_pairs={{0,1},{1,0},{2,3},{3,2},{4,5},{5,4},{6,7},{7,6},{8,9},{9,8},{10,11... | collective-permute-start | bytes 688136 | tf_op jit(solution)/shard_map/ppermute | solution.py:18
  54.5 37.6 %all-to-all-start.2 = ((bf16[16,8,224]{2,1,0:T(8,128)(2,1)}), bf16[16,8,224]{2,1,0:T(8,128)(2,1)S(1)}, u32[]{:S(2)}, u32[]{:S(2)}) async-start(bf16[16,8,224]{2,1,0:T(8,128)(2,1)} %bitcast.15), calls=%async_computation.2 | async-start | bytes 131072 | tf_op jit(solution)/shard_map/all_to_all | solution.py:14
  93.9 17.1 %all-to-all-start.3 = ((bf16[16,8,3584]{2,1,0:T(8,128)(2,1)}), bf16[16,8,3584]{2,1,0:T(8,128)(2,1)S(1)}, u32[]{:S(2)}, u32[]{:S(2)}) async-start(bf16[16,8,3584]{2,1,0:T(8,128)(2,1)} %broadcast_in_dim.14), calls=%async_computation.3 | async-start | bytes 1835008 | tf_op jit(solution)/shard_map/all_to_all | solution.py:14
  99.8 16.7 %copy-start = (f32[2,2,64,448]{3,2,1,0:T(8,128)S(1)}, f32[2,2,64,448]{3,2,1,0:T(8,128)}, u32[]{:S(2)}) copy-start(f32[2,2,64,448]{3,2,1,0:T(8,128)} %maximum_select_fusion) | copy-start | bytes 1376260
  99.8 3.6 %collective-permute-start.1 = (bf16[16,64,128]{2,1,0:T(8,128)(2,1)S(1)}, bf16[16,64,128]{2,1,0:T(8,128)(2,1)S(1)}, u32[]{:S(2)}, u32[]{:S(2)}) collective-permute-start(bf16[16,64,128]{2,1,0:T(8,128)(2,1)S(1)} %fusion.9), channel_id=1, source_target_pairs={{0,1},{1,0},{2,3},{3,2},{4,5},{5,4},{6,7},{7,6},{8,9},{9,8},{10,11... | collective-permute-start | bytes 786440 | tf_op jit(solution)/shard_map/ppermute | solution.py:18
  114.5 3.2 %collective-permute-start.2 = (bf16[128,448]{0,1:T(8,128)(2,1)S(1)}, bf16[128,448]{0,1:T(8,128)(2,1)S(1)}, u32[]{:S(2)}, u32[]{:S(2)}) collective-permute-start(bf16[128,448]{0,1:T(8,128)(2,1)S(1)} %get-tuple-element.46), channel_id=1, source_target_pairs={{0,1},{1,0},{2,3},{3,2},{4,5},{5,4},{6,7},{7,6},{8,9},{9,8},{10,11... | collective-permute-start | bytes 344072 | tf_op jit(solution)/shard_map/ppermute | solution.py:18
  117.8 22.8 %copy-start.1 = (bf16[16,64,128]{2,1,0:T(8,128)(2,1)S(1)}, bf16[16,64,128]{2,1,0:T(8,128)(2,1)}, u32[]{:S(2)}) copy-start(bf16[16,64,128]{2,1,0:T(8,128)(2,1)} %fusion.4) | copy-start | bytes 786436
  174.4 16.7 %all-to-all-start.6 = ((bf16[16,224,128]{2,1,0:T(8,128)(2,1)}), bf16[16,224,128]{2,1,0:T(8,128)(2,1)S(1)}, u32[]{:S(2)}, u32[]{:S(2)}) async-start(bf16[16,224,128]{2,1,0:T(8,128)(2,1)} %broadcast_in_dim.15), calls=%async_computation.6 | async-start | bytes 1835008 | tf_op jit(solution)/shard_map/all_to_all | solution.py:14
Sparse Core Ops, SparseCore 0:
  10.1 82.4 all-gather.3

commit v4 on v1

v4 whole, which is shorter than its diff:
```python
import jax
import jax.numpy as jnp
from jax import lax
from jax.sharding import Mesh, PartitionSpec as P

D = 7168
DP = ("y", "x")
Z = ("zh", "zl")
F32 = jnp.float32
BF16 = jnp.bfloat16


def exchange(chunks, axes):
    return lax.all_to_all(chunks, axes, 0, 0, tiled=True)


def swap(block, axis):
    return lax.ppermute(block, axis, [(0, 1), (1, 0)])


def both(block, axis):
    theirs = swap(block, axis)
    return jnp.where(
        lax.axis_index(axis) == 0, jnp.stack([block, theirs]), jnp.stack([theirs, block])
    )


def on_device(grad_parts, left_basis, right_basis, first_moment, second_moment):
    rows = left_basis.shape[0]
    cols = right_basis.shape[0]
    turns = right_basis.shape[1]
    n_dp = left_basis.shape[1] // rows
    n_zh = lax.axis_size("zh")
    n_z = 2 * n_zh
    sub = rows // n_zh
    half = rows // 2
    core = lax.axis_index("core")
    block = n_dp * sub
    depth = n_zh * cols

    basis_z = lax.all_gather(right_basis, "zh", axis=0, tiled=True)

    parts = grad_parts[0].T.reshape(cols, n_dp, rows).transpose(1, 0, 2)
    grad_t = jnp.sum(exchange(parts, DP).astype(F32), axis=0).astype(BF16)

    basis_p = (
        left_basis.reshape(rows, n_zh, n_dp, sub).transpose(0, 2, 1, 3).reshape(rows, n_dp, rows)
    )
    left_term = lax.dot_general(
        basis_p, grad_t, (((0,), (1,)), ((), ())), preferred_element_type=F32
    )
    moments = both(both(jnp.stack([first_moment.T, second_moment.T]), "core"), "zl")
    turned, moments = lax.optimization_barrier((exchange(left_term.astype(BF16), DP), moments))
    turned = jnp.sum(turned.astype(F32), axis=0).astype(BF16).reshape(n_zh, sub, cols)
    turned = exchange(turned, "zh")
    turned = turned.transpose(1, 0, 2).reshape(1, sub, depth)
    turned = exchange(jnp.broadcast_to(turned, (n_dp, sub, depth)), DP)

    turned, grad_here = lax.optimization_barrier((turned, grad_t))
    grad_all = exchange(jnp.broadcast_to(grad_here[None], (n_dp, cols, rows)), DP)

    rotated = jnp.dot(turned.reshape(block, depth), basis_z, preferred_element_type=F32)
    rotated = rotated + swap(rotated.astype(BF16), "core").astype(F32)
    rotated = rotated + swap(rotated.astype(BF16), "zl").astype(F32)
    new_first = 0.9 * moments[:, :, 0].reshape(block, turns) + 0.1 * rotated
    new_second = 0.95 * moments[:, :, 1].reshape(block, turns) + 0.05 * rotated * rotated
    update = (new_first / 0.19 / (jnp.sqrt(new_second / 0.0975) + 1e-08)).astype(BF16)
    mine = (2 * lax.axis_index("zl") + core) * half
    new_first = lax.dynamic_slice_in_dim(new_first, mine, half, 0)
    new_second = lax.dynamic_slice_in_dim(new_second, mine, half, 0)
    back = lax.dot_general(
        update, basis_z, (((1,), (1,)), ((), ())), preferred_element_type=F32
    ).astype(BF16)
    back, grad_all = lax.optimization_barrier((back, grad_all))
    back = exchange(back.reshape(n_dp, sub, depth), DP)

    gram = lax.dot_general(
        grad_all, grad_t, (((1,), (0,)), ((), ())), preferred_element_type=F32
    ).reshape(n_z, 2, half, rows) / D
    mine = lax.dynamic_index_in_dim(gram, core, 1, keepdims=False)
    other = lax.dynamic_index_in_dim(gram, 1 - core, 1, keepdims=False)
    gram = (mine + swap(other.astype(BF16), "core").astype(F32)).astype(BF16)
    back, gram = lax.optimization_barrier((back, gram))

    back = jnp.sum(back.astype(F32), axis=0).astype(BF16)
    back = exchange(back.reshape(sub, n_zh, cols).transpose(1, 0, 2), "zh")
    back, gram = lax.optimization_barrier((back, gram))
    left_gram = jnp.sum(exchange(gram, Z).astype(F32), axis=0)
    back = lax.all_gather(back.reshape(rows, cols).T, DP, axis=0, tiled=False)
    direction = lax.dot_general(
        basis_p, back, (((1, 2), (0, 2)), ((), ())), preferred_element_type=F32
    )
    return (left_gram.T, new_first.T, new_second.T, direction)


def solution(mesh):
    n_dp, n_col = mesh.shape["dp"], mesh.shape["col"]
    side = int(round(n_dp**0.5))
    fine = Mesh(
        mesh.devices.reshape(side, side, n_col // 4, 2, 2), ("y", "x", "zh", "zl", "core")
    )
    dp, col = ("y", "x"), ("zh", "zl", "core")
    in_specs = (P(dp, None, col), P(dp, None), P(col, dp), P(dp, col), P(dp, col))
    out_specs = (P(dp, col), P(dp, col), P(dp, col), P(dp, col))
    return jax.shard_map(
        on_device, mesh=fine, in_specs=in_specs, out_specs=out_specs, check_vma=False
    )
```

time: 239 us -> 233 us (0.975)
  the two profiles are of different devices: /device:TPU:2 before, /device:TPU:32 now
where the time goes in v4:
time: 233 us; the launch traced here: 232 us
  blocking collectives  87.2 us (37%)
  waiting for transfers between devices  67.7 us (29%)
  starting transfers between devices  34.3 us (15%)
  between operations  14.4 us (6%)
  local copies, waits for them, and re-layouts  10.7 us (5%)
  matrix products  9.46 us (4%)
  other arithmetic  7.84 us (3%)
    all_to_all x3, blocking collectives, exchange(): return lax.all_to_all(chunks, axes, 0, 0, tiled=True)  64.6 us
    ppermute x5, waiting for transfers between devices, swap(): return lax.ppermute(block, axis, [(0, 1), (1, 0)])  43.8 us
    all_to_all x5, starting transfers between devices, exchange(): return lax.all_to_all(chunks, axes, 0, 0, tiled=True)  24.5 us
    all_to_all x5, waiting for transfers between devices, exchange(): return lax.all_to_all(chunks, axes, 0, 0, tiled=True)  23.2 us
    all_gather x1, blocking collectives, on_device(): back = lax.all_gather(back.reshape(rows, cols).T, DP, axis=0, tiled=False)  22.6 us
    ppermute x5, starting transfers between devices, swap(): return lax.ppermute(block, axis, [(0, 1), (1, 0)])  9.74 us
    unnamed x22, local copies, waits for them, and re-layouts  4.78 us
  transfers between devices with their start and end apart: 11, of which 6 were waited for; matrix products, arithmetic and copies ran while one was open for 8% of the time, Pallas kernels for 0%

profile of v4, /device:TPU:32, one launch (start us, length us, event | category | flops | bytes accessed | tf_op | source)
XLA Modules:
  0.0 231.5 jit_solution(7532244509777094562)
XLA Ops:
  7.2 1.4 copy.68
  8.6 1.2 copy.51
  9.7 7.2 %all-to-all-start = ((bf16[16,224,128]{2,1,0:T(8,128)(2,1)}), bf16[16,224,128]{2,1,0:T(8,128)(2,1)S(1)}, u32[]{:S(2)}, u32[]{:S(2)}) async-start(bf16[16,224,128]{2,1,0:T(8,128)(2,1)} %copy.51), calls=%async_computation | async-start | bytes 1835008 | tf_op jit(solution)/shard_map/all_to_all | solution.py:14
  18.5 1.9 collective-permute-start
  20.7 12.2 %all-to-all-done = bf16[16,224,128]{2,1,0:T(8,128)(2,1)S(1)} async-done(((bf16[16,224,128]{2,1,0:T(8,128)(2,1)}), bf16[16,224,128]{2,1,0:T(8,128)(2,1)S(1)}, u32[]{:S(2)}, u32[]{:S(2)}) %all-to-all-start) | async-done | bytes 917536 | tf_op jit(solution)/shard_map/all_to_all | solution.py:14
  33.1 1.3 fusion
  34.4 3.6 %all-to-all-start.1 = ((bf16[16,128,224]{1,2,0:T(8,128)(2,1)}), bf16[16,128,224]{1,2,0:T(8,128)(2,1)S(1)}, u32[]{:S(2)}, u32[]{:S(2)}) async-start(bf16[16,128,224]{1,2,0:T(8,128)(2,1)} %fusion), calls=%async_computation.1 | async-start | bytes 1835008 | tf_op jit(solution)/shard_map/all_to_all | solution.py:14
  38.2 2.0 collective-permute-start.1
  40.2 36.4 %collective-permute-done.1 = f32[2,2,64,448]{3,2,1,0:T(8,128)S(1)} collective-permute-done((f32[2,2,64,448]{3,2,1,0:T(8,128)S(1)}, f32[2,2,64,448]{3,2,1,0:T(8,128)S(1)}, u32[]{:S(2)}, u32[]{:S(2)}) %collective-permute-start.1) | collective-permute-done | bytes 458784 | tf_op jit(solution)/shard_map/ppermute | solution.py:18
  77.4 1.4 maximum_select_fusion
  79.0 28.4 %all_to_all.40 = bf16[8,16,224]{2,1,0:T(8,128)(2,1)S(1)} all-to-all(bf16[8,16,224]{2,1,0:T(8,128)(2,1)S(1)} %bitcast.86), channel_id=1, replica_groups=mesh['y'=4,'x'=4,'zh'=8,'zl'=2,'core'=2] {'zh'}, dimensions={0} | all-to-all | bytes 114688 | tf_op jit(solution)/shard_map/all_to_all | solution.py:14
  107.6 20.5 %all_to_all.41 = bf16[16,16,1792]{2,1,0:T(8,128)(2,1)S(1)} all-to-all(bf16[16,16,1792]{2,1,0:T(8,128)(2,1)S(1)} %broadcast_in_dim.14), channel_id=1, replica_groups=mesh['y'=4,'x'=4,'zh'=8,'zl'=2,'core'=2] {'y','x'}, dimensions={0} | all-to-all | bytes 1835008 | tf_op jit(solution)/shard_map/all_to_all | solution.py:14
  128.1 3.0 %fusion.15 = (bf16[256,448]{0,1:T(8,128)(2,1)}, f32[256,448]{0,1:T(8,128)S(1)}) fusion(bf16[256,1792]{1,0:T(8,128)(2,1)S(1)} %bitcast.75, bf16[1792,448]{1,0:T(8,128)(2,1)} %all-gather.3.cloned.1.call-done), kind=kOutput, calls=%fused_computation.35 | convolution fusion | flops 411156480 | bytes 3211264 | tf_op jit(solution)/shard_map/dot_general | solution.py:62
  131.1 1.9 collective-permute-start.2
  133.0 1.0 broadcast_in_dim.15
  134.1 3.6 %all-to-all-start.4 = ((bf16[16,224,128]{2,1,0:T(8,128)(2,1)}), bf16[16,224,128]{2,1,0:T(8,128)(2,1)S(1)}, u32[]{:S(2)}, u32[]{:S(2)}) async-start(bf16[16,224,128]{2,1,0:T(8,128)(2,1)} %broadcast_in_dim.15), calls=%async_computation.4 | async-start | bytes 1835008 | tf_op jit(solution)/shard_map/all_to_all | solution.py:14
  138.5 1.9 collective-permute-start.3
  141.4 1.2 copy.57
  142.8 5.9 %collective-permute-done.3 = bf16[256,448]{0,1:T(8,128)(2,1)} collective-permute-done((bf16[256,448]{0,1:T(8,128)(2,1)}, bf16[256,448]{0,1:T(8,128)(2,1)}, u32[]{:S(2)}, u32[]{:S(2)}) %collective-permute-start.3) | collective-permute-done | bytes 229408 | tf_op jit(solution)/shard_map/ppermute | solution.py:18
  148.7 2.0 multiply_add_fusion
  151.4 2.8 %convolution_convert_fusion = bf16[256,1792]{1,0:T(8,128)(2,1)} fusion(bf16[1792,448]{1,0:T(8,128)(2,1)S(1)} %copy-done, f32[256,448]{0,1:T(8,128)} %get-tuple-element.47, f32[256,448]{0,1:T(8,128)S(1)} %get-tuple-element.46), kind=kOutput, calls=%fused_computation | convolution fusion | flops 412073984 | bytes 3440640 | tf_op jit(solution)/shard_map/dot_general | solution.py:71
  154.3 1.2 all-to-all-done.4
  156.0 5.7 %all-to-all-start.5 = ((bf16[16,16,1792]{2,1,0:T(8,128)(2,1)}), bf16[16,16,1792]{2,1,0:T(8,128)(2,1)S(1)}, u32[]{:S(2)}, u32[]{:S(2)}) async-start(bf16[16,16,1792]{2,1,0:T(8,128)(2,1)} %bitcast.82), calls=%async_computation.5 | async-start | bytes 1835008 | tf_op jit(solution)/shard_map/all_to_all | solution.py:14
  161.7 1.2 convolution_multiply_fusion
  163.0 2.1 collective-permute-start.4
  165.1 1.5 collective-permute-done.4
  167.3 9.8 %all-to-all-done.5 = bf16[16,16,1792]{2,1,0:T(8,128)(2,1)S(1)} async-done(((bf16[16,16,1792]{2,1,0:T(8,128)(2,1)}), bf16[16,16,1792]{2,1,0:T(8,128)(2,1)S(1)}, u32[]{:S(2)}, u32[]{:S(2)}) %all-to-all-start.5) | async-done | bytes 917536 | tf_op jit(solution)/shard_map/all_to_all | solution.py:14
  177.4 15.7 %all_to_all.42 = bf16[8,16,224]{2,1,0:T(8,128)(2,1)S(1)} all-to-all(bf16[8,16,224]{2,1,0:T(8,128)(2,1)S(1)} %copy.60), channel_id=1, replica_groups=mesh['y'=4,'x'=4,'zh'=8,'zl'=2,'core'=2] {'zh'}, dimensions={0} | all-to-all | bytes 114688 | tf_op jit(solution)/shard_map/all_to_all | solution.py:14
  193.2 4.4 %all-to-all-start.7 = ((bf16[16,64,128]{2,1,0:T(8,128)(2,1)}), bf16[16,64,128]{2,1,0:T(8,128)(2,1)S(1)}, u32[]{:S(2)}, u32[]{:S(2)}) async-start(bf16[16,64,128]{2,1,0:T(8,128)(2,1)} %fusion.1), calls=%async_computation.7 | async-start | bytes 524288 | tf_op jit(solution)/shard_map/all_to_all | solution.py:14
  197.6 1.1 dynamic-slice_bitcast_fusion
  200.4 22.6 %all-gather = bf16[3584,128]{1,0:T(8,128)(2,1)S(1)} all-gather(bf16[224,128]{1,0:T(8,128)(2,1)S(1)} %copy.61), channel_id=2, replica_groups=mesh['y'=4,'x'=4,'zh'=8,'zl'=2,'core'=2] {'y','x'}, dimensions={0}, use_global_device_ids=true | all-gather | bytes 974848 | tf_op jit(solution)/shard_map/all_gather | solution.py:89
  223.0 1.1 convolution_bitcast_fusion
  (49 shorter events, 10.0 us)
Async XLA Ops:
  8.5 9.1 %copy-start.7 = (f32[448,64]{0,1:T(8,128)S(1)}, f32[448,64]{0,1:T(8,128)}, u32[]{:S(2)}) copy-start(f32[448,64]{0,1:T(8,128)} %param.9) | copy-start | bytes 344068
  8.5 9.1 %copy-start.8 = (f32[448,64]{0,1:T(8,128)S(1)}, f32[448,64]{0,1:T(8,128)}, u32[]{:S(2)}) copy-start(f32[448,64]{0,1:T(8,128)} %param.8) | copy-start | bytes 344068
  9.7 10.7 %copy-start.6 = (bf16[128,2048]{1,0:T(8,128)(2,1)S(1)}, bf16[128,2048]{1,0:T(8,128)(2,1)}, u32[]{:S(2)}) copy-start(bf16[128,2048]{1,0:T(8,128)(2,1)} %param.6) | copy-start | bytes 1572868
  9.7 23.2 %all-to-all-start = ((bf16[16,224,128]{2,1,0:T(8,128)(2,1)}), bf16[16,224,128]{2,1,0:T(8,128)(2,1)S(1)}, u32[]{:S(2)}, u32[]{:S(2)}) async-start(bf16[16,224,128]{2,1,0:T(8,128)(2,1)} %copy.51), calls=%async_computation | async-start | bytes 1835008 | tf_op jit(solution)/shard_map/all_to_all | solution.py:14
  16.9 111.2 %all-gather.3.cloned.1.call-start = ((), (), s32[]{:S(2)}) async-start(), calls=%async_computation.8 | async-start | bytes 2064384 | tf_op jit(solution)/shard_map/all_gather | solution.py:41
  18.5 19.6 %collective-permute-start = (f32[2,64,448]{2,1,0:T(8,128)}, f32[2,64,448]{2,1,0:T(8,128)S(1)}, u32[]{:S(2)}, u32[]{:S(2)}) collective-permute-start(f32[2,64,448]{2,1,0:T(8,128)} %get-tuple-element.50), channel_id=1, source_target_pairs={{0,1},{1,0},{2,3},{3,2},{4,5},{5,4},{6,7},{7,6},{8,9},{9,8},{10,11... | collective-permute-start | bytes 688136 | tf_op jit(solution)/shard_map/ppermute | solution.py:18
  33.1 99.9 %copy-start.4 = (bf16[224,128]{1,0:T(8,128)(2,1)}, bf16[224,128]{1,0:T(8,128)(2,1)S(1)}, u32[]{:S(2)}) copy-start(bf16[224,128]{1,0:T(8,128)(2,1)S(1)} %reduce_sum.45) | copy-start | bytes 172036
  34.4 44.3 %all-to-all-start.1 = ((bf16[16,128,224]{1,2,0:T(8,128)(2,1)}), bf16[16,128,224]{1,2,0:T(8,128)(2,1)S(1)}, u32[]{:S(2)}, u32[]{:S(2)}) async-start(bf16[16,128,224]{1,2,0:T(8,128)(2,1)} %fusion), calls=%async_computation.1 | async-start | bytes 1835008 | tf_op jit(solution)/shard_map/all_to_all | solution.py:14
  38.2 38.4 %collective-permute-start.1 = (f32[2,2,64,448]{3,2,1,0:T(8,128)S(1)}, f32[2,2,64,448]{3,2,1,0:T(8,128)S(1)}, u32[]{:S(2)}, u32[]{:S(2)}) collective-permute-start(f32[2,2,64,448]{3,2,1,0:T(8,128)S(1)} %maximum_select_fusion.2), channel_id=1, source_target_pairs={{0,2},{2,0},{1,3},{3,1},{4,6},{6,4},{5,7},{7,5},{8,10},{10,8},{9,1... | collective-permute-start | bytes 1376264 | tf_op jit(solution)/shard_map/ppermute | solution.py:18
  76.5 0.8 copy-start.5
  131.1 6.6 %collective-permute-start.2 = (bf16[256,448]{0,1:T(8,128)(2,1)}, bf16[256,448]{0,1:T(8,128)(2,1)S(1)}, u32[]{:S(2)}, u32[]{:S(2)}) collective-permute-start(bf16[256,448]{0,1:T(8,128)(2,1)} %get-tuple-element.51), channel_id=1, source_target_pairs={{0,1},{1,0},{2,3},{3,2},{4,5},{5,4},{6,7},{7,6},{8,9},{9,8},{10,11... | collective-permute-start | bytes 688136 | tf_op jit(solution)/shard_map/ppermute | solution.py:18
  134.1 21.4 %all-to-all-start.4 = ((bf16[16,224,128]{2,1,0:T(8,128)(2,1)}), bf16[16,224,128]{2,1,0:T(8,128)(2,1)S(1)}, u32[]{:S(2)}, u32[]{:S(2)}) async-start(bf16[16,224,128]{2,1,0:T(8,128)(2,1)} %broadcast_in_dim.15), calls=%async_computation.4 | async-start | bytes 1835008 | tf_op jit(solution)/shard_map/all_to_all | solution.py:14
  137.7 0.8 copy-start.3
  138.5 10.2 %collective-permute-start.3 = (bf16[256,448]{0,1:T(8,128)(2,1)}, bf16[256,448]{0,1:T(8,128)(2,1)}, u32[]{:S(2)}, u32[]{:S(2)}) collective-permute-start(bf16[256,448]{0,1:T(8,128)(2,1)} %fusion.3), channel_id=1, source_target_pairs={{0,2},{2,0},{1,3},{3,1},{4,6},{6,4},{5,7},{7,5},{8,10},{10,8},{9,1... | collective-permute-start | bytes 688136 | tf_op jit(solution)/shard_map/ppermute | solution.py:18
  142.8 8.6 %copy-start = (bf16[1792,448]{1,0:T(8,128)(2,1)S(1)}, bf16[1792,448]{1,0:T(8,128)(2,1)}, u32[]{:S(2)}) copy-start(bf16[1792,448]{1,0:T(8,128)(2,1)} %all-gather.3.cloned.1.call-done) | copy-start | bytes 4816900
  150.7 0.8 copy-start.1
  156.0 21.2 %all-to-all-start.5 = ((bf16[16,16,1792]{2,1,0:T(8,128)(2,1)}), bf16[16,16,1792]{2,1,0:T(8,128)(2,1)S(1)}, u32[]{:S(2)}, u32[]{:S(2)}) async-start(bf16[16,16,1792]{2,1,0:T(8,128)(2,1)} %bitcast.82), calls=%async_computation.5 | async-start | bytes 1835008 | tf_op jit(solution)/shard_map/all_to_all | solution.py:14
  162.9 34.7 %copy-start.2 = (f32[256,448]{0,1:T(8,128)S(1)}, f32[256,448]{0,1:T(8,128)}, u32[]{:S(2)}) copy-start(f32[256,448]{0,1:T(8,128)} %copy-done.1) | copy-start | bytes 1376260
  163.0 3.6 %collective-permute-start.4 = (bf16[16,64,128]{2,1,0:T(8,128)(2,1)S(1)}, bf16[16,64,128]{2,1,0:T(8,128)(2,1)S(1)}, u32[]{:S(2)}, u32[]{:S(2)}) collective-permute-start(bf16[16,64,128]{2,1,0:T(8,128)(2,1)S(1)} %fusion.4), channel_id=1, source_target_pairs={{0,1},{1,0},{2,3},{3,2},{4,5},{5,4},{6,7},{7,6},{8,9},{9,8},{10,11... | collective-permute-start | bytes 786440 | tf_op jit(solution)/shard_map/ppermute | solution.py:18
  193.2 30.8 %all-to-all-start.7 = ((bf16[16,64,128]{2,1,0:T(8,128)(2,1)}), bf16[16,64,128]{2,1,0:T(8,128)(2,1)S(1)}, u32[]{:S(2)}, u32[]{:S(2)}) async-start(bf16[16,64,128]{2,1,0:T(8,128)(2,1)} %fusion.1), calls=%async_computation.7 | async-start | bytes 524288 | tf_op jit(solution)/shard_map/all_to_all | solution.py:14
Sparse Core Ops, SparseCore 0:
  19.8 71.3 all-gather.2

commit v5 on v3

--- a/solution.py
+++ b/solution.py
@@ -63,20 +63,12 @@
     )
     turned = jnp.sum(turned.astype(F32), axis=0).astype(BF16).reshape(n_z, sub, cols)
 
-    turned, grad_here = lax.optimization_barrier((turned, grad_t))
-    turned, grad_all = lax.optimization_barrier(
-        (exchange(turned, "z"), lax.all_gather(grad_here, DP, axis=0, tiled=False))
-    )
+    turned = exchange(turned, "z")
     turned = turned.transpose(1, 0, 2).reshape(1, sub, n_z * cols)
     turned = exchange(jnp.broadcast_to(turned, (n_dp, sub, n_z * cols)), DP)
 
-    gram = lax.dot_general(
-        grad_all, grad_t, (((1,), (0,)), ((), ())), preferred_element_type=F32
-    ).reshape(n_z, 2, half, rows) / D
-    mine = lax.dynamic_index_in_dim(gram, core, 1, keepdims=False)
-    other = lax.dynamic_index_in_dim(gram, 1 - core, 1, keepdims=False)
-    gram = (mine + swap_cores(other.astype(BF16)).astype(F32)).astype(BF16)
-    turned, gram = lax.optimization_barrier((turned, gram))
+    turned, grad_here = lax.optimization_barrier((turned, grad_t))
+    grad_all = exchange(jnp.broadcast_to(grad_here[None], (n_dp, cols, rows)), DP)
 
     basis_z = basis_z.reshape(n_z * cols, turns)
     rotated = jnp.dot(
@@ -92,7 +84,17 @@
     back = lax.dot_general(
         update, basis_z, (((1,), (1,)), ((), ())), preferred_element_type=F32
     ).astype(BF16)
+    back, grad_all = lax.optimization_barrier((back, grad_all))
     back = exchange(back.reshape(n_dp, sub, n_z * cols), DP)
+
+    gram = lax.dot_general(
+        grad_all, grad_t, (((1,), (0,)), ((), ())), preferred_element_type=F32
+    ).reshape(n_z, 2, half, rows) / D
+    mine = lax.dynamic_index_in_dim(gram, core, 1, keepdims=False)
+    other = lax.dynamic_index_in_dim(gram, 1 - core, 1, keepdims=False)
+    gram = (mine + swap_cores(other.astype(BF16)).astype(F32)).astype(BF16)
+    back, gram = lax.optimization_barrier((back, gram))
+
     back = jnp.sum(back.astype(F32), axis=0).astype(BF16)
     back = back.reshape(sub, n_z, cols).transpose(1, 0, 2)
     packed = exchange(jnp.concatenate([to_tiles(back), gram], axis=1), "z")

time: 200 us -> 192 us (0.960)
  blocking collectives: 74 us -> 51.5 us
  waiting for transfers between devices: 48.4 us -> 68.1 us
  starting transfers between devices: 40.2 us -> 34.4 us
    all_gather x1 -> x0, blocking collectives: 22.4 us -> none  [on_device(): lax.all_gather(grad_here, DP, axis=0, tiled=False)]
    all_to_all x5 -> x6, waiting for transfers between devices: 43.7 us -> 63.5 us  [exchange(): return lax.all_to_all(chunks, axes, 0, 0, tiled=True)]
    all_to_all x5 -> x6, starting transfers between devices: 34.3 us -> 28.5 us  [exchange(): return lax.all_to_all(chunks, axes, 0, 0, tiled=True)]
    unnamed x17 -> x21, local copies, waits for them, and re-layouts: 3.23 us -> 4.01 us
  transfers between devices with their start and end apart: 9 -> 10, of which waited for: 7 -> 9; matrix products, arithmetic and copies ran while one was open for 6% -> 10% of each run, Pallas kernels for 0% -> 0%
where the time goes in v5:
time: 192 us; the launch traced here: 191 us
  waiting for transfers between devices  68.1 us (35%)
  blocking collectives  51.5 us (27%)
  starting transfers between devices  34.4 us (18%)
  between operations  14.4 us (8%)
  matrix products  11.5 us (6%)
  local copies, waits for them, and re-layouts  9.82 us (5%)
    all_to_all x6, waiting for transfers between devices, exchange(): return lax.all_to_all(chunks, axes, 0, 0, tiled=True)  63.5 us
    all_to_all x2, blocking collectives, exchange(): return lax.all_to_all(chunks, axes, 0, 0, tiled=True)  51.5 us
    all_to_all x6, starting transfers between devices, exchange(): return lax.all_to_all(chunks, axes, 0, 0, tiled=True)  28.5 us
    ppermute x3, starting transfers between devices, swap_cores(): return lax.ppermute(block, 'core', [(0, 1), (1, 0)])  5.89 us
    dot_general x1, matrix products, on_device(): lax.dot_general(update, basis_z, (((1,), (1,)), ((), ())), preferred_elem...  4.38 us
    unnamed x21, local copies, waits for them, and re-layouts  4.01 us
    ppermute x3, waiting for transfers between devices, swap_cores(): return lax.ppermute(block, 'core', [(0, 1), (1, 0)])  3.96 us
  transfers between devices with their start and end apart: 10, of which 9 were waited for; matrix products, arithmetic and copies ran while one was open for 10% of the time, Pallas kernels for 0%

profile of v5, /device:TPU:32, one launch (start us, length us, event | category | flops | bytes accessed | tf_op | source)
XLA Modules:
  0.0 191.1 jit_solution(1033800356456207094)
XLA Ops:
  7.9 1.4 copy.68
  9.3 1.2 copy.50
  10.5 7.2 %all-to-all-start = ((bf16[16,224,128]{2,1,0:T(8,128)(2,1)}), bf16[16,224,128]{2,1,0:T(8,128)(2,1)S(1)}, u32[]{:S(2)}, u32[]{:S(2)}) async-start(bf16[16,224,128]{2,1,0:T(8,128)(2,1)} %copy.50), calls=%async_computation | async-start | bytes 1835008 | tf_op jit(solution)/shard_map/all_to_all | solution.py:14
  17.9 15.8 %all-to-all-done = bf16[16,224,128]{2,1,0:T(8,128)(2,1)S(1)} async-done(((bf16[16,224,128]{2,1,0:T(8,128)(2,1)}), bf16[16,224,128]{2,1,0:T(8,128)(2,1)S(1)}, u32[]{:S(2)}, u32[]{:S(2)}) %all-to-all-start) | async-done | bytes 917536 | tf_op jit(solution)/shard_map/all_to_all | solution.py:14
  33.8 1.3 fusion
  35.2 3.6 %all-to-all-start.1 = ((bf16[16,128,224]{1,2,0:T(8,128)(2,1)}), bf16[16,128,224]{1,2,0:T(8,128)(2,1)S(1)}, u32[]{:S(2)}, u32[]{:S(2)}) async-start(bf16[16,128,224]{1,2,0:T(8,128)(2,1)} %fusion), calls=%async_computation.1 | async-start | bytes 1835008 | tf_op jit(solution)/shard_map/all_to_all | solution.py:14
  38.9 1.9 %collective-permute-start = (f32[2,64,448]{2,1,0:T(8,128)S(1)}, f32[2,64,448]{2,1,0:T(8,128)S(1)}, u32[]{:S(2)}, u32[]{:S(2)}) collective-permute-start(f32[2,64,448]{2,1,0:T(8,128)S(1)} %get-tuple-element.45), channel_id=1, source_target_pairs={{0,1},{1,0},{2,3},{3,2},{4,5},{5,4},{6,7},{7,6},{8,9},{9,8},{10,11... | collective-permute-start | bytes 688136 | tf_op jit(solution)/shard_map/ppermute | solution.py:18
  40.8 1.5 collective-permute-done
  42.4 11.3 %all-to-all-done.1 = bf16[16,128,224]{1,2,0:T(8,128)(2,1)S(1)} async-done(((bf16[16,128,224]{1,2,0:T(8,128)(2,1)}), bf16[16,128,224]{1,2,0:T(8,128)(2,1)S(1)}, u32[]{:S(2)}, u32[]{:S(2)}) %all-to-all-start.1) | async-done | bytes 917536 | tf_op jit(solution)/shard_map/all_to_all | solution.py:14
  53.9 27.3 %all_to_all.40 = bf16[16,8,224]{2,1,0:T(8,128)(2,1)S(1)} all-to-all(bf16[16,8,224]{2,1,0:T(8,128)(2,1)S(1)} %bitcast.91), channel_id=1, replica_groups=mesh['y'=4,'x'=4,'z'=16,'core'=2] {'z'}, dimensions={0} | all-to-all | bytes 114688 | tf_op jit(solution)/shard_map/all_to_all | solution.py:14
  81.3 1.0 broadcast_in_dim.9
  82.3 3.6 %all-to-all-start.3 = ((bf16[16,8,3584]{2,1,0:T(8,128)(2,1)}), bf16[16,8,3584]{2,1,0:T(8,128)(2,1)S(1)}, u32[]{:S(2)}, u32[]{:S(2)}) async-start(bf16[16,8,3584]{2,1,0:T(8,128)(2,1)} %broadcast_in_dim.9), calls=%async_computation.3 | async-start | bytes 1835008 | tf_op jit(solution)/shard_map/all_to_all | solution.py:14
  86.0 12.2 %all-to-all-done.3 = bf16[16,8,3584]{2,1,0:T(8,128)(2,1)S(1)} async-done(((bf16[16,8,3584]{2,1,0:T(8,128)(2,1)}), bf16[16,8,3584]{2,1,0:T(8,128)(2,1)S(1)}, u32[]{:S(2)}, u32[]{:S(2)}) %all-to-all-start.3) | async-done | bytes 917536 | tf_op jit(solution)/shard_map/all_to_all | solution.py:14
  98.2 1.1 broadcast_in_dim.10
  99.2 3.6 %all-to-all-start.4 = ((bf16[16,224,128]{2,1,0:T(8,128)(2,1)}), bf16[16,224,128]{2,1,0:T(8,128)(2,1)S(1)}, u32[]{:S(2)}, u32[]{:S(2)}) async-start(bf16[16,224,128]{2,1,0:T(8,128)(2,1)} %broadcast_in_dim.10), calls=%async_computation.4 | async-start | bytes 1835008 | tf_op jit(solution)/shard_map/all_to_all | solution.py:14
  102.9 3.5 %fusion.19 = (bf16[128,448]{0,1:T(8,128)(2,1)S(1)}, f32[128,448]{0,1:T(8,128)S(1)}) fusion(bf16[3584,448]{1,0:T(8,128)(2,1)} %all-gather.3.cloned.1.call-done, bf16[16,8,3584]{2,1,0:T(8,128)(2,1)S(1)} %all-to-all-done.3), kind=kOutput, calls=%fused_computation.40 | convolution fusion | flops 411099136 | bytes 4472832 | tf_op jit(solution)/shard_map/dot_general | solution.py:74
  106.4 1.9 %collective-permute-start.1 = (bf16[128,448]{0,1:T(8,128)(2,1)S(1)}, bf16[128,448]{0,1:T(8,128)(2,1)S(1)}, u32[]{:S(2)}, u32[]{:S(2)}) collective-permute-start(bf16[128,448]{0,1:T(8,128)(2,1)S(1)} %get-tuple-element.46), channel_id=1, source_target_pairs={{0,1},{1,0},{2,3},{3,2},{4,5},{5,4},{6,7},{7,6},{8,9},{9,8},{10,11... | collective-permute-start | bytes 344072 | tf_op jit(solution)/shard_map/ppermute | solution.py:18
  108.7 1.0 collective-permute-done.1
  109.7 0.7 copy-done
  110.5 4.4 %convolution_convert_fusion = bf16[128,3584]{1,0:T(8,128)(2,1)} fusion(bf16[3584,448]{1,0:T(8,128)(2,1)} %all-gather.3.cloned.1.call-done, f32[128,448]{0,1:T(8,128)S(1)} %get-tuple-element.43, f32[128,448]{0,1:T(8,128)S(1)} %get-tuple-element.42), kind=kOutput, calls=%fused_computation | convolution fusion | flops 411787264 | bytes 4587520 | tf_op jit(solution)/shard_map/dot_general | solution.py:84
  115.8 6.8 %all-to-all-start.5 = ((bf16[16,8,3584]{2,1,0:T(8,128)(2,1)}), bf16[16,8,3584]{2,1,0:T(8,128)(2,1)S(1)}, u32[]{:S(2)}, u32[]{:S(2)}) async-start(bf16[16,8,3584]{2,1,0:T(8,128)(2,1)} %bitcast.19), calls=%async_computation.5 | async-start | bytes 1835008 | tf_op jit(solution)/shard_map/all_to_all | solution.py:14
  122.6 1.2 convolution_multiply_fusion
  123.9 2.1 %collective-permute-start.2 = (bf16[16,64,128]{2,1,0:T(8,128)(2,1)S(1)}, bf16[16,64,128]{2,1,0:T(8,128)(2,1)S(1)}, u32[]{:S(2)}, u32[]{:S(2)}) collective-permute-start(bf16[16,64,128]{2,1,0:T(8,128)(2,1)S(1)} %fusion.8), channel_id=1, source_target_pairs={{0,1},{1,0},{2,3},{3,2},{4,5},{5,4},{6,7},{7,6},{8,9},{9,8},{10,11... | collective-permute-start | bytes 786440 | tf_op jit(solution)/shard_map/ppermute | solution.py:18
  126.0 1.5 collective-permute-done.2
  127.5 11.2 %all-to-all-done.5 = bf16[16,8,3584]{2,1,0:T(8,128)(2,1)S(1)} async-done(((bf16[16,8,3584]{2,1,0:T(8,128)(2,1)}), bf16[16,8,3584]{2,1,0:T(8,128)(2,1)S(1)}, u32[]{:S(2)}, u32[]{:S(2)}) %all-to-all-start.5) | async-done | bytes 917536 | tf_op jit(solution)/shard_map/all_to_all | solution.py:14
  139.1 24.3 %all_to_all.41 = bf16[16,80,128]{2,1,0:T(8,128)(2,1)S(1)} all-to-all(bf16[16,80,128]{2,1,0:T(8,128)(2,1)S(1)} %pad_maximum_fusion), channel_id=1, replica_groups=mesh['y'=4,'x'=4,'z'=16,'core'=2] {'z'}, dimensions={0} | all-to-all | bytes 655360 | tf_op jit(solution)/shard_map/all_to_all | solution.py:14
  163.5 1.1 broadcast_in_dim.22
  164.6 3.6 %all-to-all-start.7 = ((bf16[16,224,128]{2,1,0:T(8,128)(2,1)}), bf16[16,224,128]{2,1,0:T(8,128)(2,1)S(1)}, u32[]{:S(2)}, u32[]{:S(2)}) async-start(bf16[16,224,128]{2,1,0:T(8,128)(2,1)} %broadcast_in_dim.22), calls=%async_computation.7 | async-start | bytes 1835008 | tf_op jit(solution)/shard_map/all_to_all | solution.py:14
  168.5 0.8 copy.62
  169.2 0.8 copy.63
  170.7 12.6 %all-to-all-done.7 = bf16[16,224,128]{2,1,0:T(8,128)(2,1)S(1)} async-done(((bf16[16,224,128]{2,1,0:T(8,128)(2,1)}), bf16[16,224,128]{2,1,0:T(8,128)(2,1)S(1)}, u32[]{:S(2)}, u32[]{:S(2)}) %all-to-all-start.7) | async-done | bytes 917536 | tf_op jit(solution)/shard_map/all_to_all | solution.py:14
  183.2 1.0 convolution_bitcast_fusion
  (44 shorter events, 4.4 us)
Async XLA Ops:
  7.2 10.5 %copy-start.5 = (bf16[128,2048]{1,0:T(8,128)(2,1)S(1)}, bf16[128,2048]{1,0:T(8,128)(2,1)}, u32[]{:S(2)}) copy-start(bf16[128,2048]{1,0:T(8,128)(2,1)} %param.6) | copy-start | bytes 1572868
  7.2 95.7 %all-gather.3.cloned.1.call-start = ((), (), s32[]{:S(2)}) async-start(), calls=%async_computation.8 | async-start | bytes 3899392 | tf_op jit(solution)/shard_map/all_gather | solution.py:47
  10.5 28.4 %copy-start.6 = (f32[448,64]{0,1:T(8,128)S(1)}, f32[448,64]{0,1:T(8,128)}, u32[]{:S(2)}) copy-start(f32[448,64]{0,1:T(8,128)} %param.9) | copy-start | bytes 344068
  10.5 28.4 %copy-start.7 = (f32[448,64]{0,1:T(8,128)S(1)}, f32[448,64]{0,1:T(8,128)}, u32[]{:S(2)}) copy-start(f32[448,64]{0,1:T(8,128)} %param.8) | copy-start | bytes 344068
  10.5 23.2 %all-to-all-start = ((bf16[16,224,128]{2,1,0:T(8,128)(2,1)}), bf16[16,224,128]{2,1,0:T(8,128)(2,1)S(1)}, u32[]{:S(2)}, u32[]{:S(2)}) async-start(bf16[16,224,128]{2,1,0:T(8,128)(2,1)} %copy.50), calls=%async_computation | async-start | bytes 1835008 | tf_op jit(solution)/shard_map/all_to_all | solution.py:14
  33.8 69.0 %copy-start.4 = (bf16[224,128]{1,0:T(8,128)(2,1)}, bf16[224,128]{1,0:T(8,128)(2,1)S(1)}, u32[]{:S(2)}) copy-start(bf16[224,128]{1,0:T(8,128)(2,1)S(1)} %reduce_sum.45) | copy-start | bytes 172036
  35.2 18.5 %all-to-all-start.1 = ((bf16[16,128,224]{1,2,0:T(8,128)(2,1)}), bf16[16,128,224]{1,2,0:T(8,128)(2,1)S(1)}, u32[]{:S(2)}, u32[]{:S(2)}) async-start(bf16[16,128,224]{1,2,0:T(8,128)(2,1)} %fusion), calls=%async_computation.1 | async-start | bytes 1835008 | tf_op jit(solution)/shard_map/all_to_all | solution.py:14
  38.9 3.4 %collective-permute-start = (f32[2,64,448]{2,1,0:T(8,128)S(1)}, f32[2,64,448]{2,1,0:T(8,128)S(1)}, u32[]{:S(2)}, u32[]{:S(2)}) collective-permute-start(f32[2,64,448]{2,1,0:T(8,128)S(1)} %get-tuple-element.45), channel_id=1, source_target_pairs={{0,1},{1,0},{2,3},{3,2},{4,5},{5,4},{6,7},{7,6},{8,9},{9,8},{10,11... | collective-permute-start | bytes 688136 | tf_op jit(solution)/shard_map/ppermute | solution.py:18
  82.3 15.8 %all-to-all-start.3 = ((bf16[16,8,3584]{2,1,0:T(8,128)(2,1)}), bf16[16,8,3584]{2,1,0:T(8,128)(2,1)S(1)}, u32[]{:S(2)}, u32[]{:S(2)}) async-start(bf16[16,8,3584]{2,1,0:T(8,128)(2,1)} %broadcast_in_dim.9), calls=%async_computation.3 | async-start | bytes 1835008 | tf_op jit(solution)/shard_map/all_to_all | solution.py:14
  99.2 16.1 %all-to-all-start.4 = ((bf16[16,224,128]{2,1,0:T(8,128)(2,1)}), bf16[16,224,128]{2,1,0:T(8,128)(2,1)S(1)}, u32[]{:S(2)}, u32[]{:S(2)}) async-start(bf16[16,224,128]{2,1,0:T(8,128)(2,1)} %broadcast_in_dim.10), calls=%async_computation.4 | async-start | bytes 1835008 | tf_op jit(solution)/shard_map/all_to_all | solution.py:14
  106.4 3.2 %collective-permute-start.1 = (bf16[128,448]{0,1:T(8,128)(2,1)S(1)}, bf16[128,448]{0,1:T(8,128)(2,1)S(1)}, u32[]{:S(2)}, u32[]{:S(2)}) collective-permute-start(bf16[128,448]{0,1:T(8,128)(2,1)S(1)} %get-tuple-element.46), channel_id=1, source_target_pairs={{0,1},{1,0},{2,3},{3,2},{4,5},{5,4},{6,7},{7,6},{8,9},{9,8},{10,11... | collective-permute-start | bytes 344072 | tf_op jit(solution)/shard_map/ppermute | solution.py:18
  109.7 0.7 copy-start
  109.7 0.8 copy-start.2
  115.8 23.0 %all-to-all-start.5 = ((bf16[16,8,3584]{2,1,0:T(8,128)(2,1)}), bf16[16,8,3584]{2,1,0:T(8,128)(2,1)S(1)}, u32[]{:S(2)}, u32[]{:S(2)}) async-start(bf16[16,8,3584]{2,1,0:T(8,128)(2,1)} %bitcast.19), calls=%async_computation.5 | async-start | bytes 1835008 | tf_op jit(solution)/shard_map/all_to_all | solution.py:14
  123.8 44.4 %copy-start.1 = (f32[128,448]{0,1:T(8,128)S(1)}, f32[128,448]{0,1:T(8,128)}, u32[]{:S(2)}) copy-start(f32[128,448]{0,1:T(8,128)} %copy-done) | copy-start | bytes 688132
  123.8 44.4 %copy-start.3 = (f32[128,448]{0,1:T(8,128)S(1)}, f32[128,448]{0,1:T(8,128)}, u32[]{:S(2)}) copy-start(f32[128,448]{0,1:T(8,128)} %copy-done.2) | copy-start | bytes 688132
  123.9 3.6 %collective-permute-start.2 = (bf16[16,64,128]{2,1,0:T(8,128)(2,1)S(1)}, bf16[16,64,128]{2,1,0:T(8,128)(2,1)S(1)}, u32[]{:S(2)}, u32[]{:S(2)}) collective-permute-start(bf16[16,64,128]{2,1,0:T(8,128)(2,1)S(1)} %fusion.8), channel_id=1, source_target_pairs={{0,1},{1,0},{2,3},{3,2},{4,5},{5,4},{6,7},{7,6},{8,9},{9,8},{10,11... | collective-permute-start | bytes 786440 | tf_op jit(solution)/shard_map/ppermute | solution.py:18
  164.6 18.6 %all-to-all-start.7 = ((bf16[16,224,128]{2,1,0:T(8,128)(2,1)}), bf16[16,224,128]{2,1,0:T(8,128)(2,1)S(1)}, u32[]{:S(2)}, u32[]{:S(2)}) async-start(bf16[16,224,128]{2,1,0:T(8,128)(2,1)} %broadcast_in_dim.22), calls=%async_computation.7 | async-start | bytes 1835008 | tf_op jit(solution)/shard_map/all_to_all | solution.py:14
Sparse Core Ops, SparseCore 0:
  10.1 82.5 all-gather.2

commit v6 on v3

--- a/solution.py
+++ b/solution.py
@@ -47,7 +47,10 @@
     basis_z = lax.all_gather(right_basis, "z", axis=0, tiled=False)
 
     parts = grad_parts[0].T.reshape(cols, n_dp, rows).transpose(1, 0, 2)
-    grad_t = jnp.sum(exchange(parts, DP).astype(F32), axis=0).astype(BF16)
+    parts, moments = lax.optimization_barrier(
+        (exchange(parts, DP), both(jnp.stack([first_moment.T, second_moment.T])))
+    )
+    grad_t = jnp.sum(parts.astype(F32), axis=0).astype(BF16)
 
     basis_p = (
         left_basis.reshape(rows, n_z, n_dp, sub).transpose(0, 2, 1, 3).reshape(rows, n_dp, rows)
@@ -55,17 +58,13 @@
     left_term = lax.dot_general(
         basis_p, grad_t, (((0,), (1,)), ((), ())), preferred_element_type=F32
     )
-    turned, moments = lax.optimization_barrier(
-        (
-            exchange(left_term.astype(BF16), DP),
-            both(jnp.stack([first_moment.T, second_moment.T])),
-        )
+    turned, grad_x = lax.optimization_barrier(
+        (exchange(left_term.astype(BF16), DP), lax.all_gather(grad_t, "x", axis=0, tiled=False))
     )
     turned = jnp.sum(turned.astype(F32), axis=0).astype(BF16).reshape(n_z, sub, cols)
-
-    turned, grad_here = lax.optimization_barrier((turned, grad_t))
+    turned, grad_x = lax.optimization_barrier((turned, grad_x))
     turned, grad_all = lax.optimization_barrier(
-        (exchange(turned, "z"), lax.all_gather(grad_here, DP, axis=0, tiled=False))
+        (exchange(turned, "z"), lax.all_gather(grad_x, "y", axis=0, tiled=True))
     )
     turned = turned.transpose(1, 0, 2).reshape(1, sub, n_z * cols)
     turned = exchange(jnp.broadcast_to(turned, (n_dp, sub, n_z * cols)), DP)

time: 200 us -> 196 us (0.980)
  waiting for transfers between devices: 48.4 us -> 33.7 us
  blocking collectives: 74 us -> 85.6 us
    all_to_all x5, waiting for transfers between devices: 43.7 us -> 29.4 us  [exchange(): return lax.all_to_all(chunks, axes, 0, 0, tiled=True)]
    all_gather x1 -> x2, blocking collectives: 22.4 us -> 34.3 us  [the longest x1 19.5 us: on_device(): lax.all_gather(grad_t, 'x', axis=0, tiled=False)]
  transfers between devices with their start and end apart: 9 -> 9, of which waited for: 7 -> 6; matrix products, arithmetic and copies ran while one was open for 6% -> 6% of each run, Pallas kernels for 0% -> 0%
where the time goes in v6:
time: 196 us; the launch traced here: 195 us
  blocking collectives  85.6 us (44%)
  starting transfers between devices  39.5 us (20%)
  waiting for transfers between devices  33.7 us (17%)
  between operations  14.3 us (7%)
  matrix products  10.6 us (5%)
  local copies, waits for them, and re-layouts  8.62 us (4%)
  other arithmetic  2.85 us (1%)
    all_to_all x2, blocking collectives, exchange(): return lax.all_to_all(chunks, axes, 0, 0, tiled=True)  51.3 us
    all_to_all x5, starting transfers between devices, exchange(): return lax.all_to_all(chunks, axes, 0, 0, tiled=True)  33.6 us
    all_to_all x5, waiting for transfers between devices, exchange(): return lax.all_to_all(chunks, axes, 0, 0, tiled=True)  29.4 us
    all_gather x1, blocking collectives, on_device(): lax.all_gather(grad_t, 'x', axis=0, tiled=False)  19.5 us
    all_gather x1, blocking collectives, on_device(): lax.all_gather(grad_x, 'y', axis=0, tiled=True)  14.8 us
    ppermute x3, starting transfers between devices, swap_cores(): return lax.ppermute(block, 'core', [(0, 1), (1, 0)])  5.89 us
  transfers between devices with their start and end apart: 9, of which 6 were waited for; matrix products, arithmetic and copies ran while one was open for 6% of the time, Pallas kernels for 0%

profile of v6, /device:TPU:32, one launch (start us, length us, event | category | flops | bytes accessed | tf_op | source)
XLA Modules:
  0.0 195.2 jit_solution(8594364874303882474)
XLA Ops:
  7.9 1.4 copy.68
  9.3 1.2 copy.50
  10.5 7.0 %all-to-all-start = ((bf16[16,224,128]{2,1,0:T(8,128)(2,1)}), bf16[16,224,128]{2,1,0:T(8,128)(2,1)S(1)}, u32[]{:S(2)}, u32[]{:S(2)}) async-start(bf16[16,224,128]{2,1,0:T(8,128)(2,1)} %copy.50), calls=%async_computation | async-start | bytes 1835008 | tf_op jit(solution)/shard_map/all_to_all | solution.py:14
  17.6 1.9 collective-permute-start
  19.8 1.2 collective-permute-done
  21.0 0.9 maximum_select_fusion
  21.9 11.7 %all-to-all-done = bf16[16,224,128]{2,1,0:T(8,128)(2,1)S(1)} async-done(((bf16[16,224,128]{2,1,0:T(8,128)(2,1)}), bf16[16,224,128]{2,1,0:T(8,128)(2,1)S(1)}, u32[]{:S(2)}, u32[]{:S(2)}) %all-to-all-start) | async-done | bytes 917536 | tf_op jit(solution)/shard_map/all_to_all | solution.py:14
  33.7 1.3 fusion.1
  35.1 3.6 %all-to-all-start.1 = ((bf16[16,128,224]{1,2,0:T(8,128)(2,1)}), bf16[16,128,224]{1,2,0:T(8,128)(2,1)S(1)}, u32[]{:S(2)}, u32[]{:S(2)}) async-start(bf16[16,128,224]{1,2,0:T(8,128)(2,1)} %fusion.1), calls=%async_computation.1 | async-start | bytes 1835008 | tf_op jit(solution)/shard_map/all_to_all | solution.py:14
  38.7 19.5 %all-gather = bf16[896,128]{1,0:T(8,128)(2,1)S(1)} all-gather(bf16[224,128]{1,0:T(8,128)(2,1)S(1)} %reduce_sum.45), channel_id=2, replica_groups=mesh['y'=4,'x'=4,'z'=16,'core'=2] {'x'}, dimensions={0}, use_global_device_ids=true | all-gather | bytes 286720 | tf_op jit(solution)/shard_map/all_gather | solution.py:62
  58.4 0.7 copy.54
  59.1 15.2 %all-to-all-start.2 = ((bf16[16,8,224]{2,1,0:T(8,128)(2,1)}), bf16[16,8,224]{2,1,0:T(8,128)(2,1)S(1)}, u32[]{:S(2)}, u32[]{:S(2)}) async-start(bf16[16,8,224]{2,1,0:T(8,128)(2,1)} %bitcast.16), calls=%async_computation.2 | async-start | bytes 131072 | tf_op jit(solution)/shard_map/all_to_all | solution.py:14
  74.3 14.8 %all_gather.17 = bf16[16,224,128]{2,1,0:T(8,128)(2,1)S(1)} all-gather(bf16[4,224,128]{2,1,0:T(8,128)(2,1)S(1)} %bitcast.92), channel_id=1, replica_groups=mesh['y'=4,'x'=4,'z'=16,'core'=2] {'y'}, dimensions={0}, use_global_device_ids=true | all-gather | bytes 1146880 | tf_op jit(solution)/shard_map/all_gather | solution.py:67
  89.8 1.0 broadcast_in_dim.14
  90.8 4.1 %all-to-all-start.3 = ((bf16[16,8,3584]{2,1,0:T(8,128)(2,1)}), bf16[16,8,3584]{2,1,0:T(8,128)(2,1)S(1)}, u32[]{:S(2)}, u32[]{:S(2)}) async-start(bf16[16,8,3584]{2,1,0:T(8,128)(2,1)} %broadcast_in_dim.14), calls=%async_computation.3 | async-start | bytes 1835008 | tf_op jit(solution)/shard_map/all_to_all | solution.py:14
  94.9 1.2 convolution_multiply_fusion
  96.2 2.1 %collective-permute-start.1 = (bf16[16,64,128]{2,1,0:T(8,128)(2,1)S(1)}, bf16[16,64,128]{2,1,0:T(8,128)(2,1)S(1)}, u32[]{:S(2)}, u32[]{:S(2)}) collective-permute-start(bf16[16,64,128]{2,1,0:T(8,128)(2,1)S(1)} %fusion.9), channel_id=1, source_target_pairs={{0,1},{1,0},{2,3},{3,2},{4,5},{5,4},{6,7},{7,6},{8,9},{9,8},{10,11... | collective-permute-start | bytes 786440 | tf_op jit(solution)/shard_map/ppermute | solution.py:18
  98.2 1.5 collective-permute-done.1
  99.7 0.8 fusion.4
  100.5 6.7 %all-to-all-done.3 = bf16[16,8,3584]{2,1,0:T(8,128)(2,1)S(1)} async-done(((bf16[16,8,3584]{2,1,0:T(8,128)(2,1)}), bf16[16,8,3584]{2,1,0:T(8,128)(2,1)S(1)}, u32[]{:S(2)}, u32[]{:S(2)}) %all-to-all-start.3) | async-done | bytes 917536 | tf_op jit(solution)/shard_map/all_to_all | solution.py:14
  107.3 3.5 %fusion.20 = (bf16[128,448]{0,1:T(8,128)(2,1)S(1)}, f32[128,448]{0,1:T(8,128)S(1)}) fusion(bf16[3584,448]{1,0:T(8,128)(2,1)} %all-gather.4.cloned.1.call-done, bf16[16,8,3584]{2,1,0:T(8,128)(2,1)S(1)} %all-to-all-done.3), kind=kOutput, calls=%fused_computation.41 | convolution fusion | flops 411099136 | bytes 4472832 | tf_op jit(solution)/shard_map/dot_general | solution.py:81
  110.8 1.9 collective-permute-start.2
  113.0 1.0 collective-permute-done.2
  114.1 3.4 %fusion = bf16[16,8,3584]{2,1,0:T(8,128)(2,1)S(1)} fusion(bf16[3584,448]{1,0:T(8,128)(2,1)} %all-gather.4.cloned.1.call-done, f32[128,448]{0,1:T(8,128)S(1)} %get-tuple-element.47, f32[128,448]{0,1:T(8,128)S(1)} %get-tuple-element.46), kind=kOutput, calls=%fused_computation.1 | convolution fusion | flops 411787264 | bytes 4587520 | tf_op jit(solution)/shard_map/dot_general | solution.py:91
  117.5 19.2 %all_to_all.35 = bf16[16,8,3584]{2,1,0:T(8,128)(2,1)S(1)} all-to-all(bf16[16,8,3584]{2,1,0:T(8,128)(2,1)S(1)} %fusion), channel_id=1, replica_groups=mesh['y'=4,'x'=4,'z'=16,'core'=2] {'y','x'}, dimensions={0} | all-to-all | bytes 1835008 | tf_op jit(solution)/shard_map/all_to_all | solution.py:14
  137.1 32.1 %all_to_all.36 = bf16[16,80,128]{2,1,0:T(8,128)(2,1)S(1)} all-to-all(bf16[16,80,128]{2,1,0:T(8,128)(2,1)S(1)} %pad_maximum_fusion), channel_id=1, replica_groups=mesh['y'=4,'x'=4,'z'=16,'core'=2] {'z'}, dimensions={0} | all-to-all | bytes 655360 | tf_op jit(solution)/shard_map/all_to_all | solution.py:14
  169.3 1.1 broadcast_in_dim.15
  170.4 3.6 %all-to-all-start.6 = ((bf16[16,224,128]{2,1,0:T(8,128)(2,1)}), bf16[16,224,128]{2,1,0:T(8,128)(2,1)S(1)}, u32[]{:S(2)}, u32[]{:S(2)}) async-start(bf16[16,224,128]{2,1,0:T(8,128)(2,1)} %broadcast_in_dim.15), calls=%async_computation.6 | async-start | bytes 1835008 | tf_op jit(solution)/shard_map/all_to_all | solution.py:14
  174.2 0.8 copy.62
  175.0 0.8 copy.63
  176.4 10.9 %all-to-all-done.6 = bf16[16,224,128]{2,1,0:T(8,128)(2,1)S(1)} async-done(((bf16[16,224,128]{2,1,0:T(8,128)(2,1)}), bf16[16,224,128]{2,1,0:T(8,128)(2,1)S(1)}, u32[]{:S(2)}, u32[]{:S(2)}) %all-to-all-start.6) | async-done | bytes 917536 | tf_op jit(solution)/shard_map/all_to_all | solution.py:14
  187.3 1.0 convolution_bitcast_fusion
  (39 shorter events, 3.7 us)
Async XLA Ops:
  7.2 10.4 %copy-start.5 = (f32[448,64]{0,1:T(8,128)S(1)}, f32[448,64]{0,1:T(8,128)}, u32[]{:S(2)}) copy-start(f32[448,64]{0,1:T(8,128)} %param.8) | copy-start | bytes 344068
  7.2 10.4 %copy-start.4 = (f32[448,64]{0,1:T(8,128)S(1)}, f32[448,64]{0,1:T(8,128)}, u32[]{:S(2)}) copy-start(f32[448,64]{0,1:T(8,128)} %param.9) | copy-start | bytes 344068
  7.2 12.4 %copy-start.3 = (bf16[128,2048]{1,0:T(8,128)(2,1)S(1)}, bf16[128,2048]{1,0:T(8,128)(2,1)}, u32[]{:S(2)}) copy-start(bf16[128,2048]{1,0:T(8,128)(2,1)} %param.6) | copy-start | bytes 1572868
  7.2 100.1 %all-gather.4.cloned.1.call-start = ((), (), s32[]{:S(2)}) async-start(), calls=%async_computation.7 | async-start | bytes 3899392 | tf_op jit(solution)/shard_map/all_gather | solution.py:47
  10.5 23.1 %all-to-all-start = ((bf16[16,224,128]{2,1,0:T(8,128)(2,1)}), bf16[16,224,128]{2,1,0:T(8,128)(2,1)S(1)}, u32[]{:S(2)}, u32[]{:S(2)}) async-start(bf16[16,224,128]{2,1,0:T(8,128)(2,1)} %copy.50), calls=%async_computation | async-start | bytes 1835008 | tf_op jit(solution)/shard_map/all_to_all | solution.py:14
  17.6 3.4 %collective-permute-start = (f32[2,64,448]{2,1,0:T(8,128)S(1)}, f32[2,64,448]{2,1,0:T(8,128)S(1)}, u32[]{:S(2)}, u32[]{:S(2)}) collective-permute-start(f32[2,64,448]{2,1,0:T(8,128)S(1)} %get-tuple-element.49), channel_id=1, source_target_pairs={{0,1},{1,0},{2,3},{3,2},{4,5},{5,4},{6,7},{7,6},{8,9},{9,8},{10,11... | collective-permute-start | bytes 688136 | tf_op jit(solution)/shard_map/ppermute | solution.py:18
  33.7 55.4 %copy-start.2 = (bf16[224,128]{1,0:T(8,128)(2,1)}, bf16[224,128]{1,0:T(8,128)(2,1)S(1)}, u32[]{:S(2)}) copy-start(bf16[224,128]{1,0:T(8,128)(2,1)S(1)} %reduce_sum.45) | copy-start | bytes 172036
  35.1 23.2 %all-to-all-start.1 = ((bf16[16,128,224]{1,2,0:T(8,128)(2,1)}), bf16[16,128,224]{1,2,0:T(8,128)(2,1)S(1)}, u32[]{:S(2)}, u32[]{:S(2)}) async-start(bf16[16,128,224]{1,2,0:T(8,128)(2,1)} %fusion.1), calls=%async_computation.1 | async-start | bytes 1835008 | tf_op jit(solution)/shard_map/all_to_all | solution.py:14
  59.1 30.0 %all-to-all-start.2 = ((bf16[16,8,224]{2,1,0:T(8,128)(2,1)}), bf16[16,8,224]{2,1,0:T(8,128)(2,1)S(1)}, u32[]{:S(2)}, u32[]{:S(2)}) async-start(bf16[16,8,224]{2,1,0:T(8,128)(2,1)} %bitcast.16), calls=%async_computation.2 | async-start | bytes 131072 | tf_op jit(solution)/shard_map/all_to_all | solution.py:14
  90.8 16.5 %all-to-all-start.3 = ((bf16[16,8,3584]{2,1,0:T(8,128)(2,1)}), bf16[16,8,3584]{2,1,0:T(8,128)(2,1)S(1)}, u32[]{:S(2)}, u32[]{:S(2)}) async-start(bf16[16,8,3584]{2,1,0:T(8,128)(2,1)} %broadcast_in_dim.14), calls=%async_computation.3 | async-start | bytes 1835008 | tf_op jit(solution)/shard_map/all_to_all | solution.py:14
  96.1 16.6 %copy-start = (f32[2,2,64,448]{3,2,1,0:T(8,128)S(1)}, f32[2,2,64,448]{3,2,1,0:T(8,128)}, u32[]{:S(2)}) copy-start(f32[2,2,64,448]{3,2,1,0:T(8,128)} %maximum_select_fusion) | copy-start | bytes 1376260
  96.2 3.6 %collective-permute-start.1 = (bf16[16,64,128]{2,1,0:T(8,128)(2,1)S(1)}, bf16[16,64,128]{2,1,0:T(8,128)(2,1)S(1)}, u32[]{:S(2)}, u32[]{:S(2)}) collective-permute-start(bf16[16,64,128]{2,1,0:T(8,128)(2,1)S(1)} %fusion.9), channel_id=1, source_target_pairs={{0,1},{1,0},{2,3},{3,2},{4,5},{5,4},{6,7},{7,6},{8,9},{9,8},{10,11... | collective-permute-start | bytes 786440 | tf_op jit(solution)/shard_map/ppermute | solution.py:18
  110.8 3.2 %collective-permute-start.2 = (bf16[128,448]{0,1:T(8,128)(2,1)S(1)}, bf16[128,448]{0,1:T(8,128)(2,1)S(1)}, u32[]{:S(2)}, u32[]{:S(2)}) collective-permute-start(bf16[128,448]{0,1:T(8,128)(2,1)S(1)} %get-tuple-element.50), channel_id=1, source_target_pairs={{0,1},{1,0},{2,3},{3,2},{4,5},{5,4},{6,7},{7,6},{8,9},{9,8},{10,11... | collective-permute-start | bytes 344072 | tf_op jit(solution)/shard_map/ppermute | solution.py:18
  114.1 23.0 %copy-start.1 = (bf16[16,64,128]{2,1,0:T(8,128)(2,1)S(1)}, bf16[16,64,128]{2,1,0:T(8,128)(2,1)}, u32[]{:S(2)}) copy-start(bf16[16,64,128]{2,1,0:T(8,128)(2,1)} %fusion.4) | copy-start | bytes 786436
  170.4 17.0 %all-to-all-start.6 = ((bf16[16,224,128]{2,1,0:T(8,128)(2,1)}), bf16[16,224,128]{2,1,0:T(8,128)(2,1)S(1)}, u32[]{:S(2)}, u32[]{:S(2)}) async-start(bf16[16,224,128]{2,1,0:T(8,128)(2,1)} %broadcast_in_dim.15), calls=%async_computation.6 | async-start | bytes 1835008 | tf_op jit(solution)/shard_map/all_to_all | solution.py:14
Sparse Core Ops, SparseCore 0:
  10.1 83.0 all-gather.3

commit v7 on v5

v7 whole, which is shorter than its diff:
```python
import jax
import jax.numpy as jnp
from jax import lax
from jax.experimental import pallas as pl
from jax.experimental.pallas import tpu as pltpu
from jax.sharding import Mesh, PartitionSpec as P

D = 7168
DP = ("y", "x")
F32 = jnp.float32
BF16 = jnp.bfloat16
LANES = 128


def exchange(chunks, axes):
    return lax.all_to_all(chunks, axes, 0, 0, tiled=True)


def swap_cores(block):
    return lax.ppermute(block, "core", [(0, 1), (1, 0)])


def to_tiles(block):
    z, sub, cols = block.shape
    block = jnp.pad(block, ((0, 0), (0, 0), (0, 2 * LANES - cols)))
    return block.reshape(z, sub, 2, LANES).transpose(0, 2, 1, 3).reshape(z, 2 * sub, LANES)


def from_tiles(block, cols):
    z, rows, _ = block.shape
    block = block.reshape(z, 2, rows // 2, LANES).transpose(0, 2, 1, 3)
    return block.reshape(z, rows // 2, 2 * LANES)[:, :, :cols]


def rotate_kernel(turned_ref, basis_ref, total_ref, send_ref):
    total = jnp.dot(turned_ref[...], basis_ref[...], preferred_element_type=F32)
    total_ref[...] = total
    send_ref[...] = total.astype(BF16)


def vmem():
    return pl.BlockSpec(memory_space=pltpu.VMEM)


def rotate(turned, basis):
    rows, depth = turned.shape
    turns = basis.shape[1]
    return pl.pallas_call(
        rotate_kernel,
        in_specs=[vmem(), vmem()],
        out_specs=[vmem(), vmem()],
        out_shape=[
            jax.ShapeDtypeStruct((rows, turns), F32),
            jax.ShapeDtypeStruct((rows, turns), BF16),
        ],
        compiler_params=pltpu.CompilerParams(vmem_limit_bytes=32 * 2**20),
        cost_estimate=pl.CostEstimate(
            flops=2 * rows * depth * turns,
            bytes_accessed=2 * depth * (rows + turns) + 6 * rows * turns,
            transcendentals=0,
        ),
    )(turned, basis)


def update_kernel(
    core_ref, total_ref, theirs_ref, moments_ref, basis_ref, first_ref, second_ref, back_ref
):
    half = first_ref.shape[0]
    updates = []
    for i in range(2):
        rows = slice(i * half, (i + 1) * half)
        rotated = total_ref[rows, :] + theirs_ref[rows, :].astype(F32)
        first = 0.9 * moments_ref[i, 0] + 0.1 * rotated
        second = 0.95 * moments_ref[i, 1] + 0.05 * rotated * rotated
        updates.append(first / 0.19 / (jnp.sqrt(second / 0.0975) + 1e-08))

        @pl.when(core_ref[0] == i)
        def _():
            first_ref[...] = first
            second_ref[...] = second

    update = jnp.concatenate(updates, axis=0).astype(BF16)
    step = 512
    for i in range(basis_ref.shape[0] // step):
        part = slice(i * step, (i + 1) * step)
        back_ref[:, part] = lax.dot_general(
            update, basis_ref[part, :], (((1,), (1,)), ((), ())), preferred_element_type=F32
        ).astype(BF16)


def update_and_back(core, total, theirs, moments, basis):
    rows, turns = total.shape
    depth = basis.shape[0]
    half = rows // 2
    return pl.pallas_call(
        update_kernel,
        in_specs=[pl.BlockSpec(memory_space=pltpu.SMEM)] + [vmem()] * 4,
        out_specs=[vmem()] * 3,
        out_shape=[
            jax.ShapeDtypeStruct((half, turns), F32),
            jax.ShapeDtypeStruct((half, turns), F32),
            jax.ShapeDtypeStruct((rows, depth), BF16),
        ],
        compiler_params=pltpu.CompilerParams(vmem_limit_bytes=32 * 2**20),
        cost_estimate=pl.CostEstimate(
            flops=2 * rows * depth * turns,
            bytes_accessed=2 * depth * (rows + turns) + 22 * rows * turns,
            transcendentals=rows * turns,
        ),
    )(core.reshape(1), total, theirs, moments, basis)


def on_device(grad_parts, left_basis, right_basis, first_moment, second_moment):
    rows = left_basis.shape[0]
    cols = right_basis.shape[0]
    turns = right_basis.shape[1]
    n_dp = left_basis.shape[1] // rows
    n_z = lax.axis_size("z")
    sub = rows // n_dp
    half = rows // 2
    core = lax.axis_index("core")

    def both(block):
        theirs = swap_cores(block)
        return jnp.where(core == 0, jnp.stack([block, theirs]), jnp.stack([theirs, block]))

    basis_z = lax.all_gather(right_basis, "z", axis=0, tiled=False)

    parts, moments = lax.optimization_barrier(
        (
            exchange(grad_parts[0].reshape(n_dp, rows, cols), DP),
            both(jnp.stack([first_moment.T, second_moment.T])),
        )
    )
    grad_t = jnp.sum(parts.astype(F32), axis=0).astype(BF16).T

    basis_p = (
        left_basis.reshape(rows, n_z, n_dp, sub).transpose(0, 2, 1, 3).reshape(rows, n_dp, rows)
    )
    left_term = lax.dot_general(
        basis_p, grad_t, (((0,), (1,)), ((), ())), preferred_element_type=F32
    )
    turned = exchange(left_term.astype(BF16), DP)
    turned = jnp.sum(turned.astype(F32), axis=0).astype(BF16).reshape(n_z, sub, cols)

    turned, copies = lax.optimization_barrier(
        (exchange(turned, "z"), jnp.broadcast_to(grad_t[None], (n_dp, cols, rows)))
    )
    turned = turned.transpose(1, 0, 2).reshape(1, sub, n_z * cols)
    turned = exchange(jnp.broadcast_to(turned, (n_dp, sub, n_z * cols)), DP)

    turned, copies = lax.optimization_barrier((turned, copies))
    grad_all = exchange(copies, DP)

    basis_z = basis_z.reshape(n_z * cols, turns)
    total, send = rotate(turned.reshape(rows, n_z * cols), basis_z)
    new_first, new_second, back = update_and_back(
        core, total, swap_cores(send), moments, basis_z
    )
    back, grad_all = lax.optimization_barrier((back, grad_all))
    back = exchange(back.reshape(n_dp, sub, n_z * cols), DP)

    gram = lax.dot_general(
        grad_all, grad_t, (((1,), (0,)), ((), ())), preferred_element_type=F32
    ).reshape(n_z, 2, half, rows) / D
    mine = lax.dynamic_index_in_dim(gram, core, 1, keepdims=False)
    other = lax.dynamic_index_in_dim(gram, 1 - core, 1, keepdims=False)
    gram = mine + swap_cores(other.astype(BF16)).astype(F32)
    quarter = half // 2
    gram = gram.reshape(n_z, 2, quarter, rows)
    low = lax.axis_index("z") % 2
    mine = lax.dynamic_index_in_dim(gram, low, 1, keepdims=False)
    other = lax.dynamic_index_in_dim(gram, 1 - low, 1, keepdims=False)
    pairs = [(i, i ^ 1) for i in range(n_z)]
    gram = mine + lax.ppermute(other.astype(BF16), "z", pairs).astype(F32)
    gram = gram.astype(BF16)
    back, gram = lax.optimization_barrier((back, gram))

    back = jnp.sum(back.astype(F32), axis=0).astype(BF16)
    back = back.reshape(sub, n_z, cols).transpose(1, 0, 2)
    packed = exchange(jnp.concatenate([to_tiles(back), gram], axis=1), "z")
    back = from_tiles(packed[:, : 2 * sub], cols)
    left_gram = packed[:, 2 * sub :].reshape(n_z // 2, half, rows)
    left_gram = jnp.sum(left_gram.astype(F32), axis=0)
    back = back.reshape(rows, cols).T
    back = exchange(jnp.broadcast_to(back[None], (n_dp, cols, rows)), DP)
    direction = lax.dot_general(
        basis_p, back, (((1, 2), (0, 2)), ((), ())), preferred_element_type=F32
    )
    return (left_gram.T, new_first.T, new_second.T, direction)


def solution(mesh):
    n_dp, n_col = mesh.shape["dp"], mesh.shape["col"]
    side = int(round(n_dp**0.5))
    fine = Mesh(
        mesh.devices.reshape(side, side, n_col // 2, 2), ("y", "x", "z", "core")
    )
    dp, col = ("y", "x"), ("z", "core")
    in_specs = (P(dp, None, col), P(dp, None), P(col, dp), P(dp, col), P(dp, col))
    out_specs = (P(dp, col), P(dp, col), P(dp, col), P(dp, col))
    return jax.shard_map(
        on_device, mesh=fine, in_specs=in_specs, out_specs=out_specs, check_vma=False
    )
```

time: 192 us -> 187 us (0.974)
  blocking collectives: 51.5 us -> 81.5 us
  waiting for transfers between devices: 68.1 us -> 46.2 us
  matrix products: 11.5 us -> 1.85 us
  starting transfers between devices: 34.4 us -> 27.8 us
  Pallas kernels: 0 us -> 3.18 us
    all_to_all x2 -> x4, blocking collectives: 51.5 us -> 81.5 us  [exchange(): return lax.all_to_all(chunks, axes, 0, 0, tiled=True)]
    all_to_all x6 -> x4, waiting for transfers between devices: 63.5 us -> 38.4 us  [exchange(): return lax.all_to_all(chunks, axes, 0, 0, tiled=True)]
    all_to_all x6 -> x4, starting transfers between devices: 28.5 us -> 19.2 us  [exchange(): return lax.all_to_all(chunks, axes, 0, 0, tiled=True)]
    dot_general x2 -> x0, matrix products: 7.9 us -> none  [the longest x1 4.38 us: on_device(): lax.dot_general(update, basis_z, (((1,), (1,)), ((), ())), preferred_elem...]
    ppermute x0 -> x1, waiting for transfers between devices: none -> 4.57 us  [on_device(): gram = mine + lax.ppermute(other.astype(BF16), 'z', pairs).astype(F32)]
    pallas_call x0 -> x2, Pallas kernels: none -> 3.18 us  [the longest x1 2.54 us: update_and_back(): pl.pallas_call(update_kernel, in_specs=[pl.BlockSpec(memory_space=pltpu.S...]
    ppermute x0 -> x1, starting transfers between devices: none -> 2.79 us  [on_device(): gram = mine + lax.ppermute(other.astype(BF16), 'z', pairs).astype(F32)]
    unnamed x21 -> x13, local copies, waits for them, and re-layouts: 4.01 us -> 5.73 us
  transfers between devices with their start and end apart: 10 -> 9, of which waited for: 9 -> 7; matrix products, arithmetic and copies ran while one was open for 10% -> 3% of each run, Pallas kernels for 0% -> 2%
where the time goes in v7:
time: 187 us; the launch traced here: 186 us
  blocking collectives  81.5 us (44%)
  waiting for transfers between devices  46.2 us (25%)
  starting transfers between devices  27.8 us (15%)
  between operations  14.4 us (8%)
  local copies, waits for them, and re-layouts  10.2 us (5%)
  Pallas kernels  3.18 us (2%)
    all_to_all x4, blocking collectives, exchange(): return lax.all_to_all(chunks, axes, 0, 0, tiled=True)  81.5 us
    all_to_all x4, waiting for transfers between devices, exchange(): return lax.all_to_all(chunks, axes, 0, 0, tiled=True)  38.4 us
    all_to_all x4, starting transfers between devices, exchange(): return lax.all_to_all(chunks, axes, 0, 0, tiled=True)  19.2 us
    ppermute x3, starting transfers between devices, swap_cores(): return lax.ppermute(block, 'core', [(0, 1), (1, 0)])  5.76 us
    unnamed x13, local copies, waits for them, and re-layouts  5.73 us
    ppermute x1, waiting for transfers between devices, on_device(): gram = mine + lax.ppermute(other.astype(BF16), 'z', pairs).astype(F32)  4.57 us
  transfers between devices with their start and end apart: 9, of which 7 were waited for; matrix products, arithmetic and copies ran while one was open for 3% of the time, Pallas kernels for 2%

profile of v7, /device:TPU:32, one launch (start us, length us, event | category | flops | bytes accessed | tf_op | source)
XLA Modules:
  0.0 186.3 jit_solution(2950798154511547846)
XLA Ops:
  7.2 0.7 all-gather.3.cloned.1.call-update
  7.9 1.4 copy.48
  9.3 1.2 copy.34
  10.5 7.0 %all-to-all-start = ((bf16[16,128,224]{1,2,0:T(8,128)(2,1)}), bf16[16,128,224]{1,2,0:T(8,128)(2,1)S(1)}, u32[]{:S(2)}, u32[]{:S(2)}) async-start(bf16[16,128,224]{1,2,0:T(8,128)(2,1)} %copy.34), calls=%async_computation | async-start | bytes 1835008 | tf_op jit(solution)/shard_map/all_to_all | solution.py:16
  17.6 1.9 %collective-permute-start = (f32[2,64,448]{2,1,0:T(8,128)S(1)}, f32[2,64,448]{2,1,0:T(8,128)S(1)}, u32[]{:S(2)}, u32[]{:S(2)}) collective-permute-start(f32[2,64,448]{2,1,0:T(8,128)S(1)} %get-tuple-element.35), channel_id=1, source_target_pairs={{0,1},{1,0},{2,3},{3,2},{4,5},{5,4},{6,7},{7,6},{8,9},{9,8},{10,11... | collective-permute-start | bytes 688136 | tf_op jit(solution)/shard_map/ppermute | solution.py:20
  19.8 1.2 collective-permute-done
  21.1 12.5 %all-to-all-done = bf16[16,128,224]{1,2,0:T(8,128)(2,1)S(1)} async-done(((bf16[16,128,224]{1,2,0:T(8,128)(2,1)}), bf16[16,128,224]{1,2,0:T(8,128)(2,1)S(1)}, u32[]{:S(2)}, u32[]{:S(2)}) %all-to-all-start) | async-done | bytes 917536 | tf_op jit(solution)/shard_map/all_to_all | solution.py:16
  34.1 18.1 %all_to_all.40 = bf16[16,128,224]{1,2,0:T(8,128)(2,1)S(1)} all-to-all(bf16[16,128,224]{1,2,0:T(8,128)(2,1)S(1)} %fusion), channel_id=1, replica_groups=mesh['y'=4,'x'=4,'z'=16,'core'=2] {'y','x'}, dimensions={0} | all-to-all | bytes 1835008 | tf_op jit(solution)/shard_map/all_to_all | solution.py:16
  52.4 27.1 %all_to_all.41 = bf16[16,8,224]{2,1,0:T(8,128)(2,1)S(1)} all-to-all(bf16[16,8,224]{2,1,0:T(8,128)(2,1)S(1)} %bitcast.93), channel_id=1, replica_groups=mesh['y'=4,'x'=4,'z'=16,'core'=2] {'z'}, dimensions={0} | all-to-all | bytes 114688 | tf_op jit(solution)/shard_map/all_to_all | solution.py:16
  79.5 1.1 broadcast_in_dim.8
  80.7 16.5 %all_to_all.42 = bf16[16,8,3584]{2,1,0:T(8,128)(2,1)S(1)} all-to-all(bf16[16,8,3584]{2,1,0:T(8,128)(2,1)S(1)} %broadcast_in_dim.10), channel_id=1, replica_groups=mesh['y'=4,'x'=4,'z'=16,'core'=2] {'y','x'}, dimensions={0} | all-to-all | bytes 1835008 | tf_op jit(solution)/shard_map/all_to_all | solution.py:16
  97.3 3.6 %all-to-all-start.4 = ((bf16[16,224,128]{2,1,0:T(8,128)(2,1)}), bf16[16,224,128]{2,1,0:T(8,128)(2,1)S(1)}, u32[]{:S(2)}, u32[]{:S(2)}) async-start(bf16[16,224,128]{2,1,0:T(8,128)(2,1)} %broadcast_in_dim.8), calls=%async_computation.4 | async-start | bytes 1835008 | tf_op jit(solution)/shard_map/all_to_all | solution.py:16
  100.9 2.0 %copy-done = bf16[3584,448]{1,0:T(8,128)(2,1)S(1)} copy-done((bf16[3584,448]{1,0:T(8,128)(2,1)S(1)}, bf16[3584,448]{1,0:T(8,128)(2,1)}, u32[]{:S(2)}) %copy-start) | copy-done | bytes 3211288
  103.0 0.6 shard_map.84
  103.6 1.9 %collective-permute-start.1 = (bf16[128,448]{1,0:T(8,128)(2,1)S(1)}, bf16[128,448]{1,0:T(8,128)(2,1)S(1)}, u32[]{:S(2)}, u32[]{:S(2)}) collective-permute-start(bf16[128,448]{1,0:T(8,128)(2,1)S(1)} %get-tuple-element.24), channel_id=1, source_target_pairs={{0,1},{1,0},{2,3},{3,2},{4,5},{5,4},{6,7},{7,6},{8,9},{9,8},{10,11... | collective-permute-start | bytes 344072 | tf_op jit(solution)/shard_map/ppermute | solution.py:20
  105.5 1.3 collective-permute-done.1.theirs_ref
  106.9 2.0 %copy-done.1 = bf16[3584,448]{1,0:T(8,128)(2,1)S(1)} copy-done((bf16[3584,448]{1,0:T(8,128)(2,1)S(1)}, bf16[3584,448]{1,0:T(8,128)(2,1)}, u32[]{:S(2)}) %copy-start.1) | copy-done | bytes 3211288
  108.9 2.5 %shard_map.85 = (f32[64,448]{1,0:T(8,128)}, f32[64,448]{1,0:T(8,128)}, bf16[128,3584]{1,0:T(8,128)(2,1)}) custom-call(s32[1]{0:T(128)} %bitcast.core_ref, f32[128,448]{1,0:T(8,128)S(1)} %get-tuple-element.23.total_ref, bf16[128,448]{1,0:T(8,128)(2,1)S(1)} %collective-permute-done.1.theirs_ref, f32[2,2,64,448]{3,2,1,0:T(8,128)S(1)} %maximum_select_fusion.moments_ref, ...), custom_call_target="tpu_custom_call" | custom-call | flops 411041792 | bytes 5390336 | tf_op jit(solution)/shard_map/pallas_call | solution.py:95
  111.4 2.4 %all-to-all-done.4 = bf16[16,224,128]{2,1,0:T(8,128)(2,1)S(1)} async-done(((bf16[16,224,128]{2,1,0:T(8,128)(2,1)}), bf16[16,224,128]{2,1,0:T(8,128)(2,1)S(1)}, u32[]{:S(2)}, u32[]{:S(2)}) %all-to-all-start.4) | async-done | bytes 917536 | tf_op jit(solution)/shard_map/all_to_all | solution.py:16
  113.8 0.5 copy.40
  114.3 0.4 convolution_multiply_fusion
  114.8 1.9 %collective-permute-start.2 = (bf16[16,64,128]{2,1,0:T(8,128)(2,1)S(1)}, bf16[16,64,128]{2,1,0:T(8,128)(2,1)S(1)}, u32[]{:S(2)}, u32[]{:S(2)}) collective-permute-start(bf16[16,64,128]{2,1,0:T(8,128)(2,1)S(1)} %fusion.5), channel_id=1, source_target_pairs={{0,1},{1,0},{2,3},{3,2},{4,5},{5,4},{6,7},{7,6},{8,9},{9,8},{10,11... | collective-permute-start | bytes 786440 | tf_op jit(solution)/shard_map/ppermute | solution.py:20
  116.7 4.9 %all-to-all-start.5 = ((bf16[16,8,3584]{2,1,0:T(8,128)(2,1)}), bf16[16,8,3584]{2,1,0:T(8,128)(2,1)S(1)}, u32[]{:S(2)}, u32[]{:S(2)}) async-start(bf16[16,8,3584]{2,1,0:T(8,128)(2,1)} %bitcast.16), calls=%async_computation.5 | async-start | bytes 1835008 | tf_op jit(solution)/shard_map/all_to_all | solution.py:16
  121.8 2.8 %collective-permute-start.3 = (bf16[16,32,128]{2,1,0:T(8,128)(2,1)S(1)}, bf16[16,32,128]{2,1,0:T(8,128)(2,1)S(1)}, u32[]{:S(2)}, u32[]{:S(2)}) collective-permute-start(bf16[16,32,128]{2,1,0:T(8,128)(2,1)S(1)} %fusion.7), channel_id=1, source_target_pairs={{0,2},{2,0},{4,6},{6,4},{8,10},{10,8},{12,14},{14,12},{16,18},{18,... | collective-permute-start | bytes 393224 | tf_op jit(solution)/shard_map/ppermute | solution.py:175
  124.6 4.6 %collective-permute-done.3 = bf16[16,32,128]{2,1,0:T(8,128)(2,1)S(1)} collective-permute-done((bf16[16,32,128]{2,1,0:T(8,128)(2,1)S(1)}, bf16[16,32,128]{2,1,0:T(8,128)(2,1)S(1)}, u32[]{:S(2)}, u32[]{:S(2)}) %collective-permute-start.3) | collective-permute-done | bytes 131104 | tf_op jit(solution)/shard_map/ppermute | solution.py:175
  129.2 8.9 %all-to-all-done.5 = bf16[16,8,3584]{2,1,0:T(8,128)(2,1)S(1)} async-done(((bf16[16,8,3584]{2,1,0:T(8,128)(2,1)}), bf16[16,8,3584]{2,1,0:T(8,128)(2,1)S(1)}, u32[]{:S(2)}, u32[]{:S(2)}) %all-to-all-start.5) | async-done | bytes 917536 | tf_op jit(solution)/shard_map/all_to_all | solution.py:16
  138.4 19.9 %all_to_all.43 = bf16[16,48,128]{2,1,0:T(8,128)(2,1)S(1)} all-to-all(bf16[16,48,128]{2,1,0:T(8,128)(2,1)S(1)} %pad_maximum_fusion.1), channel_id=1, replica_groups=mesh['y'=4,'x'=4,'z'=16,'core'=2] {'z'}, dimensions={0} | all-to-all | bytes 393216 | tf_op jit(solution)/shard_map/all_to_all | solution.py:16
  158.4 1.1 broadcast_in_dim.22
  159.5 3.6 %all-to-all-start.7 = ((bf16[16,224,128]{2,1,0:T(8,128)(2,1)}), bf16[16,224,128]{2,1,0:T(8,128)(2,1)S(1)}, u32[]{:S(2)}, u32[]{:S(2)}) async-start(bf16[16,224,128]{2,1,0:T(8,128)(2,1)} %broadcast_in_dim.22), calls=%async_computation.7 | async-start | bytes 1835008 | tf_op jit(solution)/shard_map/all_to_all | solution.py:16
  163.1 0.6 convert_reduce_fusion
  163.8 14.7 %all-to-all-done.7 = bf16[16,224,128]{2,1,0:T(8,128)(2,1)S(1)} async-done(((bf16[16,224,128]{2,1,0:T(8,128)(2,1)}), bf16[16,224,128]{2,1,0:T(8,128)(2,1)S(1)}, u32[]{:S(2)}, u32[]{:S(2)}) %all-to-all-start.7) | async-done | bytes 917536 | tf_op jit(solution)/shard_map/all_to_all | solution.py:16
  178.5 1.0 convolution_bitcast_fusion
  (34 shorter events, 2.0 us)
Async XLA Ops:
  7.2 10.3 %copy-start.4 = (f32[448,64]{0,1:T(8,128)S(1)}, f32[448,64]{0,1:T(8,128)}, u32[]{:S(2)}) copy-start(f32[448,64]{0,1:T(8,128)} %param.8) | copy-start | bytes 344068
  7.2 10.3 %copy-start.3 = (f32[448,64]{0,1:T(8,128)S(1)}, f32[448,64]{0,1:T(8,128)}, u32[]{:S(2)}) copy-start(f32[448,64]{0,1:T(8,128)} %param.9) | copy-start | bytes 344068
  7.2 12.3 %copy-start.2 = (bf16[128,2048]{1,0:T(8,128)(2,1)S(1)}, bf16[128,2048]{1,0:T(8,128)(2,1)}, u32[]{:S(2)}) copy-start(bf16[128,2048]{1,0:T(8,128)(2,1)} %param.6) | copy-start | bytes 1572868
  7.2 93.7 %all-gather.3.cloned.1.call-start = ((), (), s32[]{:S(2)}) async-start(), calls=%async_computation.8 | async-start | bytes 3899392 | tf_op jit(solution)/shard_map/all_gather | solution.py:127
  10.5 23.1 %all-to-all-start = ((bf16[16,128,224]{1,2,0:T(8,128)(2,1)}), bf16[16,128,224]{1,2,0:T(8,128)(2,1)S(1)}, u32[]{:S(2)}, u32[]{:S(2)}) async-start(bf16[16,128,224]{1,2,0:T(8,128)(2,1)} %copy.34), calls=%async_computation | async-start | bytes 1835008 | tf_op jit(solution)/shard_map/all_to_all | solution.py:16
  17.6 3.4 %collective-permute-start = (f32[2,64,448]{2,1,0:T(8,128)S(1)}, f32[2,64,448]{2,1,0:T(8,128)S(1)}, u32[]{:S(2)}, u32[]{:S(2)}) collective-permute-start(f32[2,64,448]{2,1,0:T(8,128)S(1)} %get-tuple-element.35), channel_id=1, source_target_pairs={{0,1},{1,0},{2,3},{3,2},{4,5},{5,4},{6,7},{7,6},{8,9},{9,8},{10,11... | collective-permute-start | bytes 688136 | tf_op jit(solution)/shard_map/ppermute | solution.py:20
  97.3 16.5 %all-to-all-start.4 = ((bf16[16,224,128]{2,1,0:T(8,128)(2,1)}), bf16[16,224,128]{2,1,0:T(8,128)(2,1)S(1)}, u32[]{:S(2)}, u32[]{:S(2)}) async-start(bf16[16,224,128]{2,1,0:T(8,128)(2,1)} %broadcast_in_dim.8), calls=%async_computation.4 | async-start | bytes 1835008 | tf_op jit(solution)/shard_map/all_to_all | solution.py:16
  100.9 2.0 %copy-start = (bf16[3584,448]{1,0:T(8,128)(2,1)S(1)}, bf16[3584,448]{1,0:T(8,128)(2,1)}, u32[]{:S(2)}) copy-start(bf16[3584,448]{1,0:T(8,128)(2,1)} %all-gather.3.cloned.1.call-done.basis_ref) | copy-start | bytes 9633796
  103.6 3.2 %collective-permute-start.1 = (bf16[128,448]{1,0:T(8,128)(2,1)S(1)}, bf16[128,448]{1,0:T(8,128)(2,1)S(1)}, u32[]{:S(2)}, u32[]{:S(2)}) collective-permute-start(bf16[128,448]{1,0:T(8,128)(2,1)S(1)} %get-tuple-element.24), channel_id=1, source_target_pairs={{0,1},{1,0},{2,3},{3,2},{4,5},{5,4},{6,7},{7,6},{8,9},{9,8},{10,11... | collective-permute-start | bytes 344072 | tf_op jit(solution)/shard_map/ppermute | solution.py:20
  106.9 2.0 %copy-start.1 = (bf16[3584,448]{1,0:T(8,128)(2,1)S(1)}, bf16[3584,448]{1,0:T(8,128)(2,1)}, u32[]{:S(2)}) copy-start(bf16[3584,448]{1,0:T(8,128)(2,1)} %all-gather.3.cloned.1.call-done.basis_ref) | copy-start | bytes 9633796
  114.8 6.9 %collective-permute-start.2 = (bf16[16,64,128]{2,1,0:T(8,128)(2,1)S(1)}, bf16[16,64,128]{2,1,0:T(8,128)(2,1)S(1)}, u32[]{:S(2)}, u32[]{:S(2)}) collective-permute-start(bf16[16,64,128]{2,1,0:T(8,128)(2,1)S(1)} %fusion.5), channel_id=1, source_target_pairs={{0,1},{1,0},{2,3},{3,2},{4,5},{5,4},{6,7},{7,6},{8,9},{9,8},{10,11... | collective-permute-start | bytes 786440 | tf_op jit(solution)/shard_map/ppermute | solution.py:20
  116.7 21.3 %all-to-all-start.5 = ((bf16[16,8,3584]{2,1,0:T(8,128)(2,1)}), bf16[16,8,3584]{2,1,0:T(8,128)(2,1)S(1)}, u32[]{:S(2)}, u32[]{:S(2)}) async-start(bf16[16,8,3584]{2,1,0:T(8,128)(2,1)} %bitcast.16), calls=%async_computation.5 | async-start | bytes 1835008 | tf_op jit(solution)/shard_map/all_to_all | solution.py:16
  121.8 7.4 %collective-permute-start.3 = (bf16[16,32,128]{2,1,0:T(8,128)(2,1)S(1)}, bf16[16,32,128]{2,1,0:T(8,128)(2,1)S(1)}, u32[]{:S(2)}, u32[]{:S(2)}) collective-permute-start(bf16[16,32,128]{2,1,0:T(8,128)(2,1)S(1)} %fusion.7), channel_id=1, source_target_pairs={{0,2},{2,0},{4,6},{6,4},{8,10},{10,8},{12,14},{14,12},{16,18},{18,... | collective-permute-start | bytes 393224 | tf_op jit(solution)/shard_map/ppermute | solution.py:175
  159.5 19.0 %all-to-all-start.7 = ((bf16[16,224,128]{2,1,0:T(8,128)(2,1)}), bf16[16,224,128]{2,1,0:T(8,128)(2,1)S(1)}, u32[]{:S(2)}, u32[]{:S(2)}) async-start(bf16[16,224,128]{2,1,0:T(8,128)(2,1)} %broadcast_in_dim.22), calls=%async_computation.7 | async-start | bytes 1835008 | tf_op jit(solution)/shard_map/all_to_all | solution.py:16
Sparse Core Ops, SparseCore 0:
  10.1 82.5 all-gather.2

commit v8 on v7

--- a/solution.py
+++ b/solution.py
@@ -162,18 +162,16 @@
 
     gram = lax.dot_general(
         grad_all, grad_t, (((1,), (0,)), ((), ())), preferred_element_type=F32
-    ).reshape(n_z, 2, half, rows) / D
-    mine = lax.dynamic_index_in_dim(gram, core, 1, keepdims=False)
-    other = lax.dynamic_index_in_dim(gram, 1 - core, 1, keepdims=False)
-    gram = mine + swap_cores(other.astype(BF16)).astype(F32)
-    quarter = half // 2
-    gram = gram.reshape(n_z, 2, quarter, rows)
+    ).reshape(n_z, 4, half // 2, rows) / D
     low = lax.axis_index("z") % 2
-    mine = lax.dynamic_index_in_dim(gram, low, 1, keepdims=False)
-    other = lax.dynamic_index_in_dim(gram, 1 - low, 1, keepdims=False)
-    pairs = [(i, i ^ 1) for i in range(n_z)]
-    gram = mine + lax.ppermute(other.astype(BF16), "z", pairs).astype(F32)
-    gram = gram.astype(BF16)
+    place = core * 2 + low
+    mine = lax.dynamic_index_in_dim(gram, place, 1, keepdims=False)
+    col = ("z", "core")
+    for other, flip in ((place ^ 2, 1), (place ^ 1, 2), (place ^ 3, 3)):
+        piece = lax.dynamic_index_in_dim(gram, other, 1, keepdims=False).astype(BF16)
+        pairs = [(i, i ^ flip) for i in range(2 * n_z)]
+        mine = mine + lax.ppermute(piece, col, pairs).astype(F32)
+    gram = mine.astype(BF16)
     back, gram = lax.optimization_barrier((back, gram))
 
     back = jnp.sum(back.astype(F32), axis=0).astype(BF16)

time: 187 us -> 184 us (0.984)
  waiting for transfers between devices: 46.2 us -> 39.8 us
  starting transfers between devices: 27.8 us -> 32.3 us
    ppermute x1 -> x3, starting transfers between devices: 2.79 us -> 7.59 us  [on_device(): mine = mine + lax.ppermute(piece, col, pairs).astype(F32)]
    all_to_all x4, waiting for transfers between devices: 38.4 us -> 34.1 us  [exchange(): return lax.all_to_all(chunks, axes, 0, 0, tiled=True)]
    ppermute x1 -> x3, waiting for transfers between devices: 4.57 us -> 2.44 us  [on_device(): mine = mine + lax.ppermute(piece, col, pairs).astype(F32)]
    ppermute x3 -> x2, starting transfers between devices: 5.76 us -> 3.97 us  [swap_cores(): return lax.ppermute(block, 'core', [(0, 1), (1, 0)])]
    unnamed x13 -> x15, local copies, waits for them, and re-layouts: 5.73 us -> 4.67 us
  transfers between devices with their start and end apart: 9 -> 10, of which waited for: 7 -> 7; matrix products, arithmetic and copies ran while one was open for 3% -> 4% of each run, Pallas kernels for 2% -> 2%
where the time goes in v8:
time: 184 us; the launch traced here: 183 us
  blocking collectives  80.6 us (44%)
  waiting for transfers between devices  39.8 us (22%)
  starting transfers between devices  32.3 us (18%)
  between operations  14.4 us (8%)
  local copies, waits for them, and re-layouts  9.12 us (5%)
  Pallas kernels  3.24 us (2%)
  other arithmetic  2.14 us (1%)
  matrix products  1.86 us (1%)
    all_to_all x4, blocking collectives, exchange(): return lax.all_to_all(chunks, axes, 0, 0, tiled=True)  80.6 us
    all_to_all x4, waiting for transfers between devices, exchange(): return lax.all_to_all(chunks, axes, 0, 0, tiled=True)  34.1 us
    all_to_all x4, starting transfers between devices, exchange(): return lax.all_to_all(chunks, axes, 0, 0, tiled=True)  20.7 us
    ppermute x3, starting transfers between devices, on_device(): mine = mine + lax.ppermute(piece, col, pairs).astype(F32)  7.59 us
    unnamed x15, local copies, waits for them, and re-layouts  4.67 us
    ppermute x2, starting transfers between devices, swap_cores(): return lax.ppermute(block, 'core', [(0, 1), (1, 0)])  3.97 us
  transfers between devices with their start and end apart: 10, of which 7 were waited for; matrix products, arithmetic and copies ran while one was open for 4% of the time, Pallas kernels for 2%

profile of v8, /device:TPU:32, one launch (start us, length us, event | category | flops | bytes accessed | tf_op | source)
XLA Modules:
  0.0 183.4 jit_solution(14115529848885767141)
XLA Ops:
  7.2 0.7 all-gather.3.cloned.1.call-update
  7.9 1.4 copy.60
  9.3 1.2 copy.42
  10.5 7.0 %all-to-all-start = ((bf16[16,128,224]{1,2,0:T(8,128)(2,1)}), bf16[16,128,224]{1,2,0:T(8,128)(2,1)S(1)}, u32[]{:S(2)}, u32[]{:S(2)}) async-start(bf16[16,128,224]{1,2,0:T(8,128)(2,1)} %copy.42), calls=%async_computation | async-start | bytes 1835008 | tf_op jit(solution)/shard_map/all_to_all | solution.py:16
  17.6 1.9 %collective-permute-start = (f32[2,64,448]{2,1,0:T(8,128)S(1)}, f32[2,64,448]{2,1,0:T(8,128)S(1)}, u32[]{:S(2)}, u32[]{:S(2)}) collective-permute-start(f32[2,64,448]{2,1,0:T(8,128)S(1)} %get-tuple-element.38), channel_id=1, source_target_pairs={{0,1},{1,0},{2,3},{3,2},{4,5},{5,4},{6,7},{7,6},{8,9},{9,8},{10,11... | collective-permute-start | bytes 688136 | tf_op jit(solution)/shard_map/ppermute | solution.py:20
  19.8 1.2 collective-permute-done
  21.1 12.5 %all-to-all-done = bf16[16,128,224]{1,2,0:T(8,128)(2,1)S(1)} async-done(((bf16[16,128,224]{1,2,0:T(8,128)(2,1)}), bf16[16,128,224]{1,2,0:T(8,128)(2,1)S(1)}, u32[]{:S(2)}, u32[]{:S(2)}) %all-to-all-start) | async-done | bytes 917536 | tf_op jit(solution)/shard_map/all_to_all | solution.py:16
  34.1 18.1 %all_to_all.40 = bf16[16,128,224]{1,2,0:T(8,128)(2,1)S(1)} all-to-all(bf16[16,128,224]{1,2,0:T(8,128)(2,1)S(1)} %fusion), channel_id=1, replica_groups=mesh['y'=4,'x'=4,'z'=16,'core'=2] {'y','x'}, dimensions={0} | all-to-all | bytes 1835008 | tf_op jit(solution)/shard_map/all_to_all | solution.py:16
  52.4 27.0 %all_to_all.41 = bf16[16,8,224]{2,1,0:T(8,128)(2,1)S(1)} all-to-all(bf16[16,8,224]{2,1,0:T(8,128)(2,1)S(1)} %bitcast.102), channel_id=1, replica_groups=mesh['y'=4,'x'=4,'z'=16,'core'=2] {'z'}, dimensions={0} | all-to-all | bytes 114688 | tf_op jit(solution)/shard_map/all_to_all | solution.py:16
  79.5 1.0 broadcast_in_dim.8
  80.7 16.4 %all_to_all.42 = bf16[16,8,3584]{2,1,0:T(8,128)(2,1)S(1)} all-to-all(bf16[16,8,3584]{2,1,0:T(8,128)(2,1)S(1)} %broadcast_in_dim.10), channel_id=1, replica_groups=mesh['y'=4,'x'=4,'z'=16,'core'=2] {'y','x'}, dimensions={0} | all-to-all | bytes 1835008 | tf_op jit(solution)/shard_map/all_to_all | solution.py:16
  97.1 3.6 %all-to-all-start.4 = ((bf16[16,224,128]{2,1,0:T(8,128)(2,1)}), bf16[16,224,128]{2,1,0:T(8,128)(2,1)S(1)}, u32[]{:S(2)}, u32[]{:S(2)}) async-start(bf16[16,224,128]{2,1,0:T(8,128)(2,1)} %broadcast_in_dim.8), calls=%async_computation.4 | async-start | bytes 1835008 | tf_op jit(solution)/shard_map/all_to_all | solution.py:16
  100.8 2.0 %copy-done = bf16[3584,448]{1,0:T(8,128)(2,1)S(1)} copy-done((bf16[3584,448]{1,0:T(8,128)(2,1)S(1)}, bf16[3584,448]{1,0:T(8,128)(2,1)}, u32[]{:S(2)}) %copy-start) | copy-done | bytes 3211288
  102.9 0.6 shard_map.84
  103.5 2.1 %collective-permute-start.1 = (bf16[128,448]{1,0:T(8,128)(2,1)S(1)}, bf16[128,448]{1,0:T(8,128)(2,1)S(1)}, u32[]{:S(2)}, u32[]{:S(2)}) collective-permute-start(bf16[128,448]{1,0:T(8,128)(2,1)S(1)} %get-tuple-element.24), channel_id=1, source_target_pairs={{0,1},{1,0},{2,3},{3,2},{4,5},{5,4},{6,7},{7,6},{8,9},{9,8},{10,11... | collective-permute-start | bytes 344072 | tf_op jit(solution)/shard_map/ppermute | solution.py:20
  105.6 1.3 collective-permute-done.1.theirs_ref
  106.9 2.6 %shard_map.85 = (f32[64,448]{1,0:T(8,128)}, f32[64,448]{1,0:T(8,128)}, bf16[128,3584]{1,0:T(8,128)(2,1)}) custom-call(s32[1]{0:T(128)} %bitcast.core_ref, f32[128,448]{1,0:T(8,128)S(1)} %get-tuple-element.23.total_ref, bf16[128,448]{1,0:T(8,128)(2,1)S(1)} %collective-permute-done.1.theirs_ref, f32[2,2,64,448]{3,2,1,0:T(8,128)S(1)} %maximum_select_fusion.moments_ref, ...), custom_call_target="tpu_custom_call" | custom-call | flops 411041792 | bytes 5390336 | tf_op jit(solution)/shard_map/pallas_call | solution.py:95
  109.5 4.0 %all-to-all-done.4 = bf16[16,224,128]{2,1,0:T(8,128)(2,1)S(1)} async-done(((bf16[16,224,128]{2,1,0:T(8,128)(2,1)}), bf16[16,224,128]{2,1,0:T(8,128)(2,1)S(1)}, u32[]{:S(2)}, u32[]{:S(2)}) %all-to-all-start.4) | async-done | bytes 917536 | tf_op jit(solution)/shard_map/all_to_all | solution.py:16
  113.5 3.6 %all-to-all-start.5 = ((bf16[16,8,3584]{2,1,0:T(8,128)(2,1)}), bf16[16,8,3584]{2,1,0:T(8,128)(2,1)S(1)}, u32[]{:S(2)}, u32[]{:S(2)}) async-start(bf16[16,8,3584]{2,1,0:T(8,128)(2,1)} %bitcast.16), calls=%async_computation.5 | async-start | bytes 1835008 | tf_op jit(solution)/shard_map/all_to_all | solution.py:16
  118.2 1.0 copy-done.2
  119.2 1.9 %collective-permute-start.4 = (bf16[16,32,128]{2,1,0:T(8,128)(2,1)S(1)}, bf16[16,32,128]{2,1,0:T(8,128)(2,1)S(1)}, u32[]{:S(2)}, u32[]{:S(2)}) collective-permute-start(bf16[16,32,128]{2,1,0:T(8,128)(2,1)S(1)} %get-tuple-element.35), channel_id=1, source_target_pairs={{0,3},{1,2},{2,1},{3,0},{4,7},{5,6},{6,5},{7,4},{8,11},{9,10},{10,... | collective-permute-start | bytes 393224 | tf_op jit(solution)/shard_map/ppermute | solution.py:173
  121.1 2.9 %collective-permute-start.3 = (bf16[16,32,128]{2,1,0:T(8,128)(2,1)S(1)}, bf16[16,32,128]{2,1,0:T(8,128)(2,1)S(1)}, u32[]{:S(2)}, u32[]{:S(2)}) collective-permute-start(bf16[16,32,128]{2,1,0:T(8,128)(2,1)S(1)} %get-tuple-element.36), channel_id=1, source_target_pairs={{0,2},{1,3},{2,0},{3,1},{4,6},{5,7},{6,4},{7,5},{8,10},{9,11},{10,... | collective-permute-start | bytes 393224 | tf_op jit(solution)/shard_map/ppermute | solution.py:173
  124.0 2.8 %collective-permute-start.2 = (bf16[16,32,128]{2,1,0:T(8,128)(2,1)S(1)}, bf16[16,32,128]{2,1,0:T(8,128)(2,1)S(1)}, u32[]{:S(2)}, u32[]{:S(2)}) collective-permute-start(bf16[16,32,128]{2,1,0:T(8,128)(2,1)S(1)} %get-tuple-element.34), channel_id=1, source_target_pairs={{0,1},{1,0},{2,3},{3,2},{4,5},{5,4},{6,7},{7,6},{8,9},{9,8},{10,11... | collective-permute-start | bytes 393224 | tf_op jit(solution)/shard_map/ppermute | solution.py:173
  126.8 2.4 %collective-permute-done.3 = bf16[16,32,128]{2,1,0:T(8,128)(2,1)S(1)} collective-permute-done((bf16[16,32,128]{2,1,0:T(8,128)(2,1)S(1)}, bf16[16,32,128]{2,1,0:T(8,128)(2,1)S(1)}, u32[]{:S(2)}, u32[]{:S(2)}) %collective-permute-start.3) | collective-permute-done | bytes 131104 | tf_op jit(solution)/shard_map/ppermute | solution.py:173
  129.3 1.0 fusion.7
  130.3 2.7 %all-to-all-done.5 = bf16[16,8,3584]{2,1,0:T(8,128)(2,1)S(1)} async-done(((bf16[16,8,3584]{2,1,0:T(8,128)(2,1)}), bf16[16,8,3584]{2,1,0:T(8,128)(2,1)S(1)}, u32[]{:S(2)}, u32[]{:S(2)}) %all-to-all-start.5) | async-done | bytes 917536 | tf_op jit(solution)/shard_map/all_to_all | solution.py:16
  133.3 19.1 %all_to_all.43 = bf16[16,48,128]{2,1,0:T(8,128)(2,1)S(1)} all-to-all(bf16[16,48,128]{2,1,0:T(8,128)(2,1)S(1)} %pad_maximum_fusion.1), channel_id=1, replica_groups=mesh['y'=4,'x'=4,'z'=16,'core'=2] {'z'}, dimensions={0} | all-to-all | bytes 393216 | tf_op jit(solution)/shard_map/all_to_all | solution.py:16
  152.5 1.1 broadcast_in_dim.22
  153.6 6.4 %all-to-all-start.7 = ((bf16[16,224,128]{2,1,0:T(8,128)(2,1)}), bf16[16,224,128]{2,1,0:T(8,128)(2,1)S(1)}, u32[]{:S(2)}, u32[]{:S(2)}) async-start(bf16[16,224,128]{2,1,0:T(8,128)(2,1)} %broadcast_in_dim.22), calls=%async_computation.7 | async-start | bytes 1835008 | tf_op jit(solution)/shard_map/all_to_all | solution.py:16
  159.9 0.6 convert_reduce_fusion
  160.6 14.9 %all-to-all-done.7 = bf16[16,224,128]{2,1,0:T(8,128)(2,1)S(1)} async-done(((bf16[16,224,128]{2,1,0:T(8,128)(2,1)}), bf16[16,224,128]{2,1,0:T(8,128)(2,1)S(1)}, u32[]{:S(2)}, u32[]{:S(2)}) %all-to-all-start.7) | async-done | bytes 917536 | tf_op jit(solution)/shard_map/all_to_all | solution.py:16
  175.5 1.0 convolution_bitcast_fusion
  (36 shorter events, 2.9 us)
Async XLA Ops:
  7.2 10.3 %copy-start.4 = (f32[448,64]{0,1:T(8,128)S(1)}, f32[448,64]{0,1:T(8,128)}, u32[]{:S(2)}) copy-start(f32[448,64]{0,1:T(8,128)} %param.9) | copy-start | bytes 344068
  7.2 10.3 %copy-start.5 = (f32[448,64]{0,1:T(8,128)S(1)}, f32[448,64]{0,1:T(8,128)}, u32[]{:S(2)}) copy-start(f32[448,64]{0,1:T(8,128)} %param.8) | copy-start | bytes 344068
  7.2 12.3 %copy-start.3 = (bf16[128,2048]{1,0:T(8,128)(2,1)S(1)}, bf16[128,2048]{1,0:T(8,128)(2,1)}, u32[]{:S(2)}) copy-start(bf16[128,2048]{1,0:T(8,128)(2,1)} %param.6) | copy-start | bytes 1572868
  7.2 93.6 %all-gather.3.cloned.1.call-start = ((), (), s32[]{:S(2)}) async-start(), calls=%async_computation.8 | async-start | bytes 3899392 | tf_op jit(solution)/shard_map/all_gather | solution.py:127
  10.5 23.1 %all-to-all-start = ((bf16[16,128,224]{1,2,0:T(8,128)(2,1)}), bf16[16,128,224]{1,2,0:T(8,128)(2,1)S(1)}, u32[]{:S(2)}, u32[]{:S(2)}) async-start(bf16[16,128,224]{1,2,0:T(8,128)(2,1)} %copy.42), calls=%async_computation | async-start | bytes 1835008 | tf_op jit(solution)/shard_map/all_to_all | solution.py:16
  17.6 3.4 %collective-permute-start = (f32[2,64,448]{2,1,0:T(8,128)S(1)}, f32[2,64,448]{2,1,0:T(8,128)S(1)}, u32[]{:S(2)}, u32[]{:S(2)}) collective-permute-start(f32[2,64,448]{2,1,0:T(8,128)S(1)} %get-tuple-element.38), channel_id=1, source_target_pairs={{0,1},{1,0},{2,3},{3,2},{4,5},{5,4},{6,7},{7,6},{8,9},{9,8},{10,11... | collective-permute-start | bytes 688136 | tf_op jit(solution)/shard_map/ppermute | solution.py:20
  97.1 16.4 %all-to-all-start.4 = ((bf16[16,224,128]{2,1,0:T(8,128)(2,1)}), bf16[16,224,128]{2,1,0:T(8,128)(2,1)S(1)}, u32[]{:S(2)}, u32[]{:S(2)}) async-start(bf16[16,224,128]{2,1,0:T(8,128)(2,1)} %broadcast_in_dim.8), calls=%async_computation.4 | async-start | bytes 1835008 | tf_op jit(solution)/shard_map/all_to_all | solution.py:16
  100.8 2.0 %copy-start = (bf16[3584,448]{1,0:T(8,128)(2,1)S(1)}, bf16[3584,448]{1,0:T(8,128)(2,1)}, u32[]{:S(2)}) copy-start(bf16[3584,448]{1,0:T(8,128)(2,1)} %all-gather.3.cloned.1.call-done.basis_ref) | copy-start | bytes 9633796
  102.8 4.0 %copy-start.1 = (bf16[3584,448]{1,0:T(8,128)(2,1)S(1)}, bf16[3584,448]{1,0:T(8,128)(2,1)}, u32[]{:S(2)}) copy-start(bf16[3584,448]{1,0:T(8,128)(2,1)} %all-gather.3.cloned.1.call-done.basis_ref) | copy-start | bytes 9633796
  103.5 3.4 %collective-permute-start.1 = (bf16[128,448]{1,0:T(8,128)(2,1)S(1)}, bf16[128,448]{1,0:T(8,128)(2,1)S(1)}, u32[]{:S(2)}, u32[]{:S(2)}) collective-permute-start(bf16[128,448]{1,0:T(8,128)(2,1)S(1)} %get-tuple-element.24), channel_id=1, source_target_pairs={{0,1},{1,0},{2,3},{3,2},{4,5},{5,4},{6,7},{7,6},{8,9},{9,8},{10,11... | collective-permute-start | bytes 344072 | tf_op jit(solution)/shard_map/ppermute | solution.py:20
  113.5 19.4 %all-to-all-start.5 = ((bf16[16,8,3584]{2,1,0:T(8,128)(2,1)}), bf16[16,8,3584]{2,1,0:T(8,128)(2,1)S(1)}, u32[]{:S(2)}, u32[]{:S(2)}) async-start(bf16[16,8,3584]{2,1,0:T(8,128)(2,1)} %bitcast.16), calls=%async_computation.5 | async-start | bytes 1835008 | tf_op jit(solution)/shard_map/all_to_all | solution.py:16
  118.1 1.0 copy-start.2
  119.2 7.6 %collective-permute-start.4 = (bf16[16,32,128]{2,1,0:T(8,128)(2,1)S(1)}, bf16[16,32,128]{2,1,0:T(8,128)(2,1)S(1)}, u32[]{:S(2)}, u32[]{:S(2)}) collective-permute-start(bf16[16,32,128]{2,1,0:T(8,128)(2,1)S(1)} %get-tuple-element.35), channel_id=1, source_target_pairs={{0,3},{1,2},{2,1},{3,0},{4,7},{5,6},{6,5},{7,4},{8,11},{9,10},{10,... | collective-permute-start | bytes 393224 | tf_op jit(solution)/shard_map/ppermute | solution.py:173
  121.1 8.1 %collective-permute-start.3 = (bf16[16,32,128]{2,1,0:T(8,128)(2,1)S(1)}, bf16[16,32,128]{2,1,0:T(8,128)(2,1)S(1)}, u32[]{:S(2)}, u32[]{:S(2)}) collective-permute-start(bf16[16,32,128]{2,1,0:T(8,128)(2,1)S(1)} %get-tuple-element.36), channel_id=1, source_target_pairs={{0,2},{1,3},{2,0},{3,1},{4,6},{5,7},{6,4},{7,5},{8,10},{9,11},{10,... | collective-permute-start | bytes 393224 | tf_op jit(solution)/shard_map/ppermute | solution.py:173
  124.0 5.2 %collective-permute-start.2 = (bf16[16,32,128]{2,1,0:T(8,128)(2,1)S(1)}, bf16[16,32,128]{2,1,0:T(8,128)(2,1)S(1)}, u32[]{:S(2)}, u32[]{:S(2)}) collective-permute-start(bf16[16,32,128]{2,1,0:T(8,128)(2,1)S(1)} %get-tuple-element.34), channel_id=1, source_target_pairs={{0,1},{1,0},{2,3},{3,2},{4,5},{5,4},{6,7},{7,6},{8,9},{9,8},{10,11... | collective-permute-start | bytes 393224 | tf_op jit(solution)/shard_map/ppermute | solution.py:173
  153.6 21.9 %all-to-all-start.7 = ((bf16[16,224,128]{2,1,0:T(8,128)(2,1)}), bf16[16,224,128]{2,1,0:T(8,128)(2,1)S(1)}, u32[]{:S(2)}, u32[]{:S(2)}) async-start(bf16[16,224,128]{2,1,0:T(8,128)(2,1)} %broadcast_in_dim.22), calls=%async_computation.7 | async-start | bytes 1835008 | tf_op jit(solution)/shard_map/all_to_all | solution.py:16
Sparse Core Ops, SparseCore 0:
  10.1 82.5 all-gather.2

commit v9 on v8

--- a/solution.py
+++ b/solution.py
@@ -162,13 +162,14 @@
 
     gram = lax.dot_general(
         grad_all, grad_t, (((1,), (0,)), ((), ())), preferred_element_type=F32
-    ).reshape(n_z, 4, half // 2, rows) / D
+    )
+    gram = (gram / D).astype(BF16).reshape(n_z, 4, half // 2, rows)
     low = lax.axis_index("z") % 2
     place = core * 2 + low
-    mine = lax.dynamic_index_in_dim(gram, place, 1, keepdims=False)
+    mine = lax.dynamic_index_in_dim(gram, place, 1, keepdims=False).astype(F32)
     col = ("z", "core")
     for other, flip in ((place ^ 2, 1), (place ^ 1, 2), (place ^ 3, 3)):
-        piece = lax.dynamic_index_in_dim(gram, other, 1, keepdims=False).astype(BF16)
+        piece = lax.dynamic_index_in_dim(gram, other, 1, keepdims=False)
         pairs = [(i, i ^ flip) for i in range(2 * n_z)]
         mine = mine + lax.ppermute(piece, col, pairs).astype(F32)
     gram = mine.astype(BF16)

time: 184 us -> 182 us (0.989)
  waiting for transfers between devices: 39.8 us -> 42 us
    all_to_all x4, waiting for transfers between devices: 34.1 us -> 36.4 us  [exchange(): return lax.all_to_all(chunks, axes, 0, 0, tiled=True)]
    unnamed x15 -> x13, local copies, waits for them, and re-layouts: 4.67 us -> 3.7 us
  transfers between devices with their start and end apart: 10 -> 10, of which waited for: 7 -> 7; matrix products, arithmetic and copies ran while one was open for 4% -> 3% of each run, Pallas kernels for 2% -> 2%
where the time goes in v9:
time: 182 us; the launch traced here: 181 us
  blocking collectives  79.9 us (44%)
  waiting for transfers between devices  42 us (23%)
  starting transfers between devices  30.7 us (17%)
  between operations  14.4 us (8%)
  local copies, waits for them, and re-layouts  7.62 us (4%)
  Pallas kernels  3.18 us (2%)
  matrix products  1.93 us (1%)
    all_to_all x4, blocking collectives, exchange(): return lax.all_to_all(chunks, axes, 0, 0, tiled=True)  79.9 us
    all_to_all x4, waiting for transfers between devices, exchange(): return lax.all_to_all(chunks, axes, 0, 0, tiled=True)  36.4 us
    all_to_all x4, starting transfers between devices, exchange(): return lax.all_to_all(chunks, axes, 0, 0, tiled=True)  19.1 us
    ppermute x3, starting transfers between devices, on_device(): mine = mine + lax.ppermute(piece, col, pairs).astype(F32)  7.59 us
    ppermute x2, starting transfers between devices, swap_cores(): return lax.ppermute(block, 'core', [(0, 1), (1, 0)])  3.97 us
    unnamed x13, local copies, waits for them, and re-layouts  3.7 us
  transfers between devices with their start and end apart: 10, of which 7 were waited for; matrix products, arithmetic and copies ran while one was open for 3% of the time, Pallas kernels for 2%

profile of v9, /device:TPU:32, one launch (start us, length us, event | category | flops | bytes accessed | tf_op | source)
XLA Modules:
  0.0 180.9 jit_solution(10759073347561828611)
XLA Ops:
  7.2 0.7 all-gather.3.cloned.1.call-update
  7.9 1.4 copy.42
  9.3 1.2 copy.30
  10.5 7.0 %all-to-all-start = ((bf16[16,128,224]{1,2,0:T(8,128)(2,1)}), bf16[16,128,224]{1,2,0:T(8,128)(2,1)S(1)}, u32[]{:S(2)}, u32[]{:S(2)}) async-start(bf16[16,128,224]{1,2,0:T(8,128)(2,1)} %copy.30), calls=%async_computation | async-start | bytes 1835008 | tf_op jit(solution)/shard_map/all_to_all | solution.py:16
  17.6 1.9 %collective-permute-start = (f32[2,64,448]{2,1,0:T(8,128)S(1)}, f32[2,64,448]{2,1,0:T(8,128)S(1)}, u32[]{:S(2)}, u32[]{:S(2)}) collective-permute-start(f32[2,64,448]{2,1,0:T(8,128)S(1)} %get-tuple-element.38), channel_id=1, source_target_pairs={{0,1},{1,0},{2,3},{3,2},{4,5},{5,4},{6,7},{7,6},{8,9},{9,8},{10,11... | collective-permute-start | bytes 688136 | tf_op jit(solution)/shard_map/ppermute | solution.py:20
  19.8 1.2 collective-permute-done
  21.1 12.5 %all-to-all-done = bf16[16,128,224]{1,2,0:T(8,128)(2,1)S(1)} async-done(((bf16[16,128,224]{1,2,0:T(8,128)(2,1)}), bf16[16,128,224]{1,2,0:T(8,128)(2,1)S(1)}, u32[]{:S(2)}, u32[]{:S(2)}) %all-to-all-start) | async-done | bytes 917536 | tf_op jit(solution)/shard_map/all_to_all | solution.py:16
  33.7 0.4 fusion
  34.1 18.1 %all_to_all.40 = bf16[16,128,224]{1,2,0:T(8,128)(2,1)S(1)} all-to-all(bf16[16,128,224]{1,2,0:T(8,128)(2,1)S(1)} %fusion), channel_id=1, replica_groups=mesh['y'=4,'x'=4,'z'=16,'core'=2] {'y','x'}, dimensions={0} | all-to-all | bytes 1835008 | tf_op jit(solution)/shard_map/all_to_all | solution.py:16
  52.4 27.1 %all_to_all.41 = bf16[16,8,224]{2,1,0:T(8,128)(2,1)S(1)} all-to-all(bf16[16,8,224]{2,1,0:T(8,128)(2,1)S(1)} %bitcast.85), channel_id=1, replica_groups=mesh['y'=4,'x'=4,'z'=16,'core'=2] {'z'}, dimensions={0} | all-to-all | bytes 114688 | tf_op jit(solution)/shard_map/all_to_all | solution.py:16
  79.5 1.1 broadcast_in_dim.8
  80.8 16.5 %all_to_all.42 = bf16[16,8,3584]{2,1,0:T(8,128)(2,1)S(1)} all-to-all(bf16[16,8,3584]{2,1,0:T(8,128)(2,1)S(1)} %broadcast_in_dim.10), channel_id=1, replica_groups=mesh['y'=4,'x'=4,'z'=16,'core'=2] {'y','x'}, dimensions={0} | all-to-all | bytes 1835008 | tf_op jit(solution)/shard_map/all_to_all | solution.py:16
  97.2 3.6 %all-to-all-start.4 = ((bf16[16,224,128]{2,1,0:T(8,128)(2,1)}), bf16[16,224,128]{2,1,0:T(8,128)(2,1)S(1)}, u32[]{:S(2)}, u32[]{:S(2)}) async-start(bf16[16,224,128]{2,1,0:T(8,128)(2,1)} %broadcast_in_dim.8), calls=%async_computation.4 | async-start | bytes 1835008 | tf_op jit(solution)/shard_map/all_to_all | solution.py:16
  100.9 2.0 %copy-done = bf16[3584,448]{1,0:T(8,128)(2,1)S(1)} copy-done((bf16[3584,448]{1,0:T(8,128)(2,1)S(1)}, bf16[3584,448]{1,0:T(8,128)(2,1)}, u32[]{:S(2)}) %copy-start) | copy-done | bytes 3211288
  102.9 0.6 shard_map.84
  103.6 2.1 %collective-permute-start.1 = (bf16[128,448]{1,0:T(8,128)(2,1)S(1)}, bf16[128,448]{1,0:T(8,128)(2,1)S(1)}, u32[]{:S(2)}, u32[]{:S(2)}) collective-permute-start(bf16[128,448]{1,0:T(8,128)(2,1)S(1)} %get-tuple-element.24), channel_id=1, source_target_pairs={{0,1},{1,0},{2,3},{3,2},{4,5},{5,4},{6,7},{7,6},{8,9},{9,8},{10,11... | collective-permute-start | bytes 344072 | tf_op jit(solution)/shard_map/ppermute | solution.py:20
  105.6 1.3 collective-permute-done.1.theirs_ref
  107.0 2.5 %shard_map.85 = (f32[64,448]{1,0:T(8,128)}, f32[64,448]{1,0:T(8,128)}, bf16[128,3584]{1,0:T(8,128)(2,1)}) custom-call(s32[1]{0:T(128)} %bitcast.core_ref, f32[128,448]{1,0:T(8,128)S(1)} %get-tuple-element.23.total_ref, bf16[128,448]{1,0:T(8,128)(2,1)S(1)} %collective-permute-done.1.theirs_ref, f32[2,2,64,448]{3,2,1,0:T(8,128)S(1)} %maximum_select_fusion.moments_ref, ...), custom_call_target="tpu_custom_call" | custom-call | flops 411041792 | bytes 5390336 | tf_op jit(solution)/shard_map/pallas_call | solution.py:95
  109.5 4.2 %all-to-all-done.4 = bf16[16,224,128]{2,1,0:T(8,128)(2,1)S(1)} async-done(((bf16[16,224,128]{2,1,0:T(8,128)(2,1)}), bf16[16,224,128]{2,1,0:T(8,128)(2,1)S(1)}, u32[]{:S(2)}, u32[]{:S(2)}) %all-to-all-start.4) | async-done | bytes 917536 | tf_op jit(solution)/shard_map/all_to_all | solution.py:16
  113.7 3.6 %all-to-all-start.5 = ((bf16[16,8,3584]{2,1,0:T(8,128)(2,1)}), bf16[16,8,3584]{2,1,0:T(8,128)(2,1)S(1)}, u32[]{:S(2)}, u32[]{:S(2)}) async-start(bf16[16,8,3584]{2,1,0:T(8,128)(2,1)} %bitcast.16), calls=%async_computation.5 | async-start | bytes 1835008 | tf_op jit(solution)/shard_map/all_to_all | solution.py:16
  117.4 0.5 fusion.1
  118.0 1.9 %collective-permute-start.4 = (bf16[16,32,128]{2,1,0:T(8,128)(2,1)S(1)}, bf16[16,32,128]{2,1,0:T(8,128)(2,1)S(1)}, u32[]{:S(2)}, u32[]{:S(2)}) collective-permute-start(bf16[16,32,128]{2,1,0:T(8,128)(2,1)S(1)} %get-tuple-element.35), channel_id=1, source_target_pairs={{0,3},{1,2},{2,1},{3,0},{4,7},{5,6},{6,5},{7,4},{8,11},{9,10},{10,... | collective-permute-start | bytes 393224 | tf_op jit(solution)/shard_map/ppermute | solution.py:174
  119.9 2.7 %collective-permute-start.3 = (bf16[16,32,128]{2,1,0:T(8,128)(2,1)S(1)}, bf16[16,32,128]{2,1,0:T(8,128)(2,1)S(1)}, u32[]{:S(2)}, u32[]{:S(2)}) collective-permute-start(bf16[16,32,128]{2,1,0:T(8,128)(2,1)S(1)} %get-tuple-element.36), channel_id=1, source_target_pairs={{0,2},{1,3},{2,0},{3,1},{4,6},{5,7},{6,4},{7,5},{8,10},{9,11},{10,... | collective-permute-start | bytes 393224 | tf_op jit(solution)/shard_map/ppermute | solution.py:174
  122.6 3.0 %collective-permute-start.2 = (bf16[16,32,128]{2,1,0:T(8,128)(2,1)S(1)}, bf16[16,32,128]{2,1,0:T(8,128)(2,1)S(1)}, u32[]{:S(2)}, u32[]{:S(2)}) collective-permute-start(bf16[16,32,128]{2,1,0:T(8,128)(2,1)S(1)} %get-tuple-element.34), channel_id=1, source_target_pairs={{0,1},{1,0},{2,3},{3,2},{4,5},{5,4},{6,7},{7,6},{8,9},{9,8},{10,11... | collective-permute-start | bytes 393224 | tf_op jit(solution)/shard_map/ppermute | solution.py:174
  125.6 2.4 %collective-permute-done.3 = bf16[16,32,128]{2,1,0:T(8,128)(2,1)S(1)} collective-permute-done((bf16[16,32,128]{2,1,0:T(8,128)(2,1)S(1)}, bf16[16,32,128]{2,1,0:T(8,128)(2,1)S(1)}, u32[]{:S(2)}, u32[]{:S(2)}) %collective-permute-start.3) | collective-permute-done | bytes 131104 | tf_op jit(solution)/shard_map/ppermute | solution.py:174
  128.1 4.8 %all-to-all-done.5 = bf16[16,8,3584]{2,1,0:T(8,128)(2,1)S(1)} async-done(((bf16[16,8,3584]{2,1,0:T(8,128)(2,1)}), bf16[16,8,3584]{2,1,0:T(8,128)(2,1)S(1)}, u32[]{:S(2)}, u32[]{:S(2)}) %all-to-all-start.5) | async-done | bytes 917536 | tf_op jit(solution)/shard_map/all_to_all | solution.py:16
  133.3 18.3 %all_to_all.43 = bf16[16,48,128]{2,1,0:T(8,128)(2,1)S(1)} all-to-all(bf16[16,48,128]{2,1,0:T(8,128)(2,1)S(1)} %pad_maximum_fusion.1), channel_id=1, replica_groups=mesh['y'=4,'x'=4,'z'=16,'core'=2] {'z'}, dimensions={0} | all-to-all | bytes 393216 | tf_op jit(solution)/shard_map/all_to_all | solution.py:16
  151.7 1.1 broadcast_in_dim.22
  152.7 4.8 %all-to-all-start.7 = ((bf16[16,224,128]{2,1,0:T(8,128)(2,1)}), bf16[16,224,128]{2,1,0:T(8,128)(2,1)S(1)}, u32[]{:S(2)}, u32[]{:S(2)}) async-start(bf16[16,224,128]{2,1,0:T(8,128)(2,1)} %broadcast_in_dim.22), calls=%async_computation.7 | async-start | bytes 1835008 | tf_op jit(solution)/shard_map/all_to_all | solution.py:16
  157.5 0.6 convert_reduce_fusion
  158.2 14.8 %all-to-all-done.7 = bf16[16,224,128]{2,1,0:T(8,128)(2,1)S(1)} async-done(((bf16[16,224,128]{2,1,0:T(8,128)(2,1)}), bf16[16,224,128]{2,1,0:T(8,128)(2,1)S(1)}, u32[]{:S(2)}, u32[]{:S(2)}) %all-to-all-start.7) | async-done | bytes 917536 | tf_op jit(solution)/shard_map/all_to_all | solution.py:16
  173.0 1.0 convolution_bitcast_fusion
  (33 shorter events, 1.6 us)
Async XLA Ops:
  7.2 10.4 %copy-start.3 = (f32[448,64]{0,1:T(8,128)S(1)}, f32[448,64]{0,1:T(8,128)}, u32[]{:S(2)}) copy-start(f32[448,64]{0,1:T(8,128)} %param.9) | copy-start | bytes 344068
  7.2 10.4 %copy-start.4 = (f32[448,64]{0,1:T(8,128)S(1)}, f32[448,64]{0,1:T(8,128)}, u32[]{:S(2)}) copy-start(f32[448,64]{0,1:T(8,128)} %param.8) | copy-start | bytes 344068
  7.2 12.3 %copy-start.2 = (bf16[128,2048]{1,0:T(8,128)(2,1)S(1)}, bf16[128,2048]{1,0:T(8,128)(2,1)}, u32[]{:S(2)}) copy-start(bf16[128,2048]{1,0:T(8,128)(2,1)} %param.6) | copy-start | bytes 1572868
  7.2 93.7 %all-gather.3.cloned.1.call-start = ((), (), s32[]{:S(2)}) async-start(), calls=%async_computation.8 | async-start | bytes 3899392 | tf_op jit(solution)/shard_map/all_gather | solution.py:127
  10.5 23.1 %all-to-all-start = ((bf16[16,128,224]{1,2,0:T(8,128)(2,1)}), bf16[16,128,224]{1,2,0:T(8,128)(2,1)S(1)}, u32[]{:S(2)}, u32[]{:S(2)}) async-start(bf16[16,128,224]{1,2,0:T(8,128)(2,1)} %copy.30), calls=%async_computation | async-start | bytes 1835008 | tf_op jit(solution)/shard_map/all_to_all | solution.py:16
  17.6 3.4 %collective-permute-start = (f32[2,64,448]{2,1,0:T(8,128)S(1)}, f32[2,64,448]{2,1,0:T(8,128)S(1)}, u32[]{:S(2)}, u32[]{:S(2)}) collective-permute-start(f32[2,64,448]{2,1,0:T(8,128)S(1)} %get-tuple-element.38), channel_id=1, source_target_pairs={{0,1},{1,0},{2,3},{3,2},{4,5},{5,4},{6,7},{7,6},{8,9},{9,8},{10,11... | collective-permute-start | bytes 688136 | tf_op jit(solution)/shard_map/ppermute | solution.py:20
  97.2 16.5 %all-to-all-start.4 = ((bf16[16,224,128]{2,1,0:T(8,128)(2,1)}), bf16[16,224,128]{2,1,0:T(8,128)(2,1)S(1)}, u32[]{:S(2)}, u32[]{:S(2)}) async-start(bf16[16,224,128]{2,1,0:T(8,128)(2,1)} %broadcast_in_dim.8), calls=%async_computation.4 | async-start | bytes 1835008 | tf_op jit(solution)/shard_map/all_to_all | solution.py:16
  100.9 2.0 %copy-start = (bf16[3584,448]{1,0:T(8,128)(2,1)S(1)}, bf16[3584,448]{1,0:T(8,128)(2,1)}, u32[]{:S(2)}) copy-start(bf16[3584,448]{1,0:T(8,128)(2,1)} %all-gather.3.cloned.1.call-done.basis_ref) | copy-start | bytes 9633796
  102.9 4.0 %copy-start.1 = (bf16[3584,448]{1,0:T(8,128)(2,1)S(1)}, bf16[3584,448]{1,0:T(8,128)(2,1)}, u32[]{:S(2)}) copy-start(bf16[3584,448]{1,0:T(8,128)(2,1)} %all-gather.3.cloned.1.call-done.basis_ref) | copy-start | bytes 9633796
  103.6 3.4 %collective-permute-start.1 = (bf16[128,448]{1,0:T(8,128)(2,1)S(1)}, bf16[128,448]{1,0:T(8,128)(2,1)S(1)}, u32[]{:S(2)}, u32[]{:S(2)}) collective-permute-start(bf16[128,448]{1,0:T(8,128)(2,1)S(1)} %get-tuple-element.24), channel_id=1, source_target_pairs={{0,1},{1,0},{2,3},{3,2},{4,5},{5,4},{6,7},{7,6},{8,9},{9,8},{10,11... | collective-permute-start | bytes 344072 | tf_op jit(solution)/shard_map/ppermute | solution.py:20
  113.7 19.2 %all-to-all-start.5 = ((bf16[16,8,3584]{2,1,0:T(8,128)(2,1)}), bf16[16,8,3584]{2,1,0:T(8,128)(2,1)S(1)}, u32[]{:S(2)}, u32[]{:S(2)}) async-start(bf16[16,8,3584]{2,1,0:T(8,128)(2,1)} %bitcast.16), calls=%async_computation.5 | async-start | bytes 1835008 | tf_op jit(solution)/shard_map/all_to_all | solution.py:16
  118.0 7.6 %collective-permute-start.4 = (bf16[16,32,128]{2,1,0:T(8,128)(2,1)S(1)}, bf16[16,32,128]{2,1,0:T(8,128)(2,1)S(1)}, u32[]{:S(2)}, u32[]{:S(2)}) collective-permute-start(bf16[16,32,128]{2,1,0:T(8,128)(2,1)S(1)} %get-tuple-element.35), channel_id=1, source_target_pairs={{0,3},{1,2},{2,1},{3,0},{4,7},{5,6},{6,5},{7,4},{8,11},{9,10},{10,... | collective-permute-start | bytes 393224 | tf_op jit(solution)/shard_map/ppermute | solution.py:174
  119.9 8.1 %collective-permute-start.3 = (bf16[16,32,128]{2,1,0:T(8,128)(2,1)S(1)}, bf16[16,32,128]{2,1,0:T(8,128)(2,1)S(1)}, u32[]{:S(2)}, u32[]{:S(2)}) collective-permute-start(bf16[16,32,128]{2,1,0:T(8,128)(2,1)S(1)} %get-tuple-element.36), channel_id=1, source_target_pairs={{0,2},{1,3},{2,0},{3,1},{4,6},{5,7},{6,4},{7,5},{8,10},{9,11},{10,... | collective-permute-start | bytes 393224 | tf_op jit(solution)/shard_map/ppermute | solution.py:174
  122.6 5.4 %collective-permute-start.2 = (bf16[16,32,128]{2,1,0:T(8,128)(2,1)S(1)}, bf16[16,32,128]{2,1,0:T(8,128)(2,1)S(1)}, u32[]{:S(2)}, u32[]{:S(2)}) collective-permute-start(bf16[16,32,128]{2,1,0:T(8,128)(2,1)S(1)} %get-tuple-element.34), channel_id=1, source_target_pairs={{0,1},{1,0},{2,3},{3,2},{4,5},{5,4},{6,7},{7,6},{8,9},{9,8},{10,11... | collective-permute-start | bytes 393224 | tf_op jit(solution)/shard_map/ppermute | solution.py:174
  152.7 20.3 %all-to-all-start.7 = ((bf16[16,224,128]{2,1,0:T(8,128)(2,1)}), bf16[16,224,128]{2,1,0:T(8,128)(2,1)S(1)}, u32[]{:S(2)}, u32[]{:S(2)}) async-start(bf16[16,224,128]{2,1,0:T(8,128)(2,1)} %broadcast_in_dim.22), calls=%async_computation.7 | async-start | bytes 1835008 | tf_op jit(solution)/shard_map/all_to_all | solution.py:16
Sparse Core Ops, SparseCore 0:
  10.1 82.5 all-gather.2

commit v10 on v9

--- a/solution.py
+++ b/solution.py
@@ -110,6 +110,26 @@
     )(core.reshape(1), total, theirs, moments, basis)
 
 
+def split_kernel(source_ref, chunks_ref):
+    n, _, width = chunks_ref.shape
+    for i in range(n):
+        chunks_ref[i] = source_ref[:, i * width : (i + 1) * width]
+
+
+def split(source, n):
+    rows, columns = source.shape
+    return pl.pallas_call(
+        split_kernel,
+        in_specs=[vmem()],
+        out_specs=vmem(),
+        out_shape=jax.ShapeDtypeStruct((n, rows, columns // n), source.dtype),
+        compiler_params=pltpu.CompilerParams(vmem_limit_bytes=32 * 2**20),
+        cost_estimate=pl.CostEstimate(
+            flops=0, bytes_accessed=4 * rows * columns, transcendentals=0
+        ),
+    )(source)
+
+
 def on_device(grad_parts, left_basis, right_basis, first_moment, second_moment):
     rows = left_basis.shape[0]
     cols = right_basis.shape[0]
@@ -128,11 +148,11 @@
 
     parts, moments = lax.optimization_barrier(
         (
-            exchange(grad_parts[0].reshape(n_dp, rows, cols), DP),
+            exchange(split(grad_parts[0].T, n_dp), DP),
             both(jnp.stack([first_moment.T, second_moment.T])),
         )
     )
-    grad_t = jnp.sum(parts.astype(F32), axis=0).astype(BF16).T
+    grad_t = jnp.sum(parts.astype(F32), axis=0).astype(BF16)
 
     basis_p = (
         left_basis.reshape(rows, n_z, n_dp, sub).transpose(0, 2, 1, 3).reshape(rows, n_dp, rows)

time: 182 us -> 180 us (0.989)
    unnamed x13 -> x14, local copies, waits for them, and re-layouts: 3.7 us -> 3.51 us
  transfers between devices with their start and end apart: 10 -> 10, of which waited for: 7 -> 7; matrix products, arithmetic and copies ran while one was open for 3% -> 2% of each run, Pallas kernels for 2% -> 2%
where the time goes in v10:
time: 180 us
  blocking collectives  79.7 us (44%)
  waiting for transfers between devices  41.7 us (23%)
  starting transfers between devices  30.3 us (17%)
  between operations  14.3 us (8%)
  local copies, waits for them, and re-layouts  6.25 us (3%)
  Pallas kernels  4.28 us (2%)
  matrix products  1.93 us (1%)
    all_to_all x4, blocking collectives, exchange(): return lax.all_to_all(chunks, axes, 0, 0, tiled=True)  79.7 us
    all_to_all x4, waiting for transfers between devices, exchange(): return lax.all_to_all(chunks, axes, 0, 0, tiled=True)  36.1 us
    all_to_all x4, starting transfers between devices, exchange(): return lax.all_to_all(chunks, axes, 0, 0, tiled=True)  18.7 us
    ppermute x3, starting transfers between devices, on_device(): mine = mine + lax.ppermute(piece, col, pairs).astype(F32)  7.59 us
    ppermute x2, starting transfers between devices, swap_cores(): return lax.ppermute(block, 'core', [(0, 1), (1, 0)])  3.97 us
  transfers between devices with their start and end apart: 10, of which 7 were waited for; matrix products, arithmetic and copies ran while one was open for 2% of the time, Pallas kernels for 2%

profile of v10, /device:TPU:32, one launch (start us, length us, event | category | flops | bytes accessed | tf_op | source)
XLA Modules:
  0.0 179.7 jit_solution(886766023965755584)
XLA Ops:
  7.2 0.7 all-gather.3.cloned.1.call-update
  7.9 1.2 copy-done.2
  9.1 1.1 shard_map.84
  10.2 7.0 %all-to-all-start = ((bf16[16,224,128]{2,1,0:T(8,128)(2,1)}), bf16[16,224,128]{2,1,0:T(8,128)(2,1)S(1)}, u32[]{:S(2)}, u32[]{:S(2)}) async-start(bf16[16,224,128]{2,1,0:T(8,128)(2,1)} %shard_map.84), calls=%async_computation | async-start | bytes 1835008 | tf_op jit(solution)/shard_map/all_to_all | solution.py:16
  17.3 1.9 %collective-permute-start = (f32[2,64,448]{2,1,0:T(8,128)S(1)}, f32[2,64,448]{2,1,0:T(8,128)S(1)}, u32[]{:S(2)}, u32[]{:S(2)}) collective-permute-start(f32[2,64,448]{2,1,0:T(8,128)S(1)} %get-tuple-element.38), channel_id=1, source_target_pairs={{0,1},{1,0},{2,3},{3,2},{4,5},{5,4},{6,7},{7,6},{8,9},{9,8},{10,11... | collective-permute-start | bytes 688136 | tf_op jit(solution)/shard_map/ppermute | solution.py:20
  19.5 1.2 collective-permute-done
  20.8 12.5 %all-to-all-done = bf16[16,224,128]{2,1,0:T(8,128)(2,1)S(1)} async-done(((bf16[16,224,128]{2,1,0:T(8,128)(2,1)}), bf16[16,224,128]{2,1,0:T(8,128)(2,1)S(1)}, u32[]{:S(2)}, u32[]{:S(2)}) %all-to-all-start) | async-done | bytes 917536 | tf_op jit(solution)/shard_map/all_to_all | solution.py:16
  33.4 0.4 fusion
  33.8 18.1 %all_to_all.40 = bf16[16,128,224]{1,2,0:T(8,128)(2,1)S(1)} all-to-all(bf16[16,128,224]{1,2,0:T(8,128)(2,1)S(1)} %fusion), channel_id=1, replica_groups=mesh['y'=4,'x'=4,'z'=16,'core'=2] {'y','x'}, dimensions={0} | all-to-all | bytes 1835008 | tf_op jit(solution)/shard_map/all_to_all | solution.py:16
  52.1 27.3 %all_to_all.41 = bf16[16,8,224]{2,1,0:T(8,128)(2,1)S(1)} all-to-all(bf16[16,8,224]{2,1,0:T(8,128)(2,1)S(1)} %bitcast.80), channel_id=1, replica_groups=mesh['y'=4,'x'=4,'z'=16,'core'=2] {'z'}, dimensions={0} | all-to-all | bytes 114688 | tf_op jit(solution)/shard_map/all_to_all | solution.py:16
  79.4 1.0 broadcast_in_dim.8
  80.7 15.9 %all_to_all.42 = bf16[16,8,3584]{2,1,0:T(8,128)(2,1)S(1)} all-to-all(bf16[16,8,3584]{2,1,0:T(8,128)(2,1)S(1)} %broadcast_in_dim.10), channel_id=1, replica_groups=mesh['y'=4,'x'=4,'z'=16,'core'=2] {'y','x'}, dimensions={0} | all-to-all | bytes 1835008 | tf_op jit(solution)/shard_map/all_to_all | solution.py:16
  96.6 3.6 %all-to-all-start.4 = ((bf16[16,224,128]{2,1,0:T(8,128)(2,1)}), bf16[16,224,128]{2,1,0:T(8,128)(2,1)S(1)}, u32[]{:S(2)}, u32[]{:S(2)}) async-start(bf16[16,224,128]{2,1,0:T(8,128)(2,1)} %broadcast_in_dim.8), calls=%async_computation.4 | async-start | bytes 1835008 | tf_op jit(solution)/shard_map/all_to_all | solution.py:16
  100.2 2.0 %copy-done = bf16[3584,448]{1,0:T(8,128)(2,1)S(1)} copy-done((bf16[3584,448]{1,0:T(8,128)(2,1)S(1)}, bf16[3584,448]{1,0:T(8,128)(2,1)}, u32[]{:S(2)}) %copy-start) | copy-done | bytes 3211288
  102.3 0.6 shard_map.85
  102.9 2.1 %collective-permute-start.1 = (bf16[128,448]{1,0:T(8,128)(2,1)S(1)}, bf16[128,448]{1,0:T(8,128)(2,1)S(1)}, u32[]{:S(2)}, u32[]{:S(2)}) collective-permute-start(bf16[128,448]{1,0:T(8,128)(2,1)S(1)} %get-tuple-element.24), channel_id=1, source_target_pairs={{0,1},{1,0},{2,3},{3,2},{4,5},{5,4},{6,7},{7,6},{8,9},{9,8},{10,11... | collective-permute-start | bytes 344072 | tf_op jit(solution)/shard_map/ppermute | solution.py:20
  105.0 1.3 collective-permute-done.1.theirs_ref
  106.3 2.5 %shard_map.86 = (f32[64,448]{1,0:T(8,128)}, f32[64,448]{1,0:T(8,128)}, bf16[128,3584]{1,0:T(8,128)(2,1)}) custom-call(s32[1]{0:T(128)} %bitcast.core_ref, f32[128,448]{1,0:T(8,128)S(1)} %get-tuple-element.23.total_ref, bf16[128,448]{1,0:T(8,128)(2,1)S(1)} %collective-permute-done.1.theirs_ref, f32[2,2,64,448]{3,2,1,0:T(8,128)S(1)} %maximum_select_fusion.moments_ref, ...), custom_call_target="tpu_custom_call" | custom-call | flops 411041792 | bytes 5390336 | tf_op jit(solution)/shard_map/pallas_call | solution.py:95
  108.8 3.9 %all-to-all-done.4 = bf16[16,224,128]{2,1,0:T(8,128)(2,1)S(1)} async-done(((bf16[16,224,128]{2,1,0:T(8,128)(2,1)}), bf16[16,224,128]{2,1,0:T(8,128)(2,1)S(1)}, u32[]{:S(2)}, u32[]{:S(2)}) %all-to-all-start.4) | async-done | bytes 917536 | tf_op jit(solution)/shard_map/all_to_all | solution.py:16
  112.8 3.6 %all-to-all-start.5 = ((bf16[16,8,3584]{2,1,0:T(8,128)(2,1)}), bf16[16,8,3584]{2,1,0:T(8,128)(2,1)S(1)}, u32[]{:S(2)}, u32[]{:S(2)}) async-start(bf16[16,8,3584]{2,1,0:T(8,128)(2,1)} %bitcast.17), calls=%async_computation.5 | async-start | bytes 1835008 | tf_op jit(solution)/shard_map/all_to_all | solution.py:16
  116.4 0.5 fusion.1
  117.0 2.2 %collective-permute-start.4 = (bf16[16,32,128]{2,1,0:T(8,128)(2,1)S(1)}, bf16[16,32,128]{2,1,0:T(8,128)(2,1)S(1)}, u32[]{:S(2)}, u32[]{:S(2)}) collective-permute-start(bf16[16,32,128]{2,1,0:T(8,128)(2,1)S(1)} %get-tuple-element.35), channel_id=1, source_target_pairs={{0,3},{1,2},{2,1},{3,0},{4,7},{5,6},{6,5},{7,4},{8,11},{9,10},{10,... | collective-permute-start | bytes 393224 | tf_op jit(solution)/shard_map/ppermute | solution.py:194
  119.2 3.2 %collective-permute-start.3 = (bf16[16,32,128]{2,1,0:T(8,128)(2,1)S(1)}, bf16[16,32,128]{2,1,0:T(8,128)(2,1)S(1)}, u32[]{:S(2)}, u32[]{:S(2)}) collective-permute-start(bf16[16,32,128]{2,1,0:T(8,128)(2,1)S(1)} %get-tuple-element.36), channel_id=1, source_target_pairs={{0,2},{1,3},{2,0},{3,1},{4,6},{5,7},{6,4},{7,5},{8,10},{9,11},{10,... | collective-permute-start | bytes 393224 | tf_op jit(solution)/shard_map/ppermute | solution.py:194
  122.4 2.2 %collective-permute-start.2 = (bf16[16,32,128]{2,1,0:T(8,128)(2,1)S(1)}, bf16[16,32,128]{2,1,0:T(8,128)(2,1)S(1)}, u32[]{:S(2)}, u32[]{:S(2)}) collective-permute-start(bf16[16,32,128]{2,1,0:T(8,128)(2,1)S(1)} %get-tuple-element.34), channel_id=1, source_target_pairs={{0,1},{1,0},{2,3},{3,2},{4,5},{5,4},{6,7},{7,6},{8,9},{9,8},{10,11... | collective-permute-start | bytes 393224 | tf_op jit(solution)/shard_map/ppermute | solution.py:194
  124.6 2.4 %collective-permute-done.3 = bf16[16,32,128]{2,1,0:T(8,128)(2,1)S(1)} collective-permute-done((bf16[16,32,128]{2,1,0:T(8,128)(2,1)S(1)}, bf16[16,32,128]{2,1,0:T(8,128)(2,1)S(1)}, u32[]{:S(2)}, u32[]{:S(2)}) %collective-permute-start.3) | collective-permute-done | bytes 131104 | tf_op jit(solution)/shard_map/ppermute | solution.py:194
  127.1 5.3 %all-to-all-done.5 = bf16[16,8,3584]{2,1,0:T(8,128)(2,1)S(1)} async-done(((bf16[16,8,3584]{2,1,0:T(8,128)(2,1)}), bf16[16,8,3584]{2,1,0:T(8,128)(2,1)S(1)}, u32[]{:S(2)}, u32[]{:S(2)}) %all-to-all-start.5) | async-done | bytes 917536 | tf_op jit(solution)/shard_map/all_to_all | solution.py:16
  132.7 18.5 %all_to_all.43 = bf16[16,48,128]{2,1,0:T(8,128)(2,1)S(1)} all-to-all(bf16[16,48,128]{2,1,0:T(8,128)(2,1)S(1)} %pad_maximum_fusion.1), channel_id=1, replica_groups=mesh['y'=4,'x'=4,'z'=16,'core'=2] {'z'}, dimensions={0} | all-to-all | bytes 393216 | tf_op jit(solution)/shard_map/all_to_all | solution.py:16
  151.4 1.1 broadcast_in_dim.22
  152.4 4.4 %all-to-all-start.7 = ((bf16[16,224,128]{2,1,0:T(8,128)(2,1)}), bf16[16,224,128]{2,1,0:T(8,128)(2,1)S(1)}, u32[]{:S(2)}, u32[]{:S(2)}) async-start(bf16[16,224,128]{2,1,0:T(8,128)(2,1)} %broadcast_in_dim.22), calls=%async_computation.7 | async-start | bytes 1835008 | tf_op jit(solution)/shard_map/all_to_all | solution.py:16
  156.8 0.6 convert_reduce_fusion
  157.5 14.4 %all-to-all-done.7 = bf16[16,224,128]{2,1,0:T(8,128)(2,1)S(1)} async-done(((bf16[16,224,128]{2,1,0:T(8,128)(2,1)}), bf16[16,224,128]{2,1,0:T(8,128)(2,1)S(1)}, u32[]{:S(2)}, u32[]{:S(2)}) %all-to-all-start.7) | async-done | bytes 917536 | tf_op jit(solution)/shard_map/all_to_all | solution.py:16
  171.8 1.0 convolution_bitcast_fusion
  (34 shorter events, 1.6 us)
Async XLA Ops:
  7.2 10.1 %copy-start.4 = (f32[448,64]{0,1:T(8,128)S(1)}, f32[448,64]{0,1:T(8,128)}, u32[]{:S(2)}) copy-start(f32[448,64]{0,1:T(8,128)} %param.9) | copy-start | bytes 344068
  7.2 93.0 %all-gather.3.cloned.1.call-start = ((), (), s32[]{:S(2)}) async-start(), calls=%async_computation.8 | async-start | bytes 3899392 | tf_op jit(solution)/shard_map/all_gather | solution.py:147
  7.9 1.2 copy-start.2
  9.1 8.1 %copy-start.5 = (f32[448,64]{0,1:T(8,128)S(1)}, f32[448,64]{0,1:T(8,128)}, u32[]{:S(2)}) copy-start(f32[448,64]{0,1:T(8,128)} %param.8) | copy-start | bytes 344068
  9.1 10.2 %copy-start.3 = (bf16[128,2048]{1,0:T(8,128)(2,1)S(1)}, bf16[128,2048]{1,0:T(8,128)(2,1)}, u32[]{:S(2)}) copy-start(bf16[128,2048]{1,0:T(8,128)(2,1)} %param.6) | copy-start | bytes 1572868
  10.2 23.1 %all-to-all-start = ((bf16[16,224,128]{2,1,0:T(8,128)(2,1)}), bf16[16,224,128]{2,1,0:T(8,128)(2,1)S(1)}, u32[]{:S(2)}, u32[]{:S(2)}) async-start(bf16[16,224,128]{2,1,0:T(8,128)(2,1)} %shard_map.84), calls=%async_computation | async-start | bytes 1835008 | tf_op jit(solution)/shard_map/all_to_all | solution.py:16
  17.3 3.4 %collective-permute-start = (f32[2,64,448]{2,1,0:T(8,128)S(1)}, f32[2,64,448]{2,1,0:T(8,128)S(1)}, u32[]{:S(2)}, u32[]{:S(2)}) collective-permute-start(f32[2,64,448]{2,1,0:T(8,128)S(1)} %get-tuple-element.38), channel_id=1, source_target_pairs={{0,1},{1,0},{2,3},{3,2},{4,5},{5,4},{6,7},{7,6},{8,9},{9,8},{10,11... | collective-permute-start | bytes 688136 | tf_op jit(solution)/shard_map/ppermute | solution.py:20
  96.6 16.2 %all-to-all-start.4 = ((bf16[16,224,128]{2,1,0:T(8,128)(2,1)}), bf16[16,224,128]{2,1,0:T(8,128)(2,1)S(1)}, u32[]{:S(2)}, u32[]{:S(2)}) async-start(bf16[16,224,128]{2,1,0:T(8,128)(2,1)} %broadcast_in_dim.8), calls=%async_computation.4 | async-start | bytes 1835008 | tf_op jit(solution)/shard_map/all_to_all | solution.py:16
  100.2 2.0 %copy-start = (bf16[3584,448]{1,0:T(8,128)(2,1)S(1)}, bf16[3584,448]{1,0:T(8,128)(2,1)}, u32[]{:S(2)}) copy-start(bf16[3584,448]{1,0:T(8,128)(2,1)} %all-gather.3.cloned.1.call-done.basis_ref) | copy-start | bytes 9633796
  102.3 4.0 %copy-start.1 = (bf16[3584,448]{1,0:T(8,128)(2,1)S(1)}, bf16[3584,448]{1,0:T(8,128)(2,1)}, u32[]{:S(2)}) copy-start(bf16[3584,448]{1,0:T(8,128)(2,1)} %all-gather.3.cloned.1.call-done.basis_ref) | copy-start | bytes 9633796
  102.9 3.4 %collective-permute-start.1 = (bf16[128,448]{1,0:T(8,128)(2,1)S(1)}, bf16[128,448]{1,0:T(8,128)(2,1)S(1)}, u32[]{:S(2)}, u32[]{:S(2)}) collective-permute-start(bf16[128,448]{1,0:T(8,128)(2,1)S(1)} %get-tuple-element.24), channel_id=1, source_target_pairs={{0,1},{1,0},{2,3},{3,2},{4,5},{5,4},{6,7},{7,6},{8,9},{9,8},{10,11... | collective-permute-start | bytes 344072 | tf_op jit(solution)/shard_map/ppermute | solution.py:20
  112.8 19.6 %all-to-all-start.5 = ((bf16[16,8,3584]{2,1,0:T(8,128)(2,1)}), bf16[16,8,3584]{2,1,0:T(8,128)(2,1)S(1)}, u32[]{:S(2)}, u32[]{:S(2)}) async-start(bf16[16,8,3584]{2,1,0:T(8,128)(2,1)} %bitcast.17), calls=%async_computation.5 | async-start | bytes 1835008 | tf_op jit(solution)/shard_map/all_to_all | solution.py:16
  117.0 7.6 %collective-permute-start.4 = (bf16[16,32,128]{2,1,0:T(8,128)(2,1)S(1)}, bf16[16,32,128]{2,1,0:T(8,128)(2,1)S(1)}, u32[]{:S(2)}, u32[]{:S(2)}) collective-permute-start(bf16[16,32,128]{2,1,0:T(8,128)(2,1)S(1)} %get-tuple-element.35), channel_id=1, source_target_pairs={{0,3},{1,2},{2,1},{3,0},{4,7},{5,6},{6,5},{7,4},{8,11},{9,10},{10,... | collective-permute-start | bytes 393224 | tf_op jit(solution)/shard_map/ppermute | solution.py:194
  119.2 7.8 %collective-permute-start.3 = (bf16[16,32,128]{2,1,0:T(8,128)(2,1)S(1)}, bf16[16,32,128]{2,1,0:T(8,128)(2,1)S(1)}, u32[]{:S(2)}, u32[]{:S(2)}) collective-permute-start(bf16[16,32,128]{2,1,0:T(8,128)(2,1)S(1)} %get-tuple-element.36), channel_id=1, source_target_pairs={{0,2},{1,3},{2,0},{3,1},{4,6},{5,7},{6,4},{7,5},{8,10},{9,11},{10,... | collective-permute-start | bytes 393224 | tf_op jit(solution)/shard_map/ppermute | solution.py:194
  122.4 4.6 %collective-permute-start.2 = (bf16[16,32,128]{2,1,0:T(8,128)(2,1)S(1)}, bf16[16,32,128]{2,1,0:T(8,128)(2,1)S(1)}, u32[]{:S(2)}, u32[]{:S(2)}) collective-permute-start(bf16[16,32,128]{2,1,0:T(8,128)(2,1)S(1)} %get-tuple-element.34), channel_id=1, source_target_pairs={{0,1},{1,0},{2,3},{3,2},{4,5},{5,4},{6,7},{7,6},{8,9},{9,8},{10,11... | collective-permute-start | bytes 393224 | tf_op jit(solution)/shard_map/ppermute | solution.py:194
  152.4 19.4 %all-to-all-start.7 = ((bf16[16,224,128]{2,1,0:T(8,128)(2,1)}), bf16[16,224,128]{2,1,0:T(8,128)(2,1)S(1)}, u32[]{:S(2)}, u32[]{:S(2)}) async-start(bf16[16,224,128]{2,1,0:T(8,128)(2,1)} %broadcast_in_dim.22), calls=%async_computation.7 | async-start | bytes 1835008 | tf_op jit(solution)/shard_map/all_to_all | solution.py:16
Sparse Core Ops, SparseCore 0:
  10.1 82.7 all-gather.2
